TPU v7x, 32 devices: a whole 2x2x4 slice. The times are simulated.
32 devices in a mesh: rep: 2 (over x), shard: 16 (over z, y, core).
Axes of the slice: x: 2, y: 2, z: 4, core: 2. Of those that a mesh axis runs over, the one named last changes fastest.
Arguments:
- row_ids: int32 [32768, 16, 4, 2], P(('rep', 'shard')), may hold values from 0 to 1023, as said below
- bag_lengths: int32 [32768, 16], P(('rep', 'shard')), may hold values from 3 to 4
- sample_counts: int32 [32], replicated, may hold values from 1 to 1024, as said below
- label_mask: int32 [32768, 5], P(('rep', 'shard')), may hold values 0 or 1
- labels: int32 [32768, 5], P(('rep', 'shard')), may hold values 0 or 1
- tables: float32 [262144, 128], P('shard'), may hold values from -4 to 4
- table_m: float32 [262144, 128], P('shard'), may hold values from -4.7683716e-07 to 4.7683716e-07
- table_v: float32 [262144, 128], P('shard'), may hold values from 4.8894437e-16 to 1.9790605e-15
- expert_w: float32 [8, 1024, 512], P(None, 'shard'), may hold values from -0.1875 to 0.1875
- expert_m: float32 [8, 1024, 512], P(None, 'shard'), may hold values from -1.9073486e-05 to 1.9073486e-05
- expert_v: float32 [8, 1024, 512], P(None, 'shard'), may hold values from 8.850098e-13 to 3.6621092e-12
- gate_w: float32 [1024, 40], P('shard'), may hold values from -0.09375 to 0.09375
- gate_m: float32 [1024, 40], P('shard'), may hold values from -0.00024414062 to 0.00024414062
- gate_v: float32 [1024, 40], P('shard'), may hold values from 1.14440915e-10 to 4.5776366e-10
- tower_weight_matrix: float32 [5, 512, 64], P(None, 'shard'), may hold values from -0.25 to 0.25
- tower_m: float32 [5, 512, 64], P(None, 'shard'), may hold values from -0.00021362305 to 0.00021362305
- tower_v: float32 [5, 512, 64], P(None, 'shard'), may hold values from 9.155274e-11 to 3.6621095e-10
- small_params: float32 [4741], replicated, may hold values from -1.5 to 1.5
- small_m: float32 [4741], replicated, may hold values from -1 to 1
- small_v: float32 [4741], replicated, may hold values from 0 to 1
Outputs:
- loss_parts: float32 [2], replicated
- table_new: float32 [262144, 128], P('shard')
- table_m_new: float32 [262144, 128], P('shard')
- table_v_new: float32 [262144, 128], P('shard')
- expert_new: float32 [8, 1024, 512], P(None, 'shard')
- expert_m_new: float32 [8, 1024, 512], P(None, 'shard')
- expert_v_new: float32 [8, 1024, 512], P(None, 'shard')
- gate_new: float32 [1024, 40], P('shard')
- gate_m_new: float32 [1024, 40], P('shard')
- gate_v_new: float32 [1024, 40], P('shard')
- tower_new: float32 [5, 512, 64], P(None, 'shard')
- tower_m_new: float32 [5, 512, 64], P(None, 'shard')
- tower_v_new: float32 [5, 512, 64], P(None, 'shard')
- small_new: float32 [4741], replicated
- small_m_new: float32 [4741], replicated
- small_v_new: float32 [4741], replicated
Inputs may be any that keep to these rules, and one draw needn't show every extreme that they name: row_ids[..., 0] * 1024 + row_ids[..., 1] is a row number of 0 to 262143, and row_ids[..., 1] is under 1024. In the 65536 slots of each device's samples (used or not), every block of 16384 consecutive row numbers is named exactly 4096 times, 4096 / 2 times by bags of each table; among those slots of one device that name one block through one table, every row named is named exactly twice, so that they hold exactly 1024 distinct rows. `sample_counts`: entry d counts the samples that take part on device d (devices in the order of rep+shard); they are its first ones. The last device's count is 1024.
All inputs are finite; a program needn't handle non-finite values. No bound on the sum of `label_mask` or of `labels` on one device may be relied on, other than what follows from the above.
Results may differ from a plain program's by a relative error of at most 0.0074.
Values may be sent and summed in bfloat16 or wider, within the bound.
No kernel may reach another device: no remote copies, remote signals or barrier semaphores. Data moves between devices by JAX's collectives and lax.ppermute only.
A program may use at most 256 MiB of HBM per device.

v0:
```python
import math

import jax
import jax.numpy as jnp
from jax import lax
from jax.sharding import PartitionSpec as P

TABLES = 2
WIDTH = 64
ROW_BASE = 1024
EXPERTS = 8
HID = 512
TASKS = 5
TOWER = 64
STEP = 10


beta_first = 0.9
beta_second = 0.999
adam_epsilon = 1e-08
weight_decay = 0.01
rate_table = 1.0
rate_expert = 0.06
rate_gate = 0.03
rate_tower = 0.08
rate_small = 0.5
top_precision = lax.Precision.HIGHEST


def swish(value):
    return value * jax.nn.sigmoid(value)


def swish_slope(value):
    sigma = jax.nn.sigmoid(value)
    return sigma * (1.0 + value * (1.0 - sigma))


def adamw(weight, grad, first, second, rate):
    first_new = beta_first * first + (1.0 - beta_first) * grad
    second_new = beta_second * second + (1.0 - beta_second) * grad * grad
    first_hat = first_new / (1.0 - beta_first**STEP)
    second_hat = second_new / (1.0 - beta_second**STEP)
    weight_new = weight - rate * (
        first_hat / (jnp.sqrt(second_hat) + adam_epsilon) + weight_decay * weight
    )
    return (weight_new, first_new, second_new)


def unpack_small(small_params):
    first_end = EXPERTS * HID
    second_end = first_end + TASKS * TOWER
    third_end = second_end + TASKS * TOWER
    expert_bias = small_params[:first_end].reshape(EXPERTS, HID)
    tower_layer_bias = small_params[first_end:second_end].reshape(TASKS, TOWER)
    head_weight = small_params[second_end:third_end].reshape(TASKS, TOWER)
    head_bias = small_params[third_end:]
    return (expert_bias, tower_layer_bias, head_weight, head_bias)


def owner_places(owner_of, shards, capacity):
    slot_count = owner_of.shape[0]
    block_len = math.gcd(slot_count, 512)
    block_num = slot_count // block_len
    columns = jnp.arange(shards, dtype=jnp.int32)
    one_hot = (
        (owner_of[:, None] == columns[None, :])
        .astype(jnp.bfloat16)
        .reshape(block_num, block_len, shards)
    )
    line = jnp.arange(block_len, dtype=jnp.int32)
    lower = (line[None, :] < line[:, None]).astype(jnp.bfloat16)
    inside = jnp.einsum("ij,bjk->bik", lower, one_hot, preferred_element_type=jnp.float32)
    block_totals = jnp.sum(one_hot.astype(jnp.float32), axis=1)
    before = jnp.cumsum(block_totals, axis=0) - block_totals
    counted = (inside + before[:, None, :]) * one_hot.astype(jnp.float32)
    rank = jnp.sum(counted, axis=-1).reshape(slot_count).astype(jnp.int32)
    return owner_of * capacity + rank


def on_device(
    row_ids,
    bag_lengths,
    sample_counts,
    label_mask,
    labels,
    tables,
    table_m,
    table_v,
    expert_w,
    expert_m,
    expert_v,
    gate_w,
    gate_m,
    gate_v,
    tower_weight_matrix,
    tower_m,
    tower_v,
    small_params,
    small_m,
    small_v,
):
    shards = lax.axis_size("shard")
    rep_index = lax.axis_index("rep")
    shard_index = lax.axis_index("shard")
    samples, bag_count, longest = row_ids.shape[:3]
    rows_dev, packed = tables.shape
    slot_count = samples * bag_count * longest
    capacity = slot_count // shards
    table_span = rows_dev * TABLES
    dense_parts = (
        expert_w.astype(jnp.bfloat16),
        gate_w.astype(jnp.bfloat16),
        tower_weight_matrix.astype(jnp.bfloat16),
    )
    expert_full, gate_full, tower_activation_full = (
        lax.all_gather(dense_parts[0], "shard", axis=1, tiled=True),
        lax.all_gather(dense_parts[1], "shard", axis=0, tiled=True),
        lax.all_gather(dense_parts[2], "shard", axis=1, tiled=True),
    )
    flat_ids = (row_ids[..., 0] * ROW_BASE + row_ids[..., 1]).reshape(slot_count)
    slot_index = jnp.arange(slot_count, dtype=jnp.int32)
    table_of = slot_index // longest % bag_count // (bag_count // TABLES)
    local_key = flat_ids % rows_dev * TABLES + table_of
    owner_of = flat_ids // rows_dev
    table_rows = tables.astype(jnp.bfloat16).reshape(table_span, WIDTH)
    destination = owner_places(owner_of, shards, capacity)
    request = (
        jnp.zeros((slot_count,), jnp.int32).at[destination].set(local_key).reshape(shards, capacity)
    )
    sort_order = jnp.zeros((slot_count,), jnp.int32).at[destination].set(slot_index)
    wanted = lax.all_to_all(request, "shard", split_axis=0, concat_axis=0, tiled=True)
    wanted_flat = wanted.reshape(slot_count)
    found_rows = jnp.take(table_rows, wanted_flat, axis=0).reshape(
        shards, capacity * WIDTH // packed, packed
    )
    replies = lax.all_to_all(found_rows, "shard", split_axis=0, concat_axis=0, tiled=True)
    looked = jnp.take(replies.reshape(slot_count, WIDTH), destination, axis=0)
    looked = looked.reshape(samples, bag_count, longest, WIDTH)
    used_mask = (
        jnp.arange(longest, dtype=jnp.int32)[None, None, :] < bag_lengths[:, :, None]
    ).astype(jnp.float32)
    pooled = jnp.sum(looked.astype(jnp.float32) * used_mask[..., None], axis=2).reshape(
        samples, bag_count * WIDTH
    )
    pooled_low = pooled.astype(jnp.bfloat16)
    expert_bias, tower_layer_bias, head_weight, head_bias = unpack_small(small_params)
    expert_pre = (
        jnp.einsum("sd,edh->esh", pooled_low, expert_full, preferred_element_type=jnp.float32)
        + expert_bias[:, None, :]
    )
    expert_out = swish(expert_pre)
    gate_logits = jnp.dot(pooled_low, gate_full, preferred_element_type=jnp.float32).reshape(
        samples, TASKS, EXPERTS
    )
    gates = jax.nn.softmax(gate_logits, axis=-1)
    mixed_features = jnp.einsum("ske,esh->skh", gates, expert_out, precision=top_precision)
    mixed_features_reduced = mixed_features.astype(jnp.bfloat16)
    tower_preactivation = (
        jnp.einsum(
            "bme,meu->bmu",
            mixed_features_reduced,
            tower_activation_full,
            preferred_element_type=jnp.float32,
        )
        + tower_layer_bias[None]
    )
    tower_out = swish(tower_preactivation)
    logit_out = jnp.sum(tower_out * head_weight[None], axis=-1) + head_bias[None]
    live_count = jnp.take(sample_counts, rep_index * shards + shard_index)
    live_mask = (jnp.arange(samples, dtype=jnp.int32) < live_count).astype(jnp.float32)[
        :, None
    ] * label_mask.astype(jnp.float32)
    label_values = labels.astype(jnp.float32)
    sample_total = jnp.sum(sample_counts).astype(jnp.float32)
    loss_local = jnp.sum(live_mask * (jax.nn.softplus(logit_out) - label_values * logit_out))
    logit_grad = live_mask * (jax.nn.sigmoid(logit_out) - label_values) / sample_total
    head_weight_grad = jnp.sum(logit_grad[..., None] * tower_out, axis=0)
    head_bias_grad = jnp.sum(logit_grad, axis=0)
    tower_preactivation_gradient = (
        logit_grad[..., None] * head_weight[None] * swish_slope(tower_preactivation)
    ).astype(jnp.bfloat16)
    tower_bias_grad = jnp.sum(tower_preactivation_gradient, axis=0, dtype=jnp.float32)
    tower_grad = jnp.einsum(
        "ajb,ajp->jbp",
        mixed_features_reduced,
        tower_preactivation_gradient,
        preferred_element_type=jnp.float32,
    )
    mixed_grad = jnp.einsum(
        "byr,yer->bye",
        tower_preactivation_gradient,
        tower_activation_full,
        preferred_element_type=jnp.float32,
    )
    gate_prob_grad = jnp.einsum("skh,esh->ske", mixed_grad, expert_out, precision=top_precision)
    expert_out_grad = jnp.einsum("ske,skh->esh", gates, mixed_grad, precision=top_precision)
    centered = gate_prob_grad - jnp.sum(gates * gate_prob_grad, axis=-1, keepdims=True)
    logit_gate_grad = (gates * centered).astype(jnp.bfloat16).reshape(samples, TASKS * EXPERTS)
    expert_grad_pre = (expert_out_grad * swish_slope(expert_pre)).astype(jnp.bfloat16)
    expert_bias_grad = jnp.sum(expert_grad_pre, axis=1, dtype=jnp.float32)
    expert_grad = jnp.einsum(
        "sd,esh->edh", pooled_low, expert_grad_pre, preferred_element_type=jnp.float32
    )
    gate_grad = jnp.einsum(
        "sd,sk->dk", pooled_low, logit_gate_grad, preferred_element_type=jnp.float32
    )
    pooled_grad = jnp.einsum(
        "esh,edh->sd", expert_grad_pre, expert_full, preferred_element_type=jnp.float32
    )
    pooled_grad = pooled_grad + jnp.einsum(
        "sk,dk->sd", logit_gate_grad, gate_full, preferred_element_type=jnp.float32
    )
    slot_grad = (pooled_grad.reshape(samples, bag_count, 1, WIDTH) * used_mask[..., None]).reshape(
        slot_count, WIDTH
    )
    sent_grad = jnp.take(slot_grad, sort_order, axis=0).reshape(
        shards, capacity * WIDTH // packed, packed
    )
    arrived = lax.all_to_all(sent_grad, "shard", split_axis=0, concat_axis=0, tiled=True)
    table_grad = jax.ops.segment_sum(
        arrived.reshape(slot_count, WIDTH), wanted_flat, num_segments=table_span
    ).reshape(rows_dev, packed)
    table_total = lax.psum(table_grad, "rep")
    table_new, table_m_new, table_v_new = adamw(tables, table_total, table_m, table_v, rate_table)
    owned = (
        lax.psum_scatter(expert_grad, "shard", scatter_dimension=1, tiled=True),
        lax.psum_scatter(gate_grad, "shard", scatter_dimension=0, tiled=True),
        lax.psum_scatter(tower_grad, "shard", scatter_dimension=1, tiled=True),
    )
    expert_sum, gate_sum, tower_sum = lax.psum((owned[0], owned[1], owned[2]), "rep")
    small_grad = jnp.concatenate(
        [
            expert_bias_grad.reshape(-1),
            tower_bias_grad.reshape(-1),
            head_weight_grad.reshape(-1),
            head_bias_grad,
        ]
    )
    small_sum, loss_sum = lax.psum((small_grad, loss_local), ("rep", "shard"))
    expert_new, expert_m_new, expert_v_new = adamw(
        expert_w, expert_sum, expert_m, expert_v, rate_expert
    )
    gate_new, gate_m_new, gate_v_new = adamw(gate_w, gate_sum, gate_m, gate_v, rate_gate)
    tower_new, tower_m_new, tower_v_new = adamw(
        tower_weight_matrix, tower_sum, tower_m, tower_v, rate_tower
    )
    small_new, small_m_new, small_v_new = adamw(
        small_params, small_sum, small_m, small_v, rate_small
    )
    loss_parts = jnp.stack([loss_sum, sample_total])
    return (
        loss_parts,
        table_new,
        table_m_new,
        table_v_new,
        expert_new,
        expert_m_new,
        expert_v_new,
        gate_new,
        gate_m_new,
        gate_v_new,
        tower_new,
        tower_m_new,
        tower_v_new,
        small_new,
        small_m_new,
        small_v_new,
    )


def solution(mesh):
    placed = (
        P(("rep", "shard"), None, None, None),
        P(("rep", "shard"), None),
        P(),
        P(("rep", "shard"), None),
        P(("rep", "shard"), None),
        P("shard", None),
        P("shard", None),
        P("shard", None),
        P(None, "shard", None),
        P(None, "shard", None),
        P(None, "shard", None),
        P("shard", None),
        P("shard", None),
        P("shard", None),
        P(None, "shard", None),
        P(None, "shard", None),
        P(None, "shard", None),
        P(),
        P(),
        P(),
    )
    return jax.shard_map(
        on_device,
        mesh=mesh,
        in_specs=placed,
        out_specs=(
            P(),
            P("shard", None),
            P("shard", None),
            P("shard", None),
            P(None, "shard", None),
            P(None, "shard", None),
            P(None, "shard", None),
            P("shard", None),
            P("shard", None),
            P("shard", None),
            P(None, "shard", None),
            P(None, "shard", None),
            P(None, "shard", None),
            P(),
            P(),
            P(),
        ),
        check_vma=False,
    )
```

profile of v0, /device:TPU:0, one launch (start us, length us, event | category | flops | bytes accessed | tf_op | source)
XLA Modules:
  0.0 3145.6 jit_solution(8570962733103789053)
XLA Ops:
  15.2 8.2 add.313
  23.3 11.6 add.309
  34.9 8.6 add.302
  49.0 240.2 %scatter_custom_fusion = s32[65536]{0:T(1024)} fusion(s32[65536]{0:T(1024)S(1)} %bitcast.143, s32[65536]{0:T(1024)S(1)} %fusion.46, s32[]{:T(128)} %constant.104.clone.1), kind=kCustom, calls=%fused_computation.136 | custom fusion | bytes 262148 | tf_op jit(solution)/shard_map/scatter | solution.py:129
  289.1 7.8 all-to-all-start
  302.0 11.0 reshape.322
  318.9 243.1 %gather_fusion = bf16[65536,64]{1,0:T(8,128)(2,1)} fusion(bf16[32768,64]{1,0:T(8,128)(2,1)} %reshape.322, s32[65536]{0:T(1024)} %broadcast_clamp_fusion.1), kind=kCustom, calls=%fused_computation | custom fusion | bytes 17039360 | tf_op jit(solution)/shard_map/jit(_take)/gather | solution.py:134
  562.0 21.5 gather.24
  583.5 12.2 copy.197
  595.7 7.7 bitcast_select_fusion.1
  603.4 6.3 all-to-all-start.1
  612.8 213.7 %all-gather = bf16[16,64,40]{1,2,0:T(8,128)(2,1)S(1)} all-gather(bf16[1,64,40]{1,2,0:T(8,128)(2,1)S(1)} %convert_bitcast_fusion), channel_id=1, replica_groups=mesh['rep'=2,'shard'=16] {'shard'}, dimensions={0}, use_global_device_ids=true | all-gather | bytes 87040 | tf_op jit(solution)/shard_map/all_gather | solution.py:118
  826.9 8.4 fusion.18
  835.4 8.8 reshape.358
  844.2 240.0 %scatter_custom_fusion.1 = s32[65536]{0:T(1024)S(1)} fusion(s32[65536]{0:T(1024)} %bitcast.144, s32[65536]{0:T(1024)S(1)} %iota.37, s32[]{:T(128)} %constant.104.clone.1), kind=kCustom, calls=%fused_computation.134 | custom fusion | bytes 262656 | tf_op jit(solution)/shard_map/scatter | solution.py:131
  1084.2 19.4 broadcast_in_dim.70
  1103.7 8.1 copy.207
  1111.8 10.0 convert_element_type.112
  1133.0 48.4 %all_gather.11 = bf16[5,512,64]{2,1,0:T(8,128)(2,1)S(1)} all-gather(bf16[5,32,64]{2,1,0:T(8,128)(2,1)S(1)} %convert_element_type.122), channel_id=1, replica_groups=mesh['rep'=2,'shard'=16] {'shard'}, dimensions={1}, use_global_device_ids=true | all-gather | bytes 348160 | tf_op jit(solution)/shard_map/all_gather | solution.py:119
  1183.1 12.4 copy.198
  1195.5 21.0 reshape.324
  1216.5 225.7 %gather_fusion.1 = bf16[65536,64]{1,0:T(8,128)(2,1)} fusion(bf16[65536,64]{1,0:T(8,128)(2,1)} %reshape.324, s32[65536]{0:T(1024)S(1)} %broadcast_clamp_fusion), kind=kCustom, calls=%fused_computation.1 | custom fusion | bytes 17039360 | tf_op jit(solution)/shard_map/jit(_take)/gather | solution.py:138
  1442.2 45.2 %multiply_reduce_fusion = bf16[1024,16,64]{2,1,0:T(8,128)(2,1)} fusion(f32[1024,16,4]{2,1,0:T(8,128)} %fusion.18, bf16[1024,16,4,64]{3,2,1,0:T(4,128)(2,1)} %bitcast.134, pred[1024,16,4]{2,1,0:T(8,128)(4,1)S(1)} %copy.191), kind=kLoop, calls=%fused_computation.8 | loop fusion | flops 15728640 | bytes 10813440 | tf_op jit(solution)/shard_map/reduce_sum | solution.py:143
  1495.2 21.1 bitcast_multiply_fusion.2
  1516.2 30.5 fusion.13
  1559.0 51.9 %fusion.2 = f32[1024,5,8]{2,1,0:T(8,128)} fusion(f32[1024,5,512]{2,0,1:T(8,128)} %convolution_bitcast_fusion.1, f32[8,1024,512]{2,1,0:T(8,128)} %get-tuple-element.144), kind=kOutput, calls=%fused_computation.9 | convolution fusion | flops 251658240 | bytes 27426816 | tf_op jit(solution)/shard_map/skh,esh->ske/dot_general | solution.py:196
  1610.9 28.7 fusion.4
  1642.2 14.3 convert_reduce_fusion
  1659.8 12.8 fusion.89
  1677.5 8.1 copy.215
  1685.6 13.9 mul.380
  1699.4 23.1 broadcast_multiply_fusion
  1722.5 226.0 %gather_fusion.2 = f32[65536,64]{1,0:T(8,128)} fusion(f32[65536,64]{1,0:T(8,128)} %broadcast_multiply_fusion, s32[65536]{0:T(1024)S(1)} %copy-done.19), kind=kCustom, calls=%fused_computation.2 | custom fusion | bytes 33816576 | tf_op jit(solution)/shard_map/jit(_take)/gather | solution.py:217
  1948.6 26.7 gather.28
  1975.3 17.6 copy.216
  1993.0 12.0 bitcast_select_fusion
  2010.3 14.6 convolution_bitcast_fusion
  2024.9 17.6 copy.221
  2045.1 8.0 fusion.84
  2053.1 321.3 %all-to-all-done.2 = f32[16,2048,128]{1,2,0:T(8,128)} async-done(((f32[16,2048,128]{1,2,0:T(8,128)}), f32[16,2048,128]{1,2,0:T(8,128)}, u32[]{:S(2)}, u32[]{:S(2)}) %all-to-all-start.2) | async-done | bytes 16777248 | tf_op jit(solution)/shard_map/all_to_all | solution.py:220
  2374.4 17.7 copy.217
  2392.1 24.4 reshape.405
  2416.5 354.1 %scatter_custom_fusion.2 = f32[32768,64]{1,0:T(8,128)} fusion(s32[65536]{0:T(1024)} %bitcast.142, f32[65536,64]{1,0:T(8,128)} %reshape.405, f32[]{:T(128)} %constant.192.clone.1), kind=kCustom, calls=%fused_computation.36 | custom fusion | flops 4194304 | bytes 8389120 | tf_op jit(solution)/shard_map/scatter-add | solution.py:221
  2770.6 13.7 reshape.327
  2787.1 140.3 %all-reduce = (f32[1]{0:T(128)}, f32[4741]{0:T(1024)}) all-reduce(f32[1]{0:T(128)} %bitcast.20, f32[4741]{0:T(1024)S(1)} %concatenate.3), channel_id=1, replica_groups=mesh['rep'=2,'shard'=16] {'rep','shard'}, use_global_device_ids=true, to_apply=%region_9.10 | all-reduce | flops 4742 | bytes 37936 | tf_op jit(solution)/shard_map/psum | solution.py:240
  2930.8 13.6 all-reduce.1
  2946.6 162.4 %all-reduce.5.cloned.1.call-done = (f32[16384,128]{1,0:T(8,128)}, f32[8,64,512]{2,0,1:T(8,128)}) async-done(((f32[16384,128]{1,0:T(8,128)}, f32[8,64,512]{2,0,1:T(8,128)}), (f32[16384,128]{1,0:T(8,128)}, f32[8,64,512]{2,0,1:T(8,128)})) %all-reduce.5.cloned.1.call-update) | async-done | bytes 9437200 | tf_op jit(solution)/shard_map/psum | solution.py:224
  3117.3 21.6 add_subtract_fusion
  (164 shorter events, 94.8 us)
Async XLA Ops:
  49.0 264.1 %copy-start.18 = (s32[65536,1]{0,1:T(1,128)}, s32[65536,1]{0,1:T(1,128)S(1)}, u32[]{:S(2)}) copy-start(s32[65536,1]{0,1:T(1,128)S(1)} %compare_select_fusion.2) | copy-start | bytes 786436
  289.1 23.9 all-to-all-start
  313.1 1.8 copy-start.11
  603.4 6.4 copy-start.5
  603.4 7.3 copy-start.39
  603.4 8.5 copy-start.25
  603.4 9.4 slice-start
  603.4 9.4 copy-start.21
  603.4 9.4 copy-start.27
  603.4 223.3 %copy-start.30 = (s32[1024,16]{0,1:T(8,128)S(1)}, s32[1024,16]{0,1:T(8,128)}, u32[]{:S(2)}) copy-start(s32[1024,16]{0,1:T(8,128)} %param.21) | copy-start | bytes 196612
  603.4 579.7 %all-to-all-start.1 = ((bf16[16,2048,128]{1,2,0:T(8,128)(2,1)}), bf16[16,2048,128]{1,2,0:T(8,128)(2,1)}, u32[]{:S(2)}, u32[]{:S(2)}) async-start(bf16[16,2048,128]{1,2,0:T(8,128)(2,1)} %bitcast_select_fusion.1), calls=%async_computation.1 | async-start | bytes 16777216 | tf_op jit(solution)/shard_map/all_to_all | solution.py:137
  609.7 885.4 %all-gather.3.cloned.1.call-start = ((), (), s32[]{:S(2)}) async-start(), calls=%async_computation.6 | async-start | bytes 8912896 | tf_op jit(solution)/shard_map/all_gather | solution.py:117
  835.4 276.4 %copy-start.17 = (s32[128,512]{1,0:T(8,128)S(1)}, s32[128,512]{1,0:T(8,128)}, u32[]{:S(2)}) copy-start(s32[128,512]{1,0:T(8,128)} %get-tuple-element.137) | copy-start | bytes 786436
  1491.8 24.4 copy-start.2
  1492.4 180.2 %copy-start.9 = (f32[1024,5,8]{0,2,1:T(8,128)}, f32[1024,5,8]{0,2,1:T(8,128)S(1)}, u32[]{:S(2)}) copy-start(f32[1024,5,8]{0,2,1:T(8,128)S(1)} %broadcast_divide_fusion) | copy-start | bytes 491524
  1495.2 21.1 copy-start
  1546.8 5.8 copy-start.1
  1546.8 3.6 copy-start.31
  1546.8 3.6 copy-start.32
  1552.6 0.8 copy-start.7
  1642.2 30.4 copy-start.12
  1656.4 3.4 copy-start.4
  1685.6 13.9 copy-start.14
  1699.4 23.1 copy-start.19
  1975.3 17.6 copy-start.20
  2005.0 5.3 copy-start.3
  2005.0 369.4 %all-to-all-start.2 = ((f32[16,2048,128]{1,2,0:T(8,128)}), f32[16,2048,128]{1,2,0:T(8,128)}, u32[]{:S(2)}, u32[]{:S(2)}) async-start(f32[16,2048,128]{1,2,0:T(8,128)} %bitcast_select_fusion), calls=%async_computation.2 | async-start | bytes 33554432 | tf_op jit(solution)/shard_map/all_to_all | solution.py:220
  2010.3 774.2 %reduce-scatter.6.cloned.1.call-start = ((), (), s32[]{:S(2)}) async-start(), calls=%async_computation.7 | async-start | bytes 17825792 | tf_op jit(solution)/shard_map/reduce_scatter | solution.py:227
  2042.5 0.9 copy-start.10
  2042.5 1.0 copy-start.13
  2042.5 2.6 copy-start.8
  2042.5 887.5 %reduce-scatter.10.cloned.1.call-start = ((), (), s32[]{:S(2)}) async-start(), calls=%async_computation.9 | async-start | bytes 557056
  2045.0 885.8 %reduce-scatter.8.cloned.1.call-start = ((), (), s32[]{:S(2)}) async-start(), calls=%async_computation.8 | async-start | bytes 1392640 | tf_op jit(solution)/shard_map/reduce_scatter | solution.py:229
  2053.1 1055.9 %all-reduce.5.cloned.1.call-start = ((), (), s32[]{:S(2)}) async-start(), calls=%async_computation.10 | async-start | bytes 18874368 | tf_op jit(solution)/shard_map/psum | solution.py:224
  2784.3 1.3 copy-start.37
  2784.3 2.0 copy-start.29
  2784.3 144.3 %copy-start.26 = (f32[4741]{0:T(1024)S(1)}, f32[4741]{0:T(1024)}, u32[]{:S(2)}) copy-start(f32[4741]{0:T(1024)} %param.37) | copy-start | bytes 56896
  2784.3 144.3 %copy-start.33 = (f32[4741]{0:T(1024)S(1)}, f32[4741]{0:T(1024)}, u32[]{:S(2)}) copy-start(f32[4741]{0:T(1024)} %param.38) | copy-start | bytes 56896
  2784.4 144.3 %copy-start.34 = (f32[4741]{0:T(1024)S(1)}, f32[4741]{0:T(1024)}, u32[]{:S(2)}) copy-start(f32[4741]{0:T(1024)} %param.39) | copy-start | bytes 56896
  2784.4 160.1 %copy-start.28 = (f32[64,40]{0,1:T(8,128)S(1)}, f32[64,40]{0,1:T(8,128)}, u32[]{:S(2)}) copy-start(f32[64,40]{0,1:T(8,128)} %param.31) | copy-start | bytes 30724
  2784.4 160.1 %copy-start.35 = (f32[64,40]{0,1:T(8,128)S(1)}, f32[64,40]{0,1:T(8,128)}, u32[]{:S(2)}) copy-start(f32[64,40]{0,1:T(8,128)} %param.32) | copy-start | bytes 30724
  2784.4 160.1 %copy-start.36 = (f32[64,40]{0,1:T(8,128)S(1)}, f32[64,40]{0,1:T(8,128)}, u32[]{:S(2)}) copy-start(f32[64,40]{0,1:T(8,128)} %param.33) | copy-start | bytes 30724
  2784.4 161.4 %copy-start.22 = (f32[5,32,64]{2,1,0:T(8,128)S(1)}, f32[5,32,64]{2,1,0:T(8,128)}, u32[]{:S(2)}) copy-start(f32[5,32,64]{2,1,0:T(8,128)} %param.34) | copy-start | bytes 122884
  2784.4 161.4 %copy-start.23 = (f32[5,32,64]{2,1,0:T(8,128)S(1)}, f32[5,32,64]{2,1,0:T(8,128)}, u32[]{:S(2)}) copy-start(f32[5,32,64]{2,1,0:T(8,128)} %param.35) | copy-start | bytes 122884
  2784.4 161.4 %copy-start.24 = (f32[5,32,64]{2,1,0:T(8,128)S(1)}, f32[5,32,64]{2,1,0:T(8,128)}, u32[]{:S(2)}) copy-start(f32[5,32,64]{2,1,0:T(8,128)} %param.36) | copy-start | bytes 122884
  2784.4 324.6 %copy-start.6 = (f32[8,64,512]{2,1,0:T(8,128)S(1)}, f32[8,64,512]{2,1,0:T(8,128)}, u32[]{:S(2)}) copy-start(f32[8,64,512]{2,1,0:T(8,128)} %param.28) | copy-start | bytes 3145732
  2784.4 324.5 %copy-start.15 = (f32[8,64,512]{2,1,0:T(8,128)S(1)}, f32[8,64,512]{2,1,0:T(8,128)}, u32[]{:S(2)}) copy-start(f32[8,64,512]{2,1,0:T(8,128)} %param.29) | copy-start | bytes 3145732
  2784.5 324.5 %copy-start.16 = (f32[8,64,512]{2,1,0:T(8,128)S(1)}, f32[8,64,512]{2,1,0:T(8,128)}, u32[]{:S(2)}) copy-start(f32[8,64,512]{2,1,0:T(8,128)} %param.30) | copy-start | bytes 3145732
  (1 other events, 0.7 us)
Sparse Core Ops, SparseCore 0:
  613.3 183.2 all-gather.2
  2042.6 428.5 reduce-scatter.5
  2475.3 54.7 reduce-scatter.9
  2534.6 57.4 reduce-scatter.7
  2784.6 324.2 all-reduce.4
where the time goes:
time: 3160 us; the launch traced here: 3150 us
  local copies, waits for them, and re-layouts  1510 us (48%)
  other arithmetic  513 us (16%)
  waiting for transfers between devices  484 us (15%)
  blocking collectives  416 us (13%)
  matrix products  185 us (6%)
    scatter-add x1, other arithmetic, on_device(): jax.ops.segment_sum(arrived.reshape(slot_count, WIDTH), wanted_flat, num_...  354 us
    all_to_all x1, waiting for transfers between devices, on_device(): lax.all_to_all(sent_grad, 'shard', split_axis=0, concat_axis=0, tiled=True)  321 us
    gather x3, local copies, waits for them, and re-layouts, on_device(): jnp.take(table_rows, wanted_flat, axis=0)  277 us
    gather x3, local copies, waits for them, and re-layouts, on_device(): jnp.take(slot_grad, sort_order, axis=0)  270 us
    scatter x1, local copies, waits for them, and re-layouts, on_device(): jnp.zeros((slot_count,), jnp.int32).at[destination].set(local_key)  240 us
    scatter x1, local copies, waits for them, and re-layouts, on_device(): jnp.zeros((slot_count,), jnp.int32).at[destination].set(slot_index)  240 us
    gather x1, local copies, waits for them, and re-layouts, on_device(): looked = jnp.take(replies.reshape(slot_count, WIDTH), destination, axis=0)  226 us
    all_gather x1, blocking collectives, on_device(): lax.all_gather(dense_parts[1], 'shard', axis=0, tiled=True)  214 us
  transfers between devices with their start and end apart: 8, of which 2 were waited for; matrix products, arithmetic and copies ran while one was open for 35% of the time, Pallas kernels for 0%

commit v1 on v0

v1 whole, which is shorter than its diff:
```python
import functools

import jax
import jax.numpy as jnp
from jax import lax
from jax.experimental import pallas as pl
from jax.experimental.pallas import tpu as pltpu
from jax.sharding import PartitionSpec as P

TABLES = 2
WIDTH = 64
ROW_BASE = 1024
EXPERTS = 8
HID = 512
TASKS = 5
TOWER = 64
STEP = 10
LANES = 128
UNROLL = 16
VMEM_BYTES = 60 << 20

beta_first = 0.9
beta_second = 0.999
adam_epsilon = 1e-08
weight_decay = 0.01
rate_table = 1.0
rate_expert = 0.06
rate_gate = 0.03
rate_tower = 0.08
rate_small = 0.5


def adamw(weight, grad, first, second, rate):
    first_new = beta_first * first + (1.0 - beta_first) * grad
    second_new = beta_second * second + (1.0 - beta_second) * grad * grad
    first_hat = first_new / (1.0 - beta_first**STEP)
    second_hat = second_new / (1.0 - beta_second**STEP)
    weight_new = weight - rate * (
        first_hat / (jnp.sqrt(second_hat) + adam_epsilon) + weight_decay * weight
    )
    return (weight_new, first_new, second_new)


def left_lanes(rows=1):
    return lax.broadcasted_iota(jnp.int32, (rows, LANES), 1) < WIDTH


def params(**kw):
    return pltpu.CompilerParams(vmem_limit_bytes=VMEM_BYTES, **kw)


def owner_gather_kernel(distinct, want_ref, table_ref, out_ref, rows_ref):
    left = left_lanes()

    def body(step, carry):
        base = step * UNROLL
        for u in range(UNROLL):
            first = table_ref[pl.ds(want_ref[2 * (base + u)], 1), :]
            second = table_ref[pl.ds(want_ref[2 * (distinct + base + u)], 1), :]
            rows_ref[pl.ds(base + u, 1), :] = jnp.where(left, first, second)
        return carry

    lax.fori_loop(0, distinct // UNROLL, body, 0)
    out_ref[0] = rows_ref[...].astype(jnp.bfloat16)


def owner_gather(wanted, table, shards, distinct):
    rows = table.shape[0]
    return pl.pallas_call(
        functools.partial(owner_gather_kernel, distinct),
        name="owner_gather",
        grid=(shards,),
        in_specs=[
            pl.BlockSpec((4 * distinct,), lambda i: (i,), memory_space=pltpu.SMEM),
            pl.BlockSpec((rows, LANES), lambda i: (0, 0), pipeline_mode=pl.Buffered(1)),
        ],
        out_specs=pl.BlockSpec((1, distinct, LANES), lambda i: (i, 0, 0)),
        out_shape=jax.ShapeDtypeStruct((shards, distinct, LANES), jnp.bfloat16),
        scratch_shapes=[pltpu.VMEM((distinct, LANES), jnp.float32)],
        compiler_params=params(),
    )(wanted, table)


def pool_kernel(samples, longest, q0_ref, q1_ref, reply_ref, out_ref, rows_ref, sum_ref):
    count = reply_ref.shape[0]

    @pl.when(pl.program_id(0) == 0)
    def _():
        rows_ref[0:count, :] = reply_ref[...].astype(jnp.float32)
        rows_ref[count : count + 8, :] = jnp.zeros((8, LANES), jnp.float32)

    left = left_lanes()
    unroll = UNROLL // 4

    def summed(index_ref, s):
        total = rows_ref[pl.ds(index_ref[s], 1), :]
        for slot in range(1, longest):
            total = total + rows_ref[pl.ds(index_ref[slot * samples + s], 1), :]
        return total

    def body(step, carry):
        for u in range(unroll):
            s = step * unroll + u
            sum_ref[pl.ds(s, 1), :] = jnp.where(left, summed(q0_ref, s), summed(q1_ref, s))
        return carry

    lax.fori_loop(0, samples // unroll, body, 0)
    out_ref[0] = sum_ref[...].astype(jnp.bfloat16)


def pool(places, replies, samples, longest, pairs):
    count = replies.shape[0]
    return pl.pallas_call(
        functools.partial(pool_kernel, samples, longest),
        name="pool",
        grid=(pairs,),
        in_specs=[
            pl.BlockSpec((longest * samples,), lambda i: (i,), memory_space=pltpu.SMEM),
            pl.BlockSpec((longest * samples,), lambda i: (i + pairs,), memory_space=pltpu.SMEM),
            pl.BlockSpec((count, LANES), lambda i: (0, 0), pipeline_mode=pl.Buffered(1)),
        ],
        out_specs=pl.BlockSpec((1, samples, LANES), lambda i: (i, 0, 0)),
        out_shape=jax.ShapeDtypeStruct((pairs, samples, LANES), jnp.bfloat16),
        scratch_shapes=[
            pltpu.VMEM((count + 8, LANES), jnp.float32),
            pltpu.VMEM((samples, LANES), jnp.float32),
        ],
        compiler_params=params(),
    )(places, places, replies)


def grad_gather_kernel(distinct, index_ref, grad_ref, out_ref, grads_ref, rows_ref):
    count = grad_ref.shape[0]

    @pl.when(pl.program_id(0) == 0)
    def _():
        grads_ref[0:count, :] = grad_ref[...]
        grads_ref[count : count + 8, :] = jnp.zeros((8, LANES), jnp.float32)

    left = left_lanes()
    unroll = UNROLL // 2

    def both(at):
        first = grads_ref[pl.ds(index_ref[at], 1), :]
        return first + grads_ref[pl.ds(index_ref[at + 1], 1), :]

    def body(step, carry):
        for u in range(unroll):
            r = step * unroll + u
            rows_ref[pl.ds(r, 1), :] = jnp.where(left, both(2 * r), both(2 * (distinct + r)))
        return carry

    lax.fori_loop(0, distinct // unroll, body, 0)
    out_ref[0] = rows_ref[...].astype(jnp.bfloat16)


def grad_gather(index, grads, shards, distinct):
    count = grads.shape[0]
    return pl.pallas_call(
        functools.partial(grad_gather_kernel, distinct),
        name="grad_gather",
        grid=(shards,),
        in_specs=[
            pl.BlockSpec((4 * distinct,), lambda i: (i,), memory_space=pltpu.SMEM),
            pl.BlockSpec((count, LANES), lambda i: (0, 0), pipeline_mode=pl.Buffered(1)),
        ],
        out_specs=pl.BlockSpec((1, distinct, LANES), lambda i: (i, 0, 0)),
        out_shape=jax.ShapeDtypeStruct((shards, distinct, LANES), jnp.bfloat16),
        scratch_shapes=[
            pltpu.VMEM((count + 8, LANES), jnp.float32),
            pltpu.VMEM((distinct, LANES), jnp.float32),
        ],
        compiler_params=params(),
    )(index, grads)


def scatter_kernel(distinct, want_ref, got_ref, out_ref, sum0_ref, sum1_ref, rows_ref):

    @pl.when(pl.program_id(0) == 0)
    def _():
        sum0_ref[...] = jnp.zeros_like(sum0_ref)
        sum1_ref[...] = jnp.zeros_like(sum1_ref)

    rows_ref[...] = got_ref[0].astype(jnp.float32)

    def body(step, carry):
        base = step * UNROLL
        span = range(UNROLL)
        at0 = [want_ref[2 * (base + u)] for u in span]
        at1 = [want_ref[2 * (distinct + base + u)] for u in span]
        came = [rows_ref[pl.ds(base + u, 1), :] for u in span]
        new0 = [sum0_ref[pl.ds(at0[u], 1), :] + came[u] for u in span]
        new1 = [sum1_ref[pl.ds(at1[u], 1), :] + came[u] for u in span]
        for u in span:
            sum0_ref[pl.ds(at0[u], 1), :] = new0[u]
        for u in span:
            sum1_ref[pl.ds(at1[u], 1), :] = new1[u]
        return carry

    lax.fori_loop(0, distinct // UNROLL, body, 0)

    @pl.when(pl.program_id(0) == pl.num_programs(0) - 1)
    def _():
        out_ref[...] = jnp.where(left_lanes(), sum0_ref[...], sum1_ref[...]).astype(jnp.bfloat16)


def scatter(wanted, arrived, rows):
    shards, distinct = arrived.shape[:2]
    return pl.pallas_call(
        functools.partial(scatter_kernel, distinct),
        name="scatter",
        grid=(shards,),
        in_specs=[
            pl.BlockSpec((4 * distinct,), lambda i: (i,), memory_space=pltpu.SMEM),
            pl.BlockSpec((1, distinct, LANES), lambda i: (i, 0, 0)),
        ],
        out_specs=pl.BlockSpec((rows, LANES), lambda i: (0, 0)),
        out_shape=jax.ShapeDtypeStruct((rows, LANES), jnp.bfloat16),
        scratch_shapes=[
            pltpu.VMEM((rows, LANES), jnp.float32),
            pltpu.VMEM((rows, LANES), jnp.float32),
            pltpu.VMEM((distinct, LANES), jnp.float32),
        ],
        compiler_params=params(),
    )(wanted, arrived)


def group_reduce(value, op):
    lane = lax.broadcasted_iota(jnp.int32, value.shape, 1)
    shift = 1
    while shift < EXPERTS:
        other = jnp.where(
            (lane & shift) != 0,
            pltpu.roll(value, shift, 1),
            pltpu.roll(value, LANES - shift, 1),
        )
        value = op(value, other)
        shift *= 2
    return value


def tower_spot(k, depth):
    half = depth // 2
    return (0 if k < 3 else half), (k % 3 + 1) * LANES


def dense_kernel(
    shards,
    pooled_ref,
    weight_ref,
    bias_ref,
    tower_bias_ref,
    head_ref,
    head_bias_ref,
    live_ref,
    label_ref,
    scale_ref,
    grad_ref,
    expert_grad_ref,
    x_out_ref,
    gate_grad_ref,
    tower_grad_ref,
    small_ref,
    x_ref,
    out_ref,
    slope_ref,
    mixed_ref,
    mixed_grad_ref,
    gates_ref,
    gate_prob_ref,
    tower_ref,
):
    pairs = pooled_ref.shape[0]
    block = pooled_ref.shape[1]
    depth = weight_ref.shape[1] // shards
    half = depth // 2
    step = pl.program_id(0)

    @pl.when(step == 0)
    def _():
        for k in range(TASKS):
            row, col = tower_spot(k, depth)
            for i in range(shards):
                tower_ref[k, i * half : (i + 1) * half, :] = weight_ref[
                    EXPERTS, i * depth + row : i * depth + row + half, col : col + TOWER
                ]
        small_ref[...] = jnp.zeros_like(small_ref)
        tower_grad_ref[...] = jnp.zeros_like(tower_grad_ref)

    left = left_lanes(block)
    for m in range(pairs // 2):
        even = pooled_ref[2 * m].astype(jnp.float32)
        odd = pooled_ref[2 * m + 1].astype(jnp.float32)
        low = jnp.where(left, even, pltpu.roll(odd, WIDTH, 1)).astype(jnp.bfloat16)
        high = jnp.where(left, pltpu.roll(even, WIDTH, 1), odd).astype(jnp.bfloat16)
        x_ref[:, m * LANES : (m + 1) * LANES] = low
        high_at = (m + pairs // 2) * LANES
        x_ref[:, high_at : high_at + LANES] = high
    x_out_ref[...] = x_ref[...]

    logits = jnp.dot(
        x_ref[...], weight_ref[EXPERTS, :, 0:LANES], preferred_element_type=jnp.float32
    )
    top = group_reduce(logits, jnp.maximum)
    powers = jnp.exp(logits - top)
    gates_ref[...] = powers / group_reduce(powers, jnp.add)

    def expert(e, carry):
        pre = jnp.dot(x_ref[...], weight_ref[e], preferred_element_type=jnp.float32)
        pre = pre + bias_ref[e]
        sigma = jax.nn.sigmoid(pre)
        out = pre * sigma
        out_ref[e] = out
        slope_ref[e] = sigma + out * (1.0 - sigma)
        return carry

    lax.fori_loop(0, EXPERTS, expert, 0)

    def mix(c, carry):
        rows = pl.ds(c * 16, 16)
        gates = gates_ref[rows, :]
        for part in range(2):
            cols = slice(part * 256, (part + 1) * 256)
            totals = [None] * TASKS
            for e in range(EXPERTS):
                out = out_ref[e, rows, cols]
                for k in range(TASKS):
                    at = k * EXPERTS + e
                    term = out * gates[:, at : at + 1]
                    totals[k] = term if totals[k] is None else totals[k] + term
            for k in range(TASKS):
                mixed_ref[k, rows, cols] = totals[k].astype(jnp.bfloat16)
        return carry

    lax.fori_loop(0, block // 16, mix, 0)

    lane = lax.broadcasted_iota(jnp.int32, (block, LANES), 1)
    towers = []
    logit = jnp.zeros((block, LANES), jnp.float32)
    for k in range(TASKS):
        pre = jnp.dot(mixed_ref[k], tower_ref[k], preferred_element_type=jnp.float32)
        pre = pre + tower_bias_ref[k : k + 1, :]
        sigma = jax.nn.sigmoid(pre)
        out = pre * sigma
        towers.append((out, sigma + out * (1.0 - sigma)))
        score = jnp.sum(out * head_ref[k : k + 1, :], axis=1, keepdims=True)
        logit = jnp.where(lane == k, score + head_bias_ref[k], logit)
    live = live_ref[...]
    label = label_ref[...]
    softplus = jnp.maximum(logit, 0.0) + jnp.log1p(jnp.exp(-jnp.abs(logit)))
    losses = live * (softplus - label * logit)
    logit_grad = live * (jax.nn.sigmoid(logit) - label) * scale_ref[0]
    small_ref[2 * TASKS : 2 * TASKS + 1, :] += jnp.sum(logit_grad, axis=0, keepdims=True)
    small_ref[2 * TASKS + 1 : 2 * TASKS + 2, :] += jnp.sum(losses, axis=0, keepdims=True)
    for k in range(TASKS):
        out, slope = towers[k]
        signal = logit_grad[:, k : k + 1]
        small_ref[k : k + 1, 0:TOWER] += jnp.sum(signal * out, axis=0, keepdims=True)
        pre_grad = (signal * head_ref[k : k + 1, :] * slope).astype(jnp.bfloat16)
        small_ref[TASKS + k : TASKS + k + 1, 0:TOWER] += jnp.sum(
            pre_grad.astype(jnp.float32), axis=0, keepdims=True
        )
        tower_grad_ref[k] += lax.dot_general(
            mixed_ref[k], pre_grad, (((0,), (0,)), ((), ())), preferred_element_type=jnp.float32
        )
        mixed_grad_ref[k] = lax.dot_general(
            pre_grad, tower_ref[k], (((1,), (1,)), ((), ())), preferred_element_type=jnp.float32
        )

    lane8 = lax.broadcasted_iota(jnp.int32, (8, LANES), 1)

    def gate_back(c, carry):
        rows = pl.ds(c * 8, 8)
        totals = [[None] * EXPERTS for _ in range(TASKS)]
        for part in range(HID // LANES):
            cols = slice(part * LANES, (part + 1) * LANES)
            mixed = [mixed_grad_ref[k, rows, cols] for k in range(TASKS)]
            for e in range(EXPERTS):
                out = out_ref[e, rows, cols]
                for k in range(TASKS):
                    term = mixed[k] * out
                    totals[k][e] = term if totals[k][e] is None else totals[k][e] + term
        result = jnp.zeros((8, LANES), jnp.float32)
        for k in range(TASKS):
            for e in range(EXPERTS):
                value = jnp.sum(totals[k][e], axis=1, keepdims=True)
                result = jnp.where(lane8 == k * EXPERTS + e, value, result)
        gate_prob_ref[rows, :] = result
        return carry

    lax.fori_loop(0, block // 8, gate_back, 0)
    gates = gates_ref[...]
    weighed = gates * gate_prob_ref[...]
    gate_pre = weighed - gates * group_reduce(weighed, jnp.add)
    gate_grad_ref[...] = gate_pre.astype(jnp.bfloat16)

    def expert_back(c, carry):
        rows = pl.ds(c * 16, 16)
        gates = gates_ref[rows, :]
        for e in range(EXPERTS):
            column = [gates[:, k * EXPERTS + e : k * EXPERTS + e + 1] for k in range(TASKS)]
            for part in range(2):
                cols = slice(part * 256, (part + 1) * 256)
                total = None
                for k in range(TASKS):
                    term = mixed_grad_ref[k, rows, cols] * column[k]
                    total = term if total is None else total + term
                expert_grad_ref[e, rows, cols] = (total * slope_ref[e, rows, cols]).astype(
                    jnp.bfloat16
                )
        return carry

    lax.fori_loop(0, block // 16, expert_back, 0)

    transposed = (((1,), (1,)), ((), ()))
    for m in range(pairs // 2):
        low_at, high_at = m * LANES, (m + pairs // 2) * LANES
        parts = []
        for at in (low_at, high_at):
            total = lax.dot_general(
                gate_grad_ref[...],
                weight_ref[EXPERTS, at : at + LANES, 0:LANES],
                transposed,
                preferred_element_type=jnp.float32,
            )
            for e in range(EXPERTS):
                total = total + lax.dot_general(
                    expert_grad_ref[e],
                    weight_ref[e, at : at + LANES, :],
                    transposed,
                    preferred_element_type=jnp.float32,
                )
            parts.append(total)
        low, high = parts
        grad_ref[2 * m] = jnp.where(left, low, pltpu.roll(high, WIDTH, 1))
        grad_ref[2 * m + 1] = jnp.where(left, pltpu.roll(low, WIDTH, 1), high)


def dense(pooled, weights, bias, tower_bias, head, head_bias, live, label, scale, shards):
    pairs, samples = pooled.shape[:2]
    slabs, inner = weights.shape[:2]
    block = 256
    whole = lambda *shape: pl.BlockSpec(
        shape, lambda i: (0,) * len(shape), pipeline_mode=pl.Buffered(1)
    )
    kept = lambda *shape: pl.BlockSpec(shape, lambda i: (0,) * len(shape))
    smem = pl.BlockSpec(memory_space=pltpu.SMEM)
    f32, bf16 = jnp.float32, jnp.bfloat16
    return pl.pallas_call(
        functools.partial(dense_kernel, shards),
        name="dense",
        grid=(samples // block,),
        in_specs=[
            pl.BlockSpec((pairs, block, LANES), lambda i: (0, i, 0)),
            whole(slabs, inner, HID),
            whole(EXPERTS, 1, HID),
            whole(TASKS, TOWER),
            whole(TASKS, TOWER),
            smem,
            pl.BlockSpec((block, LANES), lambda i: (i, 0)),
            pl.BlockSpec((block, LANES), lambda i: (i, 0)),
            smem,
        ],
        out_specs=[
            pl.BlockSpec((pairs, block, LANES), lambda i: (0, i, 0)),
            pl.BlockSpec((EXPERTS, block, HID), lambda i: (0, i, 0)),
            pl.BlockSpec((block, inner), lambda i: (i, 0)),
            pl.BlockSpec((block, LANES), lambda i: (i, 0)),
            kept(TASKS, HID, TOWER),
            kept(16, LANES),
        ],
        out_shape=[
            jax.ShapeDtypeStruct((pairs, samples, LANES), f32),
            jax.ShapeDtypeStruct((EXPERTS, samples, HID), bf16),
            jax.ShapeDtypeStruct((samples, inner), bf16),
            jax.ShapeDtypeStruct((samples, LANES), bf16),
            jax.ShapeDtypeStruct((TASKS, HID, TOWER), f32),
            jax.ShapeDtypeStruct((16, LANES), f32),
        ],
        scratch_shapes=[
            pltpu.VMEM((block, inner), bf16),
            pltpu.VMEM((EXPERTS, block, HID), f32),
            pltpu.VMEM((EXPERTS, block, HID), f32),
            pltpu.VMEM((TASKS, block, HID), bf16),
            pltpu.VMEM((TASKS, block, HID), f32),
            pltpu.VMEM((block, LANES), f32),
            pltpu.VMEM((block, LANES), f32),
            pltpu.VMEM((TASKS, HID, TOWER), bf16),
        ],
        compiler_params=params(),
    )(pooled, weights, bias, tower_bias, head, head_bias, live, label, scale)


def weight_grad_kernel(
    shards, x_ref, expert_ref, gate_ref, tower_ref, out_ref, bias_ref, turned_ref
):
    step = pl.program_id(0)
    inner = x_ref.shape[1]
    depth = inner // shards
    half = depth // 2

    @pl.when(step == 0)
    def _():
        turned_ref[...] = x_ref[...].T

    @pl.when(step < EXPERTS)
    def _():
        grad = jnp.dot(turned_ref[...], expert_ref[0], preferred_element_type=jnp.float32)
        out_ref[0] = grad.astype(jnp.bfloat16)
        bias_ref[0] = jnp.sum(expert_ref[0].astype(jnp.float32), axis=0, keepdims=True)

    @pl.when(step == EXPERTS)
    def _():
        bias_ref[...] = jnp.zeros_like(bias_ref)
        out_ref[...] = jnp.zeros_like(out_ref)
        grad = jnp.dot(turned_ref[...], gate_ref[...], preferred_element_type=jnp.float32)
        out_ref[0, :, 0:LANES] = grad.astype(jnp.bfloat16)
        for k in range(TASKS):
            row, col = tower_spot(k, depth)
            for i in range(shards):
                out_ref[0, i * depth + row : i * depth + row + half, col : col + TOWER] = tower_ref[
                    k, i * half : (i + 1) * half, :
                ].astype(jnp.bfloat16)


def weight_grads(x, expert_grad, gate_grad, tower_grad, shards):
    samples, inner = x.shape
    whole = lambda *shape: pl.BlockSpec(
        shape, lambda i: (0,) * len(shape), pipeline_mode=pl.Buffered(1)
    )
    return pl.pallas_call(
        functools.partial(weight_grad_kernel, shards),
        name="weight_grads",
        grid=(EXPERTS + 1,),
        in_specs=[
            whole(samples, inner),
            pl.BlockSpec((1, samples, HID), lambda i: (jnp.minimum(i, EXPERTS - 1), 0, 0)),
            whole(samples, LANES),
            whole(TASKS, HID, TOWER),
        ],
        out_specs=[
            pl.BlockSpec((1, inner, HID), lambda i: (i, 0, 0)),
            pl.BlockSpec((1, 1, HID), lambda i: (i, 0, 0)),
        ],
        out_shape=[
            jax.ShapeDtypeStruct((EXPERTS + 1, inner, HID), jnp.bfloat16),
            jax.ShapeDtypeStruct((EXPERTS + 1, 1, HID), jnp.float32),
        ],
        scratch_shapes=[pltpu.VMEM((inner, samples), jnp.bfloat16)],
        compiler_params=params(),
    )(x, expert_grad, gate_grad, tower_grad)


def over_rep(value):
    if lax.axis_size("rep") == 2:
        other = lax.ppermute(value, "rep", [(0, 1), (1, 0)])
        return value.astype(jnp.float32) + other.astype(jnp.float32)
    return lax.psum(value.astype(jnp.float32), "rep")


def pack_extra(gate, tower):
    depth = gate.shape[0]
    half = depth // 2
    slab = jnp.zeros((depth, HID), gate.dtype)
    slab = lax.dynamic_update_slice(slab, gate, (0, 0))
    for k in range(TASKS):
        slab = lax.dynamic_update_slice(slab, tower[k], tower_spot(k, depth))
    return slab


def on_device(
    row_ids,
    bag_lengths,
    sample_counts,
    label_mask,
    labels,
    tables,
    table_m,
    table_v,
    expert_w,
    expert_m,
    expert_v,
    gate_w,
    gate_m,
    gate_v,
    tower_weight_matrix,
    tower_m,
    tower_v,
    small_params,
    small_m,
    small_v,
):
    shards = lax.axis_size("shard")
    device = lax.axis_index("rep") * shards + lax.axis_index("shard")
    samples, bags, longest = row_ids.shape[:3]
    rows_dev = tables.shape[0]
    depth = gate_w.shape[0]
    slots = samples * bags * longest
    capacity = slots // shards
    distinct = capacity // 4
    pairs = bags // TABLES
    int32 = jnp.int32

    own = jnp.concatenate(
        [
            expert_w.astype(jnp.bfloat16),
            pack_extra(gate_w, tower_weight_matrix).astype(jnp.bfloat16)[None],
        ],
        axis=0,
    )
    weights = lax.all_gather(own, "shard", axis=1, tiled=True)

    ids = jnp.transpose(row_ids, (1, 2, 3, 0))
    row = ids[:, :, 0, :] * ROW_BASE + ids[:, :, 1, :]
    table_of = lax.broadcasted_iota(int32, row.shape, 0) // pairs
    key = (row // rows_dev * TABLES + table_of) * rows_dev + row % rows_dev
    place = lax.broadcasted_iota(int32, row.shape, 1)
    unused = (place >= jnp.transpose(bag_lengths)[:, None, :]).astype(int32)
    number = (
        lax.broadcasted_iota(int32, row.shape, 0) * longest + place
    ) * samples + lax.broadcasted_iota(int32, row.shape, 2)
    payload = number + unused * slots
    key, payload = lax.sort(
        (key.reshape(slots), payload.reshape(slots)), num_keys=1, is_stable=False
    )
    position = jnp.arange(slots, dtype=int32)
    skipped = payload >= slots
    number = jnp.where(skipped, payload - slots, payload)
    wanted = lax.all_to_all(
        (key % rows_dev).reshape(shards, capacity), "shard", 0, 0, tiled=True
    ).reshape(slots)
    bag = number // (longest * samples)
    grad_place = jnp.where(skipped, pairs * samples, bag % pairs * samples + number % samples)
    reply_place = jnp.where(
        skipped,
        shards * distinct,
        position // capacity * distinct + position % (2 * distinct) // 2,
    )
    span = 2 * shards * distinct
    places = lax.sort(number * span + reply_place, is_stable=False) % span

    found = owner_gather(wanted, tables, shards, distinct)
    replies = lax.all_to_all(found, "shard", 0, 0, tiled=True).reshape(shards * distinct, LANES)
    pooled = pool(places, replies, samples, longest, pairs)

    first_end = EXPERTS * HID
    second_end = first_end + TASKS * TOWER
    third_end = second_end + TASKS * TOWER
    sample_total = jnp.sum(sample_counts).astype(jnp.float32)
    live_count = jnp.take(sample_counts, device)
    live = (jnp.arange(samples, dtype=int32) < live_count).astype(jnp.float32)[:, None]
    live = jnp.pad(live * label_mask.astype(jnp.float32), ((0, 0), (0, LANES - TASKS)))
    label = jnp.pad(labels.astype(jnp.float32), ((0, 0), (0, LANES - TASKS)))
    pooled_grad, expert_grad, x, gate_grad, tower_grad, sums = dense(
        pooled,
        weights,
        small_params[:first_end].reshape(EXPERTS, 1, HID),
        small_params[first_end:second_end].reshape(TASKS, TOWER),
        small_params[second_end:third_end].reshape(TASKS, TOWER),
        small_params[third_end:],
        live,
        label,
        (1.0 / sample_total).reshape(1),
        shards,
    )

    sent = grad_gather(grad_place, pooled_grad.reshape(pairs * samples, LANES), shards, distinct)
    arrived = lax.all_to_all(sent, "shard", 0, 0, tiled=True)
    table_total = over_rep(scatter(wanted, arrived, rows_dev))
    table_new, table_m_new, table_v_new = adamw(tables, table_total, table_m, table_v, rate_table)

    dense_grad, bias_grad = weight_grads(x, expert_grad, gate_grad, tower_grad, shards)
    owned = over_rep(lax.psum_scatter(dense_grad, "shard", scatter_dimension=1, tiled=True))
    extra = owned[EXPERTS]
    gate_sum = extra[:, : TASKS * EXPERTS]
    half = depth // 2
    spots = [tower_spot(k, depth) for k in range(TASKS)]
    tower_sum = jnp.stack([extra[r : r + half, c : c + TOWER] for r, c in spots])
    expert_new, expert_m_new, expert_v_new = adamw(
        expert_w, owned[:EXPERTS], expert_m, expert_v, rate_expert
    )
    gate_new, gate_m_new, gate_v_new = adamw(gate_w, gate_sum, gate_m, gate_v, rate_gate)
    tower_new, tower_m_new, tower_v_new = adamw(
        tower_weight_matrix, tower_sum, tower_m, tower_v, rate_tower
    )

    small_grad = jnp.concatenate(
        [
            bias_grad[:EXPERTS].reshape(-1),
            sums[TASKS : 2 * TASKS, :TOWER].reshape(-1),
            sums[:TASKS, :TOWER].reshape(-1),
            sums[2 * TASKS, :TASKS],
            jnp.sum(sums[2 * TASKS + 1, :TASKS]).reshape(1),
        ]
    )
    small_size = small_params.shape[0]
    padded = -(-(small_size + 1) // 1024) * 1024
    small_grad = jnp.pad(small_grad, (0, padded - small_size - 1))
    small_all = lax.all_gather(small_grad.reshape(8, padded // 8), ("rep", "shard"))
    small_sum = jnp.sum(small_all, axis=0).reshape(padded)
    small_new, small_m_new, small_v_new = adamw(
        small_params, small_sum[:small_size], small_m, small_v, rate_small
    )
    loss_parts = jnp.stack([small_sum[small_size], sample_total])
    return (
        loss_parts,
        table_new,
        table_m_new,
        table_v_new,
        expert_new,
        expert_m_new,
        expert_v_new,
        gate_new,
        gate_m_new,
        gate_v_new,
        tower_new,
        tower_m_new,
        tower_v_new,
        small_new,
        small_m_new,
        small_v_new,
    )


def solution(mesh):
    by_sample = ("rep", "shard")
    ins = (
        [P(by_sample, None, None, None), P(by_sample, None), P()]
        + [P(by_sample, None)] * 2
        + [P("shard", None)] * 3
        + [P(None, "shard", None)] * 3
        + [P("shard", None)] * 3
        + [P(None, "shard", None)] * 3
        + [P()] * 3
    )
    outs = (
        [P()]
        + [P("shard", None)] * 3
        + [P(None, "shard", None)] * 3
        + [P("shard", None)] * 3
        + [P(None, "shard", None)] * 3
        + [P()] * 3
    )
    return jax.shard_map(
        on_device, mesh=mesh, in_specs=tuple(ins), out_specs=tuple(outs), check_vma=False
    )
```

time: 3160 us -> 746 us (0.24)
  local copies, waits for them, and re-layouts: 1510 us -> 18.7 us
  other arithmetic: 513 us -> 68.2 us
  waiting for transfers between devices: 484 us -> 102 us
  Pallas kernels: 0 us -> 330 us
  blocking collectives: 416 us -> 192 us
  matrix products: 185 us -> 0 us
    gather x7 -> x0, local copies, waits for them, and re-layouts: 773 us -> none  [the longest x3 277 us: on_device(): jnp.take(table_rows, wanted_flat, axis=0)]
    scatter x2 -> x0, local copies, waits for them, and re-layouts: 480 us -> none  [the longest x1 240 us: on_device(): jnp.zeros((slot_count,), jnp.int32).at[destination].set(local_key)]
    scatter-add x1 -> x0, other arithmetic: 354 us -> none  [on_device(): jax.ops.segment_sum(arrived.reshape(slot_count, WIDTH), wanted_flat, num_...]
    pallas_call x0 -> x6, Pallas kernels: none -> 330 us  [the longest x1 95.9 us: dense(): pl.pallas_call(functools.partial(dense_kernel, shards), name='dense', gri...]
    all_to_all x3 -> x1, waiting for transfers between devices: 321 us -> 59.3 us  [on_device(): lax.all_to_all(found, 'shard', 0, 0, tiled=True)]
    all_gather x2 -> x1, blocking collectives: 262 us -> 42.7 us  [on_device(): lax.all_gather(small_grad.reshape(8, padded // 8), ('rep', 'shard'))]
    dot_general x11 -> x0, matrix products: 183 us -> none  [the longest x1 51.9 us: on_device(): jnp.einsum('skh,esh->ske', mixed_grad, expert_out, precision=top_precision)]
    psum x1 -> x0, waiting for transfers between devices: 162 us -> none  [on_device(): table_total = lax.psum(table_grad, 'rep')]
  transfers between devices with their start and end apart: 8 -> 5, of which waited for: 2 -> 2; matrix products, arithmetic and copies ran while one was open for 35% -> 9% of each run, Pallas kernels for 0% -> 30%
where the time goes in v1:
time: 746 us; the launch traced here: 735 us
  Pallas kernels  330 us (44%)
  blocking collectives  192 us (26%)
  waiting for transfers between devices  102 us (14%)
  other arithmetic  68.2 us (9%)
  local copies, waits for them, and re-layouts  18.7 us (3%)
  between operations  16.1 us (2%)
  starting transfers between devices  7.7 us (1%)
    all_to_all x1, blocking collectives, on_device(): arrived = lax.all_to_all(sent, 'shard', 0, 0, tiled=True)  131 us
    pallas_call x1, Pallas kernels, dense(): pl.pallas_call(functools.partial(dense_kernel, shards), name='dense', gri...  95.9 us
    pallas_call x1, Pallas kernels, grad_gather(): pl.pallas_call(functools.partial(grad_gather_kernel, distinct), name='gra...  67.8 us
    pallas_call x1, Pallas kernels, pool(): pl.pallas_call(functools.partial(pool_kernel, samples, longest), name='po...  60.3 us
    all_to_all x1, waiting for transfers between devices, on_device(): lax.all_to_all(found, 'shard', 0, 0, tiled=True)  59.3 us
    pallas_call x1, Pallas kernels, scatter(): pl.pallas_call(functools.partial(scatter_kernel, distinct), name='scatter...  51.9 us
    ppermute x2, waiting for transfers between devices, over_rep(): other = lax.ppermute(value, 'rep', [(0, 1), (1, 0)])  43.1 us
    all_gather x1, blocking collectives, on_device(): lax.all_gather(small_grad.reshape(8, padded // 8), ('rep', 'shard'))  42.7 us
  transfers between devices with their start and end apart: 5, of which 2 were waited for; matrix products, arithmetic and copies ran while one was open for 9% of the time, Pallas kernels for 30%

profile of v1, /device:TPU:0, one launch (start us, length us, event | category | flops | bytes accessed | tf_op | source)
XLA Modules:
  0.0 735.1 jit_solution(12895752383147527084)
XLA Ops:
  7.2 0.8 copy.56
  8.0 0.8 slice_bitcast_fusion.6
  8.8 1.3 convert_element_type.40
  12.3 0.9 pad_maximum_fusion
  13.4 1.0 add_bitcast_fusion
  14.4 1.7 slice_add_fusion
  16.4 18.3 %sort.22 = (s32[65536]{0:T(1024)S(1)}, s32[65536]{0:T(1024)S(1)}) sort(s32[65536]{0:T(1024)S(1)} %fusion.9, s32[65536]{0:T(1024)S(1)} %bitcast.62), dimensions={0}, to_apply=%region_0.1 | sort | flops 1048576 | bytes 1048576 | tf_op jit(solution)/shard_map/sort | solution.py:623
  34.9 18.4 %all_to_all.19 = s32[16,1,4096]{2,1,0:T(1,128)} all-to-all(s32[16,1,4096]{2,1,0:T(1,128)S(1)} %bitcast.63), channel_id=1, replica_groups=mesh['rep'=2,'shard'=16] {'shard'}, dimensions={0} | all-to-all | bytes 524288 | tf_op jit(solution)/shard_map/all_to_all | solution.py:629
  53.3 37.4 %owner_gather.1 = bf16[16,1024,128]{2,1,0:T(8,128)(2,1)} custom-call(s32[65536]{0:T(1024)} %bitcast.58, f32[16384,128]{1,0:T(8,128)} %table_ref.1), custom_call_target="tpu_custom_call" | custom-call | tf_op jit(solution)/shard_map/owner_gather/pallas_call | solution.py:69
  90.6 4.6 all-to-all-start.1
  95.3 0.6 reduce_sum.27
  97.0 0.6 slice.85
  98.3 0.7 reshape.113.head_ref
  99.0 0.7 reshape.112.tower_bias_ref
  99.7 1.2 fusion.21
  100.8 8.8 %sort.23 = s32[65536]{0:T(1024)S(1)} sort(s32[65536]{0:T(1024)S(1)} %get-tuple-element.111), dimensions={0}, to_apply=%region_1.2 | sort | flops 1048576 | bytes 524288 | tf_op jit(solution)/shard_map/sort | solution.py:640
  109.9 0.8 pad.13.label_ref
  111.8 0.8 pad.12.live_ref
  112.7 0.8 add_select_fusion.4.q0_ref.q1_ref
  113.5 59.3 %all-to-all-done.1 = bf16[16,1024,128]{2,1,0:T(8,128)(2,1)} async-done(((bf16[16,1024,128]{2,1,0:T(8,128)(2,1)}), bf16[16,1024,128]{2,1,0:T(8,128)(2,1)}, u32[]{:S(2)}, u32[]{:S(2)}) %all-to-all-start.1) | async-done | bytes 4194336 | tf_op jit(solution)/shard_map/all_to_all | solution.py:643
  172.8 60.3 %pool.1.pooled_ref = bf16[8,1024,128]{2,1,0:T(8,128)(2,1)} custom-call(s32[65536]{0:T(1024)} %add_select_fusion.4.q0_ref.q1_ref, s32[65536]{0:T(1024)} %add_select_fusion.4.q0_ref.q1_ref, bf16[16384,128]{1,0:T(8,128)(2,1)} %bitcast.5.reply_ref), custom_call_target="tpu_custom_call" | custom-call | tf_op jit(solution)/shard_map/pool/pallas_call | solution.py:113
  233.1 95.9 %dense.1 = (f32[8,1024,128]{2,1,0:T(8,128)}, bf16[8,1024,512]{2,1,0:T(8,128)(2,1)}, bf16[1024,1024]{1,0:T(8,128)(2,1)}, bf16[1024,128]{1,0:T(8,128)(2,1)}, f32[5,512,64]{2,1,0:T(8,128)}, /*index=5*/f32[16,128]{1,0:T(8,128)}) custom-call(bf16[8,1024,128]{2,1,0:T(8,128)(2,1)} %pool.1.pooled_ref, bf16[9,1024,512]{2,1,0:T(8,128)(2,1)} %all-gather.2.cloned.1.call-done.weight_ref, ...), custom_call_target="tpu_custom_call" | custom-call | tf_op jit(solution)/shard_map/dense/pallas_call | solution.py:449
  329.0 16.3 %weight_grads.1 = (bf16[9,1024,512]{2,1,0:T(8,128)(2,1)}, f32[9,1,512]{2,1,0:T(1,128)}) custom-call(bf16[1024,1024]{1,0:T(8,128)(2,1)} %get-tuple-element.28.x_ref, bf16[8,1024,512]{2,1,0:T(8,128)(2,1)} %get-tuple-element.29.expert_ref, bf16[1024,128]{1,0:T(8,128)(2,1)} %get-tuple-element.30.gate_ref, f32[5,512,64]{2,1,0:T(8,128)} %get-tuple-element.31.tower_ref), custom_call_target="tpu_custom_call" | custom-call | tf_op jit(solution)/shard_map/weight_grads/pallas_call | solution.py:531
  345.3 67.8 %grad_gather.1 = bf16[16,1024,128]{2,1,0:T(8,128)(2,1)} custom-call(s32[65536]{0:T(1024)} %get-tuple-element.110.index_ref, f32[8192,128]{1,0:T(8,128)} %bitcast.57), custom_call_target="tpu_custom_call" | custom-call | tf_op jit(solution)/shard_map/grad_gather/pallas_call | solution.py:159
  413.1 131.3 %all_to_all.20.got_ref = bf16[16,1024,128]{2,1,0:T(8,128)(2,1)} all-to-all(bf16[16,1024,128]{2,1,0:T(8,128)(2,1)} %grad_gather.1), channel_id=1, replica_groups=mesh['rep'=2,'shard'=16] {'shard'}, dimensions={0} | all-to-all | bytes 8388608 | tf_op jit(solution)/shard_map/all_to_all | solution.py:668
  544.5 51.9 %scatter.1 = bf16[16384,128]{1,0:T(8,128)(2,1)} custom-call(s32[65536]{0:T(1024)} %bitcast.59, bf16[16,1024,128]{2,1,0:T(8,128)(2,1)} %all_to_all.20.got_ref), custom_call_target="tpu_custom_call" | custom-call | tf_op jit(solution)/shard_map/scatter/pallas_call | solution.py:209
  596.3 1.6 collective-permute-start
  598.0 0.7 copy.62
  598.9 0.6 slice_reduce_fusion
  599.5 0.7 concatenate.7
  600.2 42.7 %all_gather.7 = f32[32,8,640]{2,1,0:T(8,128)S(1)} all-gather(f32[1,8,640]{2,1,0:T(8,128)S(1)} %all_gather_reshape.3), channel_id=1, replica_groups=mesh['rep'=2,'shard'=16] {'rep','shard'}, dimensions={0}, use_global_device_ids=true | all-gather | bytes 675840 | tf_op jit(solution)/shard_map/all_gather | solution.py:699
  643.6 1.2 pad_maximum_fusion.1
  644.8 0.6 multiply_subtract_fusion.3
  645.5 1.5 collective-permute-start.1
  646.9 43.1 %collective-permute-done = bf16[16384,128]{1,0:T(8,128)(2,1)} collective-permute-done((bf16[16384,128]{1,0:T(8,128)(2,1)}, bf16[16384,128]{1,0:T(8,128)(2,1)}, u32[]{:S(2)}, u32[]{:S(2)}) %collective-permute-start) | collective-permute-done | bytes 4194336 | tf_op jit(solution)/shard_map/ppermute | solution.py:556
  690.1 22.3 %add_subtract_fusion = (f32[16384,128]{1,0:T(8,128)}, f32[16384,128]{1,0:T(8,128)}, f32[16384,128]{1,0:T(8,128)}) fusion(f32[16384,128]{1,0:T(8,128)} %table_ref.1, bf16[16384,128]{1,0:T(8,128)(2,1)} %collective-permute-done, bf16[16384,128]{1,0:T(8,128)(2,1)} %scatter.1, f32[16384,128]{1,0:T(8,128)} %param.26, f32[16384,128]{1,0:T(8,128)} %param.27), kind=kLoop, calls=%fused_computation.2 | loop fusion | flops 35651584 | bytes 58720256 | tf_op jit(solution)/shard_map/sub | solution.py:38
  712.4 1.5 convert_add_fusion.1
  713.9 0.6 fusion.42
  714.5 1.4 multiply_subtract_fusion.2
  715.9 1.4 copy.65
  717.4 1.4 copy.66
  718.8 1.4 copy.67
  720.2 0.6 fusion.41
  720.8 0.6 fusion.40
  721.5 0.6 fusion.39
  722.1 0.6 fusion.38
  722.7 3.5 multiply_subtract_fusion
  726.1 1.7 multiply_subtract_fusion.1
  (67 shorter events, 5.6 us)
Async XLA Ops:
  7.2 225.9 %all-gather.2.cloned.1.call-start = ((), (), s32[]{:S(2)}) async-start(), calls=%async_computation.4 | async-start | bytes 10027008 | tf_op jit(solution)/shard_map/all_gather | solution.py:611
  53.2 42.0 %copy-start.12 = (s32[32]{0:T(128)S(1)}, s32[32]{0:T(128)}, u32[]{:S(2)}) copy-start(s32[32]{0:T(128)} %param.22) | copy-start | bytes 388
  53.3 43.2 %copy-start.3 = (f32[4741]{0:T(1024)S(1)}, f32[4741]{0:T(1024)}, u32[]{:S(2)}) copy-start(f32[4741]{0:T(1024)} %param.37) | copy-start | bytes 56896
  53.3 46.4 %copy-start.4 = (s32[1024,5]{0,1:T(8,128)S(1)}, s32[1024,5]{0,1:T(8,128)}, u32[]{:S(2)}) copy-start(s32[1024,5]{0,1:T(8,128)} %param.23) | copy-start | bytes 61444
  53.3 46.4 %copy-start.5 = (s32[1024,5]{0,1:T(8,128)S(1)}, s32[1024,5]{0,1:T(8,128)}, u32[]{:S(2)}) copy-start(s32[1024,5]{0,1:T(8,128)} %param.24) | copy-start | bytes 61444
  90.6 82.2 %all-to-all-start.1 = ((bf16[16,1024,128]{2,1,0:T(8,128)(2,1)}), bf16[16,1024,128]{2,1,0:T(8,128)(2,1)}, u32[]{:S(2)}, u32[]{:S(2)}) async-start(bf16[16,1024,128]{2,1,0:T(8,128)(2,1)} %owner_gather.1), calls=%async_computation.1 | async-start | bytes 8388608 | tf_op jit(solution)/shard_map/all_to_all | solution.py:643
  95.2 550.3 %reduce-scatter.2.cloned.1.call-start = ((), (), s32[]{:S(2)}) async-start(), calls=%async_computation.5 | async-start | bytes 10027008 | tf_op jit(solution)/shard_map/reduce_scatter | solution.py:673
  413.1 184.9 %copy-start.8 = (f32[64,40]{0,1:T(8,128)S(1)}, f32[64,40]{0,1:T(8,128)}, u32[]{:S(2)}) copy-start(f32[64,40]{0,1:T(8,128)} %param.32) | copy-start | bytes 30724
  413.1 184.9 %copy-start.9 = (f32[64,40]{0,1:T(8,128)S(1)}, f32[64,40]{0,1:T(8,128)}, u32[]{:S(2)}) copy-start(f32[64,40]{0,1:T(8,128)} %param.33) | copy-start | bytes 30724
  413.1 185.6 %copy-start.10 = (f32[9,1,512]{2,1,0:T(1,128)S(1)}, f32[9,1,512]{2,1,0:T(1,128)}, u32[]{:S(2)}) copy-start(f32[9,1,512]{2,1,0:T(1,128)} %get-tuple-element.32) | copy-start | bytes 55300
  413.1 185.6 %copy-start.11 = (f32[16,128]{1,0:T(8,128)S(1)}, f32[16,128]{1,0:T(8,128)}, u32[]{:S(2)}) copy-start(f32[16,128]{1,0:T(8,128)} %get-tuple-element.33) | copy-start | bytes 24580
  413.1 231.7 %copy-start.6 = (f32[4741]{0:T(1024)S(1)}, f32[4741]{0:T(1024)}, u32[]{:S(2)}) copy-start(f32[4741]{0:T(1024)} %param.38) | copy-start | bytes 56896
  413.1 231.7 %copy-start.7 = (f32[4741]{0:T(1024)S(1)}, f32[4741]{0:T(1024)}, u32[]{:S(2)}) copy-start(f32[4741]{0:T(1024)} %param.39) | copy-start | bytes 56896
  596.3 93.8 %collective-permute-start = (bf16[16384,128]{1,0:T(8,128)(2,1)}, bf16[16384,128]{1,0:T(8,128)(2,1)}, u32[]{:S(2)}, u32[]{:S(2)}) collective-permute-start(bf16[16384,128]{1,0:T(8,128)(2,1)} %scatter.1), channel_id=1, source_target_pairs={{0,16},{16,0},{1,17},{17,1},{2,18},{18,2},{3,19},{19,3},{4,20},{20... | collective-permute-start | bytes 12582920 | tf_op jit(solution)/shard_map/ppermute | solution.py:556
  645.5 77.2 %copy-start = (f32[8,64,512]{2,1,0:T(8,128)S(1)}, f32[8,64,512]{2,1,0:T(8,128)}, u32[]{:S(2)}) copy-start(f32[8,64,512]{2,1,0:T(8,128)} %param.28) | copy-start | bytes 3145732
  645.5 77.2 %copy-start.1 = (f32[8,64,512]{2,1,0:T(8,128)S(1)}, f32[8,64,512]{2,1,0:T(8,128)}, u32[]{:S(2)}) copy-start(f32[8,64,512]{2,1,0:T(8,128)} %param.29) | copy-start | bytes 3145732
  645.5 66.9 %collective-permute-start.1 = (bf16[9,64,512]{2,1,0:T(8,128)(2,1)}, bf16[9,64,512]{2,1,0:T(8,128)(2,1)}, u32[]{:S(2)}, u32[]{:S(2)}) collective-permute-start(bf16[9,64,512]{2,1,0:T(8,128)(2,1)} %reduce-scatter.2.cloned.1.call-done), channel_id=1, source_target_pairs={{0,16},{16,0},{1,17},{17,1},{2,18},{18,2},{3,19},{19,3},{4,20},{20... | collective-permute-start | bytes 1769480 | tf_op jit(solution)/shard_map/ppermute | solution.py:556
  712.4 13.7 %copy-start.2 = (f32[5,32,64]{2,1,0:T(8,128)S(1)}, f32[5,32,64]{2,1,0:T(8,128)}, u32[]{:S(2)}) copy-start(f32[5,32,64]{2,1,0:T(8,128)} %param.34) | copy-start | bytes 122884
Sparse Core Ops, SparseCore 0:
  13.3 86.1 all-gather.1
  345.4 166.7 reduce-scatter.1

commit v2 on v1

v2 whole, which is shorter than its diff:
```python
import functools

import jax
import jax.numpy as jnp
from jax import lax
from jax.experimental import pallas as pl
from jax.experimental.pallas import tpu as pltpu
from jax.sharding import PartitionSpec as P

TABLES = 2
WIDTH = 64
ROW_BASE = 1024
EXPERTS = 8
HID = 512
TASKS = 5
TOWER = 64
STEP = 10
LANES = 128
UNROLL = 64
RMW = 8
PARTS = 8
PACKED = 3 * LANES
ANYWHERE = pl.BlockSpec(memory_space=pl.ANY)
VMEM_BYTES = 60 << 20

beta_first = 0.9
beta_second = 0.999
adam_epsilon = 1e-08
weight_decay = 0.01
rate_table = 1.0
rate_expert = 0.06
rate_gate = 0.03
rate_tower = 0.08
rate_small = 0.5


def adamw(weight, grad, first, second, rate):
    first_new = beta_first * first + (1.0 - beta_first) * grad
    second_new = beta_second * second + (1.0 - beta_second) * grad * grad
    first_hat = first_new / (1.0 - beta_first**STEP)
    second_hat = second_new / (1.0 - beta_second**STEP)
    weight_new = weight - rate * (
        first_hat / (jnp.sqrt(second_hat) + adam_epsilon) + weight_decay * weight
    )
    return (weight_new, first_new, second_new)


def left_lanes(rows=1):
    return lax.broadcasted_iota(jnp.int32, (rows, LANES), 1) < WIDTH


def params(**kw):
    return pltpu.CompilerParams(vmem_limit_bytes=VMEM_BYTES, **kw)


def pack(first, second, table):
    left = left_lanes(first.shape[0])
    if table == 0:
        return jnp.where(left, first, pltpu.roll(second, WIDTH, 1))
    return jnp.where(left, pltpu.roll(first, WIDTH, 1), second)


def unpack(value, table):
    turned = pltpu.roll(value, WIDTH, 1)
    return (value, turned) if table == 0 else (turned, value)


def cost(micros):
    return pl.CostEstimate(flops=0, bytes_accessed=int(micros * 1.0e2), transcendentals=0)


def owner_gather_kernel(distinct, table_at, want_ref, table_ref, out_ref, rows_ref):
    def body(step, carry):
        base = step * UNROLL
        for u in range(UNROLL):
            rows_ref[pl.ds(base + u, 1), :] = table_ref[pl.ds(want_ref[2 * (base + u)], 1), :]
        return carry

    lax.fori_loop(0, distinct // UNROLL, body, 0)
    half = distinct // 2
    packed = pack(rows_ref[0:half, :], rows_ref[half:distinct, :], table_at)
    out_ref[0] = packed.astype(jnp.bfloat16)


def owner_gather(wanted, table, shards, distinct, table_at):
    rows = table.shape[0]
    return pl.pallas_call(
        functools.partial(owner_gather_kernel, distinct, table_at),
        name="owner_gather",
        grid=(shards,),
        in_specs=[
            pl.BlockSpec((2 * distinct,), lambda i: (2 * i + table_at,), memory_space=pltpu.SMEM),
            pl.BlockSpec((rows, LANES), lambda i: (0, 0), pipeline_mode=pl.Buffered(1)),
        ],
        out_specs=pl.BlockSpec((1, distinct // 2, LANES), lambda i: (i, 0, 0)),
        out_shape=jax.ShapeDtypeStruct((shards, distinct // 2, LANES), jnp.bfloat16),
        scratch_shapes=[pltpu.VMEM((distinct, LANES), jnp.float32)],
        compiler_params=params(),
        cost_estimate=cost(20),
    )(wanted, table)


def pool_kernel(samples, longest, distinct, table_at, *refs):
    if table_at == 0:
        place_ref, reply_ref, out_ref, rows_ref, sum_ref = refs
    else:
        place_ref, reply_ref, before_ref, out_ref, rows_ref, sum_ref = refs
    shards, half = reply_ref.shape[:2]

    @pl.when(pl.program_id(0) == 0)
    def _():
        def spread(i, carry):
            first, second = unpack(reply_ref[i].astype(jnp.float32), table_at)
            base = pl.multiple_of(i * distinct, 8)
            rows_ref[pl.ds(base, half), :] = first
            rows_ref[pl.ds(base + half, half), :] = second
            return carry

        lax.fori_loop(0, shards, spread, 0)
        rows_ref[shards * distinct :, :] = jnp.zeros((8, LANES), jnp.float32)

    unroll = UNROLL // 4

    def body(step, carry):
        for u in range(unroll):
            s = step * unroll + u
            total = rows_ref[pl.ds(place_ref[s], 1), :]
            for slot in range(1, longest):
                total = total + rows_ref[pl.ds(place_ref[slot * samples + s], 1), :]
            sum_ref[pl.ds(s, 1), :] = total
        return carry

    lax.fori_loop(0, samples // unroll, body, 0)
    result = sum_ref[...]
    if table_at != 0:
        result = jnp.where(left_lanes(samples), before_ref[0].astype(jnp.float32), result)
    out_ref[0] = result.astype(jnp.bfloat16)


def pool(places, replies, before, samples, longest, pairs, table_at):
    shards, half = replies.shape[:2]
    distinct = 2 * half
    block = pl.BlockSpec((1, samples, LANES), lambda i: (i, 0, 0))
    return pl.pallas_call(
        functools.partial(pool_kernel, samples, longest, distinct, table_at),
        name="pool",
        grid=(pairs,),
        in_specs=[
            pl.BlockSpec(
                (longest * samples,), lambda i: (i + table_at * pairs,), memory_space=pltpu.SMEM
            ),
            pl.BlockSpec((shards, half, LANES), lambda i: (0, 0, 0), pipeline_mode=pl.Buffered(1)),
        ]
        + [block] * len(before),
        out_specs=block,
        out_shape=jax.ShapeDtypeStruct((pairs, samples, LANES), jnp.bfloat16),
        scratch_shapes=[
            pltpu.VMEM((shards * distinct + 8, LANES), jnp.float32),
            pltpu.VMEM((samples, LANES), jnp.float32),
        ],
        compiler_params=params(),
        cost_estimate=cost(30),
    )(places, replies, *before)


def grad_gather_kernel(distinct, table_at, index_ref, grad_ref, *refs):
    out_ref, grads_ref, rows_ref = refs[-3:]
    count = grad_ref.shape[0]

    @pl.when(pl.program_id(0) == 0)
    def _():
        grads_ref[0:count, :] = grad_ref[...]
        grads_ref[count : count + 8, :] = jnp.zeros((8, LANES), jnp.float32)

    unroll = UNROLL // 2

    def body(step, carry):
        for u in range(unroll):
            r = step * unroll + u
            first = grads_ref[pl.ds(index_ref[2 * r], 1), :]
            second = grads_ref[pl.ds(index_ref[2 * r + 1], 1), :]
            rows_ref[pl.ds(r, 1), :] = first + second
        return carry

    lax.fori_loop(0, distinct // unroll, body, 0)
    half = distinct // 2
    packed = pack(rows_ref[0:half, :], rows_ref[half:distinct, :], table_at)
    out_ref[0] = packed.astype(jnp.bfloat16)


def grad_gather(index, grads, after, shards, distinct, table_at):
    count = grads.shape[0]
    return pl.pallas_call(
        functools.partial(grad_gather_kernel, distinct, table_at),
        name="grad_gather",
        grid=(shards,),
        in_specs=[
            pl.BlockSpec((2 * distinct,), lambda i: (2 * i + table_at,), memory_space=pltpu.SMEM),
            pl.BlockSpec((count, LANES), lambda i: (0, 0), pipeline_mode=pl.Buffered(1)),
        ]
        + [ANYWHERE] * len(after),
        out_specs=pl.BlockSpec((1, distinct // 2, LANES), lambda i: (i, 0, 0)),
        out_shape=jax.ShapeDtypeStruct((shards, distinct // 2, LANES), jnp.bfloat16),
        scratch_shapes=[
            pltpu.VMEM((count + 8, LANES), jnp.float32),
            pltpu.VMEM((distinct, LANES), jnp.float32),
        ],
        compiler_params=params(),
        cost_estimate=cost(32),
    )(index, grads, *after)


def scatter_kernel(distinct, table_at, outs, want0_ref, want1_ref, got_ref, *refs):
    out_refs, (sum0_ref, sum1_ref, rows_ref) = refs[-3 - outs : -3], refs[-3:]
    half = distinct // 2
    sums = (sum0_ref, sum1_ref)
    wants = (want0_ref, want1_ref)

    @pl.when(pl.program_id(0) == 0)
    def _():
        sum0_ref[...] = jnp.zeros_like(sum0_ref)
        sum1_ref[...] = jnp.zeros_like(sum1_ref)

    for i in range(2):
        first, second = unpack(got_ref[i].astype(jnp.float32), table_at)
        rows_ref[i, 0:half, :] = first
        rows_ref[i, half:distinct, :] = second

    def put(waiting):
        ref, places, values = waiting
        for place, value in zip(places, values):
            ref[pl.ds(place, 1), :] = value

    def body(step, carry):
        waiting = None
        for part in range(PARTS):
            base = (step * PARTS + part) * RMW
            for i in range(2):
                places = [wants[i][2 * (base + u)] for u in range(RMW)]
                values = [
                    sums[i][pl.ds(places[u], 1), :] + rows_ref[i, pl.ds(base + u, 1), :]
                    for u in range(RMW)
                ]
                if waiting is not None:
                    put(waiting)
                waiting = (sums[i], places, values)
        put(waiting)
        return carry

    lax.fori_loop(0, distinct // (RMW * PARTS), body, 0)

    @pl.when(pl.program_id(0) == pl.num_programs(0) - 1)
    def _():
        count = out_refs[0].shape[0]
        chunk = count // 8
        for n, out_ref in enumerate(out_refs):

            def finish(i, carry):
                low = pl.ds(pl.multiple_of(n * count + i * chunk, 16), chunk)
                high = pl.ds(pl.multiple_of((len(out_refs) + n) * count + i * chunk, 16), chunk)
                total = pack(
                    sum0_ref[low, :] + sum1_ref[low, :],
                    sum0_ref[high, :] + sum1_ref[high, :],
                    table_at,
                )
                out_ref[pl.ds(pl.multiple_of(i * chunk, 16), chunk), :] = total.astype(jnp.bfloat16)
                return carry

            lax.fori_loop(0, 8, finish, 0)


def scatter(wanted, arrived, after, rows, table_at, outs):
    shards, half = arrived.shape[:2]
    distinct = 2 * half
    want = lambda j: pl.BlockSpec(
        (2 * distinct,), lambda i: (2 * (2 * i + j) + table_at,), memory_space=pltpu.SMEM
    )
    count = rows // 2 // outs
    return pl.pallas_call(
        functools.partial(scatter_kernel, distinct, table_at, outs),
        name="scatter",
        grid=(shards // 2,),
        in_specs=[
            want(0),
            want(1),
            pl.BlockSpec((2, half, LANES), lambda i: (i, 0, 0)),
        ]
        + [ANYWHERE] * len(after),
        out_specs=[pl.BlockSpec((count, LANES), lambda i: (0, 0))] * outs,
        out_shape=[jax.ShapeDtypeStruct((count, LANES), jnp.bfloat16)] * outs,
        scratch_shapes=[
            pltpu.VMEM((rows, LANES), jnp.float32),
            pltpu.VMEM((rows, LANES), jnp.float32),
            pltpu.VMEM((2, distinct, LANES), jnp.float32),
        ],
        compiler_params=params(),
        cost_estimate=cost(24),
    )(wanted, wanted, arrived, *after)


def table_adam_kernel(*refs):
    parts = refs[:4]
    weight_ref, first_ref, second_ref = refs[4:7]
    weight_out, first_out, second_out, token_ref = refs[-4:]
    later = pl.program_id(0) >= pl.num_programs(0) // 2
    sum0 = parts[0][...].astype(jnp.float32) + parts[1][...].astype(jnp.float32)
    sum1 = parts[2][...].astype(jnp.float32) + parts[3][...].astype(jnp.float32)
    left = left_lanes(sum0.shape[0])
    early_grad = jnp.where(left, sum0, pltpu.roll(sum1, WIDTH, 1))
    late_grad = jnp.where(left, pltpu.roll(sum0, WIDTH, 1), sum1)
    grad = jnp.where(later, late_grad, early_grad)
    weight, first, second = adamw(
        weight_ref[...], grad, first_ref[...], second_ref[...], rate_table
    )
    weight_out[...] = weight
    first_out[...] = first
    second_out[...] = second
    token_ref[...] = jnp.zeros_like(token_ref)


def table_adam(first_parts, second_parts, chunk, weight, first, second, before):
    rows = weight.shape[0]
    count = second_parts[0].shape[0]
    block = min(1024, count)
    steps = count // block
    full_at = lambda i: (chunk * steps + i % steps + i // steps * (rows // 2 // block), 0)
    inside = chunk * count % first_parts[0].shape[0] // block
    early = pl.BlockSpec((block, LANES), lambda i: (inside + i % steps, 0))
    packed = pl.BlockSpec((block, LANES), lambda i: (i % steps, 0))
    full = pl.BlockSpec((block, LANES), full_at)
    return pl.pallas_call(
        table_adam_kernel,
        name="table_adam",
        grid=(2 * steps,),
        in_specs=[early] * 2
        + [packed] * 2
        + [full] * 3
        + [pl.BlockSpec(memory_space=pl.ANY)] * len(before),
        out_specs=[full] * 3 + [pl.BlockSpec((8, LANES), lambda i: (0, 0))],
        out_shape=[jax.ShapeDtypeStruct(weight.shape, jnp.float32)] * 3
        + [jax.ShapeDtypeStruct((8, LANES), jnp.float32)],
        input_output_aliases={7 + i: i for i in range(len(before))},
        compiler_params=params(),
        cost_estimate=cost(7),
    )(*first_parts, *second_parts, weight, first, second, *before)


def group_reduce(value, op):
    lane = lax.broadcasted_iota(jnp.int32, value.shape, 1)
    shift = 1
    while shift < EXPERTS:
        other = jnp.where(
            (lane & shift) != 0,
            pltpu.roll(value, shift, 1),
            pltpu.roll(value, LANES - shift, 1),
        )
        value = op(value, other)
        shift *= 2
    return value


def dot(a, b):
    return jnp.dot(a, b, preferred_element_type=jnp.float32)


def dot_nt(a, b):
    return lax.dot_general(a, b, (((1,), (1,)), ((), ())), preferred_element_type=jnp.float32)


def dot_tn(a, b):
    return lax.dot_general(a, b, (((0,), (0,)), ((), ())), preferred_element_type=jnp.float32)


def split_two(value):
    high = value.astype(jnp.bfloat16)
    low = (value - high.astype(jnp.float32)).astype(jnp.bfloat16)
    return high, low


def dense_kernel(
    shards,
    parts,
    base_ref,
    pooled_ref,
    *refs,
):
    weight_refs, refs = refs[:parts], refs[parts:]
    dense_body(shards, base_ref, pooled_ref, weight_refs, *refs)


def dense_body(
    shards,
    base_ref,
    pooled_ref,
    weight_refs,
    bias_ref,
    tower_bias_ref,
    head_ref,
    head_bias_ref,
    live_ref,
    label_ref,
    scale_ref,
    grad_ref,
    expert_grad_ref,
    x_ref,
    gate_grad_ref,
    tower_grad_ref,
    bias_grad_ref,
    small_ref,
    out_ref,
    slope_ref,
    tower_out_ref,
    spread_ref,
    total_ref,
    tower_ref,
    expand_ref,
    head_expand_ref,
):
    pairs = pooled_ref.shape[0]
    block = pooled_ref.shape[1]
    extra_ref = weight_refs[0].at[weight_refs[0].shape[0] - 1]
    in_first = weight_refs[0].shape[0] - 1
    depth = extra_ref.shape[0] // shards
    half = depth // 2
    step = pl.program_id(0)
    f32, bf16 = jnp.float32, jnp.bfloat16

    @pl.when(step == 0)
    def _():
        for i in range(shards):
            tower_ref[i * half : (i + 1) * half, :] = extra_ref[
                i * depth : i * depth + half, LANES : LANES + PACKED
            ]
        source = lax.broadcasted_iota(jnp.int32, (LANES, PACKED), 0)
        task = lax.broadcasted_iota(jnp.int32, (LANES, PACKED), 1) // TOWER
        head_expand_ref[...] = (source == task).astype(f32).astype(bf16)
        for e in range(EXPERTS):
            expert = (base_ref[0] + e) % EXPERTS
            expand_ref[e] = (source == task * EXPERTS + expert).astype(f32).astype(bf16)
        small_ref[...] = jnp.zeros_like(small_ref)
        tower_grad_ref[...] = jnp.zeros_like(tower_grad_ref)
        bias_grad_ref[...] = jnp.zeros_like(bias_grad_ref)

    left = left_lanes(block)
    for m in range(pairs // 2):
        even = pooled_ref[2 * m].astype(f32)
        odd = pooled_ref[2 * m + 1].astype(f32)
        low = jnp.where(left, even, pltpu.roll(odd, WIDTH, 1)).astype(bf16)
        high = jnp.where(left, pltpu.roll(even, WIDTH, 1), odd).astype(bf16)
        x_ref[:, m * LANES : (m + 1) * LANES] = low
        high_at = (m + pairs // 2) * LANES
        x_ref[:, high_at : high_at + LANES] = high

    def weight(e):
        return weight_refs[0][e] if e < in_first else weight_refs[1][e - in_first]

    logits = dot(x_ref[...], extra_ref[:, 0:LANES])
    powers = jnp.exp(logits - group_reduce(logits, jnp.maximum))
    gates = powers / group_reduce(powers, jnp.add)
    gates_high, gates_low = split_two(gates)

    total_ref[...] = jnp.zeros_like(total_ref)

    def expert(e, carry):
        pre = dot(x_ref[...], weight(e)) + bias_ref[e]
        sigma = jax.nn.sigmoid(pre)
        out = pre * sigma
        slope_ref[e] = sigma + out * (1.0 - sigma)
        out_low = out.astype(bf16)
        out_ref[e] = out_low
        product = dot(out_low, tower_ref[...])
        spread = dot(gates_high, expand_ref[e]) + dot(gates_low, expand_ref[e])
        tower_out_ref[e] = product
        spread_ref[e] = spread
        total_ref[...] += spread * product
        return carry

    loop(expert)

    pre = total_ref[...] + tower_bias_ref[...]
    sigma = jax.nn.sigmoid(pre)
    tower_out = pre * sigma
    slope = sigma + tower_out * (1.0 - sigma)
    high, low = split_two(tower_out * head_ref[...])
    logit = dot_nt(high, head_expand_ref[...]) + dot_nt(low, head_expand_ref[...])
    logit = logit + head_bias_ref[...]
    live = live_ref[...]
    label = label_ref[...]
    softplus = jnp.maximum(logit, 0.0) + jnp.log1p(jnp.exp(-jnp.abs(logit)))
    losses = live * (softplus - label * logit)
    logit_grad = live * (jax.nn.sigmoid(logit) - label) * scale_ref[0]
    high, low = split_two(logit_grad)
    signal = dot(high, head_expand_ref[...]) + dot(low, head_expand_ref[...])
    pre_grad = (signal * head_ref[...] * slope).astype(bf16).astype(f32)
    small_ref[0:1, :] += jnp.sum(signal * tower_out, axis=0, keepdims=True)
    small_ref[1:2, :] += jnp.sum(pre_grad, axis=0, keepdims=True)
    small_ref[2:3, 0:LANES] += jnp.sum(logit_grad, axis=0, keepdims=True)
    small_ref[3:4, 0:LANES] += jnp.sum(losses, axis=0, keepdims=True)

    total_ref[...] = pre_grad

    def back(e, carry):
        gate_prob, pooled_grad = carry
        pre_grad = total_ref[...]
        weighed = (spread_ref[e] * pre_grad).astype(bf16)
        tower_grad_ref[...] += dot_tn(weighed, out_ref[e])
        expert_grad = (dot_nt(weighed, tower_ref[...]) * slope_ref[e]).astype(bf16)
        expert_grad_ref[e] = expert_grad
        bias_grad_ref[e] += jnp.sum(expert_grad.astype(f32), axis=0, keepdims=True)
        high, low = split_two(tower_out_ref[e] * pre_grad)
        gate_prob = gate_prob + dot_nt(high, expand_ref[e]) + dot_nt(low, expand_ref[e])
        pooled_grad = pooled_grad + dot_nt(expert_grad, weight(e))
        return gate_prob, pooled_grad

    gate_prob, pooled_grad = loop(
        back, (jnp.zeros((block, LANES), f32), jnp.zeros((block, pairs * LANES), f32))
    )
    weighed = gates * gate_prob
    gate_grad = (weighed - gates * group_reduce(weighed, jnp.add)).astype(bf16)
    gate_grad_ref[...] = gate_grad
    pooled_grad = pooled_grad + dot_nt(gate_grad, extra_ref[:, 0:LANES])
    for m in range(pairs // 2):
        low = pooled_grad[:, m * LANES : (m + 1) * LANES]
        high_at = (m + pairs // 2) * LANES
        high = pooled_grad[:, high_at : high_at + LANES]
        grad_ref[2 * m] = jnp.where(left, low, pltpu.roll(high, WIDTH, 1))
        grad_ref[2 * m + 1] = jnp.where(left, pltpu.roll(low, WIDTH, 1), high)


def loop(body, carry=0):
    for e in range(EXPERTS):
        carry = body(e, carry)
    return carry


def dense(base, pooled, weights, bias, tower_bias, head, head_bias, live, label, scale, shards):
    pairs, samples = pooled.shape[:2]
    inner = weights[0].shape[1]
    slabs = [weights[0].shape[0], EXPERTS + 1 - weights[0].shape[0]][: len(weights)]
    block = 256
    whole = lambda *shape: pl.BlockSpec(
        shape, lambda i: (0,) * len(shape), pipeline_mode=pl.Buffered(1)
    )
    kept = lambda *shape: pl.BlockSpec(shape, lambda i: (0,) * len(shape))
    f32, bf16 = jnp.float32, jnp.bfloat16
    return pl.pallas_call(
        functools.partial(dense_kernel, shards, len(weights)),
        name="dense",
        grid=(samples // block,),
        in_specs=[
            pl.BlockSpec(memory_space=pltpu.SMEM),
            pl.BlockSpec((pairs, block, LANES), lambda i: (0, i, 0)),
        ]
        + [whole(n, inner, HID) for n in slabs]
        + [
            whole(EXPERTS, 1, HID),
            whole(1, PACKED),
            whole(1, PACKED),
            whole(1, LANES),
            pl.BlockSpec((block, LANES), lambda i: (i, 0)),
            pl.BlockSpec((block, LANES), lambda i: (i, 0)),
            pl.BlockSpec(memory_space=pltpu.SMEM),
        ],
        out_specs=[
            pl.BlockSpec((pairs, block, LANES), lambda i: (0, i, 0)),
            pl.BlockSpec((EXPERTS, block, HID), lambda i: (0, i, 0)),
            pl.BlockSpec((block, inner), lambda i: (i, 0)),
            pl.BlockSpec((block, LANES), lambda i: (i, 0)),
            kept(PACKED, HID),
            kept(EXPERTS, 1, HID),
            kept(8, PACKED),
        ],
        out_shape=[
            jax.ShapeDtypeStruct((pairs, samples, LANES), f32),
            jax.ShapeDtypeStruct((EXPERTS, samples, HID), bf16),
            jax.ShapeDtypeStruct((samples, inner), bf16),
            jax.ShapeDtypeStruct((samples, LANES), bf16),
            jax.ShapeDtypeStruct((PACKED, HID), f32),
            jax.ShapeDtypeStruct((EXPERTS, 1, HID), f32),
            jax.ShapeDtypeStruct((8, PACKED), f32),
        ],
        scratch_shapes=[
            pltpu.VMEM((EXPERTS, block, HID), bf16),
            pltpu.VMEM((EXPERTS, block, HID), f32),
            pltpu.VMEM((EXPERTS, block, PACKED), f32),
            pltpu.VMEM((EXPERTS, block, PACKED), f32),
            pltpu.VMEM((block, PACKED), f32),
            pltpu.VMEM((HID, PACKED), bf16),
            pltpu.VMEM((EXPERTS, LANES, PACKED), bf16),
            pltpu.VMEM((LANES, PACKED), bf16),
        ],
        compiler_params=params(),
        cost_estimate=cost(60),
    )(base, pooled, *weights, bias, tower_bias, head, head_bias, live, label, scale)


def weight_grad_kernel(
    shards, which_ref, x_ref, expert_ref, gate_ref, tower_ref, out_ref, extra_ref, turned_ref
):
    step = pl.program_id(0)
    last = pl.num_programs(0) - 1
    inner = x_ref.shape[1]
    depth = inner // shards
    half = depth // 2

    @pl.when(step == 0)
    def _():
        turned_ref[...] = x_ref[...].T

    @pl.when(step < last)
    def _():
        out_ref[0] = dot(turned_ref[...], expert_ref[0]).astype(jnp.bfloat16)

    @pl.when(step == last)
    def _():
        gate = dot(turned_ref[...], gate_ref[...])
        extra_ref[0, :, 0:LANES] = gate.astype(jnp.bfloat16)
        turned = tower_ref[...].T
        none = jnp.zeros((depth - half, PACKED), jnp.float32)
        runs = []
        for i in range(shards):
            runs += [turned[i * half : (i + 1) * half, :], none]
        extra_ref[0, :, LANES:] = jnp.concatenate(runs, axis=0).astype(jnp.bfloat16)


def weight_grads(which, x, expert_grad, gate_grad, tower_grad, shards):
    samples, inner = x.shape
    count = which.shape[0]
    whole = lambda *shape: pl.BlockSpec(
        shape, lambda i, w: (0,) * len(shape), pipeline_mode=pl.Buffered(1)
    )
    upto = lambda i: jnp.minimum(i, count - 1)
    return pl.pallas_call(
        functools.partial(weight_grad_kernel, shards),
        name="weight_grads",
        grid_spec=pltpu.PrefetchScalarGridSpec(
            num_scalar_prefetch=1,
            grid=(count + 1,),
            in_specs=[
                whole(samples, inner),
                pl.BlockSpec((1, samples, HID), lambda i, w: (w[upto(i)], 0, 0)),
                whole(samples, LANES),
                whole(PACKED, HID),
            ],
            out_specs=[
                pl.BlockSpec((1, inner, HID), lambda i, w: (upto(i), 0, 0)),
                pl.BlockSpec((1, inner, HID), lambda i, w: (0, 0, 0)),
            ],
            scratch_shapes=[pltpu.VMEM((inner, samples), jnp.bfloat16)],
        ),
        out_shape=[
            jax.ShapeDtypeStruct((count, inner, HID), jnp.bfloat16),
            jax.ShapeDtypeStruct((1, inner, HID), jnp.bfloat16),
        ],
        compiler_params=params(),
        cost_estimate=cost(18),
    )(which, x, expert_grad, gate_grad, tower_grad)


def order(value, *after):
    return pl.pallas_call(
        lambda *refs: None,
        name="order",
        in_specs=[ANYWHERE] * (1 + len(after)),
        out_specs=ANYWHERE,
        out_shape=jax.ShapeDtypeStruct(value.shape, value.dtype),
        input_output_aliases={0: 0},
    )(value, *after)


def dense_adam_kernel(part, rep_ref, here_ref, there_ref, more_ref, other_ref, *refs):
    expert, gate, tower = refs[0:3], refs[3:6], refs[6:9]
    expert_out, gate_out, tower_out = refs[9:12], refs[12:15], refs[15:18]
    step = pl.program_id(0)
    depth = more_ref.shape[1]
    half = depth // 2

    def put(outs, at, values):
        for out_ref, value in zip(outs, values):
            out_ref[at] = value

    grad = there_ref[0].astype(jnp.float32)
    if part < EXPERTS:
        mine = rep_ref[0] == step // part
        grad = jnp.where(mine, here_ref[0].astype(jnp.float32), grad)
    put(expert_out, 0, adamw(expert[0][0], grad, expert[1][0], expert[2][0], rate_expert))

    @pl.when(step == 0)
    def _():
        grad = more_ref[0].astype(jnp.float32) + other_ref[0].astype(jnp.float32)
        gate_grad = grad[:, 0:LANES].T[0 : TASKS * EXPERTS, :]
        put(gate_out, ..., adamw(gate[0][...], gate_grad, gate[1][...], gate[2][...], rate_gate))
        for k in range(TASKS):
            tower_grad = grad[0:half, LANES + k * TOWER : LANES + (k + 1) * TOWER]
            put(tower_out, k, adamw(tower[0][k], tower_grad, tower[1][k], tower[2][k], rate_tower))


def dense_adam(rep, here, there, extra, expert, gate, tower):
    part = here.shape[0]
    count, depth = expert[0].shape[:2]
    slab = lambda at: pl.BlockSpec((1, depth, HID), lambda i: (at(i), 0, 0))
    whole = lambda value: pl.BlockSpec(value.shape, lambda i: (0,) * value.ndim)
    arrays = [*expert, *gate, *tower]
    specs = [slab(lambda i: i)] * 3 + [whole(value) for value in arrays[3:]]
    outs = pl.pallas_call(
        functools.partial(dense_adam_kernel, part),
        name="dense_adam",
        grid=(count,),
        in_specs=[
            pl.BlockSpec(memory_space=pltpu.SMEM),
            slab(lambda i: i % part),
            slab(lambda i: i % part),
            slab(lambda i: extra[0].shape[0] - 1),
            slab(lambda i: extra[1].shape[0] - 1),
        ]
        + specs,
        out_specs=specs,
        out_shape=[jax.ShapeDtypeStruct(value.shape, jnp.float32) for value in arrays],
        compiler_params=params(),
    )(rep, here, there, *extra, *arrays)
    return outs[0:3], outs[3:6], outs[6:9]


def swap_rep(value):
    return lax.ppermute(value, "rep", [(0, 1), (1, 0)])


def sum_everywhere(value):
    for axis in ("shard", "rep"):
        size = lax.axis_size(axis)
        if size & (size - 1):
            value = lax.psum(value, axis)
            continue
        shift = 1
        while shift < size:
            value = value + lax.ppermute(value, axis, [(i, i ^ shift) for i in range(size)])
            shift *= 2
    return value


def pack_extra(gate, tower):
    depth = gate.shape[0]
    half = depth // 2
    side = jnp.transpose(tower, (1, 0, 2)).reshape(half, TASKS * TOWER)
    slab = jnp.pad(gate, ((0, 0), (0, HID - gate.shape[1])))
    return slab + jnp.pad(side, ((0, depth - half), (LANES, HID - LANES - TASKS * TOWER)))


def on_device(
    row_ids,
    bag_lengths,
    sample_counts,
    label_mask,
    labels,
    tables,
    table_m,
    table_v,
    expert_w,
    expert_m,
    expert_v,
    gate_w,
    gate_m,
    gate_v,
    tower_weight_matrix,
    tower_m,
    tower_v,
    small_params,
    small_m,
    small_v,
):
    shards = lax.axis_size("shard")
    reps = lax.axis_size("rep")
    rep = lax.axis_index("rep")
    device = rep * shards + lax.axis_index("shard")
    samples, bags, longest = row_ids.shape[:3]
    rows_dev = tables.shape[0]
    depth = gate_w.shape[0]
    half = depth // 2
    slots = samples * bags * longest
    capacity = slots // shards
    distinct = capacity // 4
    pairs = bags // TABLES
    int32 = jnp.int32
    both = range(TABLES)

    extra = pack_extra(gate_w, tower_weight_matrix)[None]
    if reps == 2:
        part = EXPERTS // 2
        base = rep * part
        line = jnp.arange(part, dtype=int32)
        chosen = jnp.where(rep == 0, expert_w[:part], expert_w[part:])
    else:
        base = jnp.zeros_like(rep)
        chosen = expert_w
    own = jnp.concatenate([chosen, extra], axis=0).astype(jnp.bfloat16)
    weights = [lax.all_gather(own, "shard", axis=1, tiled=True)]
    if reps == 2:
        weights += [swap_rep(weights[0][:part])]

    def by_slot(value):
        if reps != 2:
            return value
        turned = jnp.concatenate([value[part:], value[:part]], axis=0)
        return jnp.where(rep == 0, value, turned)

    ids = jnp.transpose(row_ids, (1, 2, 3, 0))
    row = ids[:, :, 0, :] * ROW_BASE + ids[:, :, 1, :]
    table_of = lax.broadcasted_iota(int32, row.shape, 0) // pairs
    key = (row // rows_dev * TABLES + table_of) * rows_dev + row % rows_dev
    place = lax.broadcasted_iota(int32, row.shape, 1)
    unused = (place >= jnp.transpose(bag_lengths)[:, None, :]).astype(int32)
    number = (
        lax.broadcasted_iota(int32, row.shape, 0) * longest + place
    ) * samples + lax.broadcasted_iota(int32, row.shape, 2)
    payload = number + unused * slots
    key, payload = lax.sort(
        (key.reshape(slots), payload.reshape(slots)), num_keys=1, is_stable=False
    )
    position = jnp.arange(slots, dtype=int32)
    skipped = payload >= slots
    number = jnp.where(skipped, payload - slots, payload)
    wanted = lax.all_to_all(
        (key % rows_dev).reshape(shards, capacity), "shard", 0, 0, tiled=True
    ).reshape(slots)
    bag = number // (longest * samples)
    grad_place = jnp.where(skipped, pairs * samples, bag % pairs * samples + number % samples)
    reply_place = jnp.where(
        skipped,
        shards * distinct,
        position // capacity * distinct + position % (2 * distinct) // 2,
    )
    span = 2 * shards * distinct
    places = lax.sort(number * span + reply_place, is_stable=False) % span

    def exchange(value):
        return lax.all_to_all(value, "shard", 0, 0, tiled=True)

    found = [owner_gather(wanted, tables, shards, distinct, t) for t in both]
    found[1], places = lax.optimization_barrier((found[1], places))
    replies = [exchange(value) for value in found]
    pooled = []
    for t in both:
        pooled = [pool(places, replies[t], pooled, samples, longest, pairs, t)]

    first_end = EXPERTS * HID
    second_end = first_end + TASKS * TOWER
    third_end = second_end + TASKS * TOWER
    fill = PACKED - TASKS * TOWER
    sample_total = jnp.sum(sample_counts).astype(jnp.float32)
    live_count = jnp.take(sample_counts, device)
    live = (jnp.arange(samples, dtype=int32) < live_count).astype(jnp.float32)[:, None]
    live = jnp.pad(live * label_mask.astype(jnp.float32), ((0, 0), (0, LANES - TASKS)))
    label = jnp.pad(labels.astype(jnp.float32), ((0, 0), (0, LANES - TASKS)))
    pooled_grad, expert_grad, x, gate_grad, tower_grad, bias_grad, sums = dense(
        base.astype(int32).reshape(1),
        pooled[0],
        weights,
        by_slot(small_params[:first_end].reshape(EXPERTS, 1, HID)),
        jnp.pad(small_params[first_end:second_end], (0, fill)).reshape(1, PACKED),
        jnp.pad(small_params[second_end:third_end], (0, fill)).reshape(1, PACKED),
        jnp.pad(small_params[third_end:], (0, LANES - TASKS)).reshape(1, LANES),
        live,
        label,
        (1.0 / sample_total).reshape(1),
        shards,
    )

    every = jnp.arange(EXPERTS, dtype=int32)
    kept, extra_grad = weight_grads(
        (every - base.astype(int32)) % EXPERTS, x, expert_grad, gate_grad, tower_grad, shards
    )
    if reps == 2:
        kept = lax.psum_scatter(kept, "rep", scatter_dimension=0, tiled=True)

    def owned_sum(value):
        return lax.psum_scatter(value, "shard", scatter_dimension=1, tiled=True)

    small_grad = jnp.concatenate(
        [
            by_slot(bias_grad).reshape(-1),
            sums[1, : TASKS * TOWER],
            sums[0, : TASKS * TOWER],
            sums[2, :TASKS],
            jnp.sum(sums[3, :TASKS]).reshape(1),
        ]
    )
    small_size = small_params.shape[0]
    padded = -(-(small_size + 1) // 1024) * 1024
    small_grad = jnp.pad(small_grad, (0, padded - small_size - 1))
    small_grad = small_grad.reshape(padded // LANES, LANES)
    pooled_grad = pooled_grad.reshape(pairs * samples, LANES)
    sent = []
    for t in both:
        sent.append(grad_gather(grad_place, pooled_grad, sent[:], shards, distinct, t))
    arrived = [exchange(value) for value in sent]
    chunks = (2, 2)
    table_parts = []
    after = [sent[1]]
    for t in both:
        mine = scatter(wanted, arrived[t], after, rows_dev, t, chunks[t])
        if reps == 2:
            table_parts.append([])
            for n, value in enumerate(mine):
                if t == 1:
                    value = order(value, (table_parts[0] + table_parts[1])[-1][1])
                table_parts[t].append((value, swap_rep(value)))
            after = [table_parts[0][0][1]]
        else:
            table_parts.append(
                [(lax.psum(v.astype(jnp.float32), "rep"), jnp.zeros_like(v)) for v in mine]
            )

    table_state = []
    tokens = []
    for chunk, second_parts in enumerate(table_parts[1]):
        first_parts = table_parts[0][chunk * chunks[0] // chunks[1]]
        *table_state, token = table_adam(
            first_parts, second_parts, chunk, tables, table_m, table_v, table_state
        )
        tokens.append(token)
    table_new, table_m_new, table_v_new = table_state

    kept = jnp.concatenate([kept, extra_grad], axis=0)
    if reps == 2:
        kept = order(kept, arrived[1], table_parts[0][0][1])
    summed = owned_sum(kept)
    expert = (expert_w, expert_m, expert_v)
    gate = [jnp.transpose(value) for value in (gate_w, gate_m, gate_v)]
    tower = (tower_weight_matrix, tower_m, tower_v)
    if reps == 2:
        summed = order(summed, tokens[-1])
        small_grad = order(small_grad, summed)
        there = swap_rep(summed)
        here = summed[:part]
        extra = (summed, there)
    else:
        here = lax.psum(summed.astype(jnp.float32), "rep")
        there = here
        extra = (here, jnp.zeros_like(here))
        here = here[:EXPERTS]
    expert_new, gate_new, tower_new = dense_adam(
        rep.astype(int32).reshape(1), here, there, extra, expert, gate, tower
    )
    expert_new, expert_m_new, expert_v_new = expert_new
    gate_new, gate_m_new, gate_v_new = [jnp.transpose(value) for value in gate_new]
    tower_new, tower_m_new, tower_v_new = tower_new
    small_sum = sum_everywhere(small_grad).reshape(padded)
    small_new, small_m_new, small_v_new = adamw(
        small_params, small_sum[:small_size], small_m, small_v, rate_small
    )
    loss_parts = jnp.stack([small_sum[small_size], sample_total])
    return (
        loss_parts,
        table_new,
        table_m_new,
        table_v_new,
        expert_new,
        expert_m_new,
        expert_v_new,
        gate_new,
        gate_m_new,
        gate_v_new,
        tower_new,
        tower_m_new,
        tower_v_new,
        small_new,
        small_m_new,
        small_v_new,
    )


def solution(mesh):
    by_sample = ("rep", "shard")
    ins = (
        [P(by_sample, None, None, None), P(by_sample, None), P()]
        + [P(by_sample, None)] * 2
        + [P("shard", None)] * 3
        + [P(None, "shard", None)] * 3
        + [P("shard", None)] * 3
        + [P(None, "shard", None)] * 3
        + [P()] * 3
    )
    outs = (
        [P()]
        + [P("shard", None)] * 3
        + [P(None, "shard", None)] * 3
        + [P("shard", None)] * 3
        + [P(None, "shard", None)] * 3
        + [P()] * 3
    )
    return jax.shard_map(
        on_device, mesh=mesh, in_specs=tuple(ins), out_specs=tuple(outs), check_vma=False
    )
```

time: 746 us -> 571 us (0.77)
  blocking collectives: 192 us -> 21.1 us
  starting transfers between devices: 7.7 us -> 56.8 us
  waiting for transfers between devices: 102 us -> 71 us
  other arithmetic: 68.2 us -> 45.4 us
    all_to_all x1 -> x0, blocking collectives: 131 us -> none  [on_device(): arrived = lax.all_to_all(sent, 'shard', 0, 0, tiled=True)]
    all_gather x1 -> x0, blocking collectives: 42.7 us -> none  [on_device(): lax.all_gather(small_grad.reshape(8, padded // 8), ('rep', 'shard'))]
    all_to_all x1 -> x4, waiting for transfers between devices: 59.3 us -> 23.7 us  [exchange(): return lax.all_to_all(value, 'shard', 0, 0, tiled=True)]
    all_to_all x1 -> x4, starting transfers between devices: 4.55 us -> 39.6 us  [exchange(): return lax.all_to_all(value, 'shard', 0, 0, tiled=True)]
    sub x5 -> x1, other arithmetic: 29.5 us -> 0.63 us  [adamw(): weight - rate * (first_hat / (jnp.sqrt(second_hat) + adam_epsilon) + weig...]
    ppermute x2 -> x11, starting transfers between devices: 3.07 us -> 16.8 us  [the longest x5 8.83 us: sum_everywhere(): lax.ppermute(value, axis, [(i, i ^ shift) for i in range(size)])]
    pallas_call x5 -> x17, Pallas kernels: 313 us -> 309 us  [the longest x2 67.9 us: grad_gather(): pl.pallas_call(functools.partial(grad_gather_kernel, distinct, table_at),...]
    ppermute x2 -> x11, waiting for transfers between devices: 43.1 us -> 47.1 us  [the longest x6 37.7 us: swap_rep(): return lax.ppermute(value, 'rep', [(0, 1), (1, 0)])]
  transfers between devices with their start and end apart: 5 -> 18, of which waited for: 2 -> 13; matrix products, arithmetic and copies ran while one was open for 9% -> 10% of each run, Pallas kernels for 30% -> 44%
where the time goes in v2:
time: 571 us; the launch traced here: 561 us
  Pallas kernels  326 us (57%)
  waiting for transfers between devices  71 us (12%)
  starting transfers between devices  56.8 us (10%)
  other arithmetic  45.4 us (8%)
  local copies, waits for them, and re-layouts  25 us (4%)
  blocking collectives  21.1 us (4%)
  between operations  15.9 us (3%)
    pallas_call x2, Pallas kernels, grad_gather(): pl.pallas_call(functools.partial(grad_gather_kernel, distinct, table_at),...  67.9 us
    pallas_call x2, Pallas kernels, pool(): pl.pallas_call(functools.partial(pool_kernel, samples, longest, distinct,...  66.8 us
    pallas_call x1, Pallas kernels, dense(): pl.pallas_call(functools.partial(dense_kernel, shards, len(weights)), nam...  53.1 us
    pallas_call x2, Pallas kernels, scatter(): pl.pallas_call(functools.partial(scatter_kernel, distinct, table_at, outs...  42.9 us
    pallas_call x2, Pallas kernels, owner_gather(): pl.pallas_call(functools.partial(owner_gather_kernel, distinct, table_at)...  41.1 us
    all_to_all x4, starting transfers between devices, exchange(): return lax.all_to_all(value, 'shard', 0, 0, tiled=True)  39.6 us
    ppermute x6, waiting for transfers between devices, swap_rep(): return lax.ppermute(value, 'rep', [(0, 1), (1, 0)])  37.7 us
    pallas_call x2, Pallas kernels, table_adam(): pl.pallas_call(table_adam_kernel, name='table_adam', grid=(2 * steps,), i...  29.7 us
  transfers between devices with their start and end apart: 18, of which 13 were waited for; matrix products, arithmetic and copies ran while one was open for 10% of the time, Pallas kernels for 44%

profile of v2, /device:TPU:0, one launch (start us, length us, event | category | flops | bytes accessed | tf_op | source)
XLA Modules:
  0.0 561.1 jit_solution(7337633170756243977)
XLA Ops:
  12.3 1.7 slice_add_fusion
  14.3 18.2 %sort.22 = (s32[65536]{0:T(1024)S(1)}, s32[65536]{0:T(1024)S(1)}) sort(s32[65536]{0:T(1024)S(1)} %fusion.7, s32[65536]{0:T(1024)S(1)} %bitcast.50), dimensions={0}, to_apply=%region_0.1 | sort | flops 1048576 | bytes 1048576 | tf_op jit(solution)/shard_map/sort | solution.py:816
  32.6 21.1 %all_to_all.29 = s32[16,1,4096]{2,1,0:T(1,128)} all-to-all(s32[16,1,4096]{2,1,0:T(1,128)S(1)} %bitcast.51), channel_id=1, replica_groups=mesh['rep'=2,'shard'=16] {'shard'}, dimensions={0} | all-to-all | bytes 524288 | tf_op jit(solution)/shard_map/all_to_all | solution.py:822
  53.7 20.6 %owner_gather.3 = bf16[16,512,128]{2,1,0:T(8,128)(2,1)} custom-call(s32[65536]{0:T(1024)} %bitcast.42, f32[16384,128]{1,0:T(8,128)} %refs_4_.3), custom_call_target="tpu_custom_call" | custom-call | bytes 2000 | tf_op jit(solution)/shard_map/owner_gather/pallas_call | solution.py:87
  74.3 6.2 %all-to-all-start.2 = ((bf16[16,512,128]{2,1,0:T(8,128)(2,1)}), bf16[16,512,128]{2,1,0:T(8,128)(2,1)S(1)}, u32[]{:S(2)}, u32[]{:S(2)}) async-start(bf16[16,512,128]{2,1,0:T(8,128)(2,1)} %owner_gather.3), calls=%async_computation.2 | async-start | bytes 4194304 | tf_op jit(solution)/shard_map/all_to_all | solution.py:836
  81.6 8.8 %sort.23 = s32[65536]{0:T(1024)S(1)} sort(s32[65536]{0:T(1024)S(1)} %get-tuple-element.99), dimensions={0}, to_apply=%region_1.2 | sort | flops 1048576 | bytes 524288 | tf_op jit(solution)/shard_map/sort | solution.py:833
  90.5 4.5 slice.95
  94.9 1.5 collective-permute-start
  97.2 20.6 %owner_gather.2 = bf16[16,512,128]{2,1,0:T(8,128)(2,1)} custom-call(s32[65536]{0:T(1024)} %bitcast.43, f32[16384,128]{1,0:T(8,128)} %refs_4_.3), custom_call_target="tpu_custom_call" | custom-call | bytes 2000 | tf_op jit(solution)/shard_map/owner_gather/pallas_call | solution.py:87
  117.8 3.8 all-to-all-done.2.refs_1_
  121.6 1.3 copy-done.3
  122.9 11.2 %all-to-all-start.1 = ((bf16[16,512,128]{2,1,0:T(8,128)(2,1)}), bf16[16,512,128]{2,1,0:T(8,128)(2,1)S(1)}, u32[]{:S(2)}, u32[]{:S(2)}) async-start(bf16[16,512,128]{2,1,0:T(8,128)(2,1)} %owner_gather.2), calls=%async_computation.1 | async-start | bytes 4194304 | tf_op jit(solution)/shard_map/all_to_all | solution.py:836
  142.2 33.2 %pool.2.refs_2_ = bf16[8,1024,128]{2,1,0:T(8,128)(2,1)} custom-call(s32[65536]{0:T(1024)} %add_select_fusion.3.refs_0_, bf16[16,512,128]{2,1,0:T(8,128)(2,1)} %copy-done.3), custom_call_target="tpu_custom_call" | custom-call | bytes 3000 | tf_op jit(solution)/shard_map/pool/pallas_call | solution.py:144
  175.5 1.3 copy-done.2
  176.8 33.6 %pool.3.pooled_ref = bf16[8,1024,128]{2,1,0:T(8,128)(2,1)} custom-call(s32[65536]{0:T(1024)} %add_select_fusion.3.refs_0_, bf16[16,512,128]{2,1,0:T(8,128)(2,1)} %copy-done.2, bf16[8,1024,128]{2,1,0:T(8,128)(2,1)} %pool.2.refs_2_), custom_call_target="tpu_custom_call" | custom-call | bytes 3000 | tf_op jit(solution)/shard_map/pool/pallas_call | solution.py:144
  210.4 53.1 %dense.1 = (f32[8,1024,128]{2,1,0:T(8,128)}, bf16[8,1024,512]{2,1,0:T(8,128)(2,1)}, bf16[1024,1024]{1,0:T(8,128)(2,1)}, bf16[1024,128]{1,0:T(8,128)(2,1)}, f32[3...) custom-call(s32[1]{0:T(128)} %bitcast.base_ref, bf16[8,1024,128]{2,1,0:T(8,128)(2,1)} %pool.3.pooled_ref, ...), custom_call_target="tpu_custom_call" | custom-call | bytes 6000 | tf_op jit(solution)/shard_map/dense/pallas_call | solution.py:546
  263.4 17.1 %weight_grads.1 = (bf16[8,1024,512]{2,1,0:T(8,128)(2,1)}, bf16[1,1024,512]{2,1,0:T(8,128)(2,1)}) custom-call(s32[8]{0:T(128)} %and_select_fusion.which_ref, bf16[1024,1024]{1,0:T(8,128)(2,1)} %get-tuple-element.55.x_ref, bf16[8,1024,512]{2,1,0:T(8,128)(2,1)} %get-tuple-element.56.expert_ref, bf16[1024,128]{1,0:T(8,128)(2,1)} %get-tuple-element.57.gate_ref, ...), custom_call_target="tpu_custom_call" | custom-call | bytes 1800 | tf_op jit(solution)/shard_map/weight_grads/pallas_call | solution.py:633
  280.6 33.9 %grad_gather.2.refs_0_ = bf16[16,512,128]{2,1,0:T(8,128)(2,1)} custom-call(s32[65536]{0:T(1024)} %get-tuple-element.98.index_ref, f32[8192,128]{1,0:T(8,128)} %bitcast.40), custom_call_target="tpu_custom_call" | custom-call | bytes 3200 | tf_op jit(solution)/shard_map/grad_gather/pallas_call | solution.py:193
  314.5 11.0 %all-to-all-start.4 = ((bf16[16,512,128]{2,1,0:T(8,128)(2,1)}), bf16[16,512,128]{2,1,0:T(8,128)(2,1)S(1)}, u32[]{:S(2)}, u32[]{:S(2)}) async-start(bf16[16,512,128]{2,1,0:T(8,128)(2,1)} %grad_gather.2.refs_0_), calls=%async_computation.5 | async-start | bytes 4194304 | tf_op jit(solution)/shard_map/all_to_all | solution.py:836
  325.5 34.0 %grad_gather.3.refs_0_ = bf16[16,512,128]{2,1,0:T(8,128)(2,1)} custom-call(s32[65536]{0:T(1024)} %get-tuple-element.98.index_ref, f32[8192,128]{1,0:T(8,128)} %bitcast.41, bf16[16,512,128]{2,1,0:T(8,128)(2,1)} %grad_gather.2.refs_0_), custom_call_target="tpu_custom_call" | custom-call | bytes 3200 | tf_op jit(solution)/shard_map/grad_gather/pallas_call | solution.py:193
  359.5 7.1 %all-to-all-done.4.got_ref = bf16[16,512,128]{2,1,0:T(8,128)(2,1)S(1)} async-done(((bf16[16,512,128]{2,1,0:T(8,128)(2,1)}), bf16[16,512,128]{2,1,0:T(8,128)(2,1)S(1)}, u32[]{:S(2)}, u32[]{:S(2)}) %all-to-all-start.4) | async-done | bytes 2097184 | tf_op jit(solution)/shard_map/all_to_all | solution.py:836
  366.6 1.3 copy-done.4
  367.9 11.2 %all-to-all-start.3 = ((bf16[16,512,128]{2,1,0:T(8,128)(2,1)}), bf16[16,512,128]{2,1,0:T(8,128)(2,1)S(1)}, u32[]{:S(2)}, u32[]{:S(2)}) async-start(bf16[16,512,128]{2,1,0:T(8,128)(2,1)} %grad_gather.3.refs_0_), calls=%async_computation.4 | async-start | bytes 4194304 | tf_op jit(solution)/shard_map/all_to_all | solution.py:836
  379.2 21.5 %scatter.2 = (bf16[4096,128]{1,0:T(8,128)(2,1)}, bf16[4096,128]{1,0:T(8,128)(2,1)}) custom-call(s32[65536]{0:T(1024)} %bitcast.44, s32[65536]{0:T(1024)} %bitcast.45, bf16[16,512,128]{2,1,0:T(8,128)(2,1)} %copy-done.4, bf16[16,512,128]{2,1,0:T(8,128)(2,1)} %grad_gather.3.refs_0_), custom_call_target="tpu_custom_call" | custom-call | bytes 2400 | tf_op jit(solution)/shard_map/scatter/pallas_call | solution.py:279
  400.7 1.5 collective-permute-start.1
  402.2 5.3 pad_maximum_fusion.refs_0_
  407.5 12.8 %all-to-all-done.3.refs_1_.got_ref = bf16[16,512,128]{2,1,0:T(8,128)(2,1)S(1)} async-done(((bf16[16,512,128]{2,1,0:T(8,128)(2,1)}), bf16[16,512,128]{2,1,0:T(8,128)(2,1)S(1)}, u32[]{:S(2)}, u32[]{:S(2)}) %all-to-all-start.3) | async-done | bytes 2097184 | tf_op jit(solution)/shard_map/all_to_all | solution.py:836
  420.3 6.1 %collective-permute-done.1.refs_2_.refs_0_.refs_1_ = bf16[4096,128]{1,0:T(8,128)(2,1)S(1)} collective-permute-done((bf16[4096,128]{1,0:T(8,128)(2,1)}, bf16[4096,128]{1,0:T(8,128)(2,1)S(1)}, u32[]{:S(2)}, u32[]{:S(2)}) %collective-permute-start.1) | collective-permute-done | bytes 1048608 | tf_op jit(solution)/shard_map/ppermute | solution.py:725
  428.6 1.5 collective-permute-start.2
  430.1 21.4 %scatter.3 = (bf16[4096,128]{1,0:T(8,128)(2,1)}, bf16[4096,128]{1,0:T(8,128)(2,1)}) custom-call(s32[65536]{0:T(1024)} %bitcast.46, s32[65536]{0:T(1024)} %bitcast.47, bf16[16,512,128]{2,1,0:T(8,128)(2,1)} %copy-done, bf16[4096,128]{1,0:T(8,128)(2,1)} %copy-done.1), custom_call_target="tpu_custom_call" | custom-call | bytes 2400 | tf_op jit(solution)/shard_map/scatter/pallas_call | solution.py:279
  451.5 1.8 collective-permute-done.2.refs_1_
  454.3 1.5 collective-permute-start.3
  455.8 22.5 %collective-permute-done.3.refs_1_.refs_3_ = bf16[4096,128]{1,0:T(8,128)(2,1)S(1)} collective-permute-done((bf16[4096,128]{1,0:T(8,128)(2,1)}, bf16[4096,128]{1,0:T(8,128)(2,1)S(1)}, u32[]{:S(2)}, u32[]{:S(2)}) %collective-permute-start.3) | collective-permute-done | bytes 1048608 | tf_op jit(solution)/shard_map/ppermute | solution.py:725
  479.3 1.5 collective-permute-start.4
  480.8 1.4 slice_reduce_fusion.2
  484.4 14.9 %table_adam.2 = (f32[16384,128]{1,0:T(8,128)}, f32[16384,128]{1,0:T(8,128)}, f32[16384,128]{1,0:T(8,128)}, f32[8,128]{1,0:T(8,128)}) custom-call(bf16[4096,128]{1,0:T(8,128)(2,1)} %get-tuple-element.62.refs_0_, bf16[4096,128]{1,0:T(8,128)(2,1)} %copy-done.1, bf16[4096,128]{1,0:T(8,128)(2,1)} %order.6.refs_2_, bf16[4096,128]{1,0:T(8,128)(2,1)} %copy-done.5, ...), custom_call_target="tpu_custom_call" | custom-call | bytes 700 | tf_op jit(solution)/shard_map/table_adam/pallas_call | solution.py:331
  499.2 3.3 collective-permute-done.4.refs_3_
  503.5 14.8 %table_adam.3 = (f32[16384,128]{1,0:T(8,128)}, f32[16384,128]{1,0:T(8,128)}, f32[16384,128]{1,0:T(8,128)}, f32[8,128]{1,0:T(8,128)}) custom-call(bf16[4096,128]{1,0:T(8,128)(2,1)} %get-tuple-element.63.refs_0_, bf16[4096,128]{1,0:T(8,128)(2,1)} %copy-done.6, ...), custom_call_target="tpu_custom_call", output_to_operand_aliasing={{0}: (7, {}), {1}: (8, {}), {2}: (9, {})} | custom-call | bytes 700 | tf_op jit(solution)/shard_map/table_adam/pallas_call | solution.py:331
  518.4 1.4 collective-permute-done.5
  521.3 3.1 collective-permute-done.6
  524.4 4.8 collective-permute-start.7
  529.2 1.8 collective-permute-done.7
  531.0 1.7 collective-permute-start.8
  532.7 3.0 collective-permute-done.8
  535.7 1.5 collective-permute-start.9
  537.1 1.7 slice.97.here_ref
  542.1 4.0 collective-permute-done.10.there_ref.other_ref
  546.8 7.3 %dense_adam.1 = (f32[8,64,512]{2,1,0:T(8,128)}, f32[8,64,512]{2,1,0:T(8,128)}, f32[8,64,512]{2,1,0:T(8,128)}, f32[40,64]{1,0:T(8,128)}, f32[40,64]{1,0:T(8,128)}...) custom-call(s32[1]{0:T(128)} %bitcast.22.rep_ref, ...), custom_call_target="tpu_custom_call" | custom-call | tf_op jit(solution)/shard_map/dense_adam/pallas_call | solution.py:705
  (103 shorter events, 27.0 us)
Async XLA Ops:
  7.2 83.3 %all-gather.2.cloned.1.call-start = ((), (), s32[]{:S(2)}) async-start(), calls=%async_computation.7 | async-start | bytes 5570560 | tf_op jit(solution)/shard_map/all_gather | solution.py:796
  74.3 47.3 %all-to-all-start.2 = ((bf16[16,512,128]{2,1,0:T(8,128)(2,1)}), bf16[16,512,128]{2,1,0:T(8,128)(2,1)S(1)}, u32[]{:S(2)}, u32[]{:S(2)}) async-start(bf16[16,512,128]{2,1,0:T(8,128)(2,1)} %owner_gather.3), calls=%async_computation.2 | async-start | bytes 4194304 | tf_op jit(solution)/shard_map/all_to_all | solution.py:836
  94.9 115.4 %collective-permute-start = (bf16[4,1024,512]{2,1,0:T(8,128)(2,1)}, bf16[4,1024,512]{2,1,0:T(8,128)(2,1)}, u32[]{:S(2)}, u32[]{:S(2)}) collective-permute-start(bf16[4,1024,512]{2,1,0:T(8,128)(2,1)} %slice.95), channel_id=1, source_target_pairs={{0,16},{16,0},{1,17},{17,1},{2,18},{18,2},{3,19},{19,3},{4,20},{20... | collective-permute-start | bytes 12582920 | tf_op jit(solution)/shard_map/ppermute | solution.py:725
  97.2 37.2 %copy-start.16 = (s32[32]{0:T(128)S(1)}, s32[32]{0:T(128)}, u32[]{:S(2)}) copy-start(s32[32]{0:T(128)} %param.22) | copy-start | bytes 388
  97.2 38.4 %copy-start.10 = (f32[4741]{0:T(1024)S(1)}, f32[4741]{0:T(1024)}, u32[]{:S(2)}) copy-start(f32[4741]{0:T(1024)} %param.37) | copy-start | bytes 56896
  97.2 40.3 %copy-start.12 = (s32[1024,5]{0,1:T(8,128)S(1)}, s32[1024,5]{0,1:T(8,128)}, u32[]{:S(2)}) copy-start(s32[1024,5]{0,1:T(8,128)} %param.23) | copy-start | bytes 61444
  97.2 40.3 %copy-start.13 = (s32[1024,5]{0,1:T(8,128)S(1)}, s32[1024,5]{0,1:T(8,128)}, u32[]{:S(2)}) copy-start(s32[1024,5]{0,1:T(8,128)} %param.24) | copy-start | bytes 61444
  117.8 23.8 %slice-start = ((f32[4741]{0:T(1024)}), f32[4096]{0:T(1024)S(1)}, s32[]{:S(2)}) async-start(f32[4741]{0:T(1024)} %param.37), calls=%async_computation.10 | async-start | bytes 32768 | tf_op jit(solution)/shard_map/slice | solution.py:858
  121.6 1.3 copy-start.3
  122.9 52.6 %all-to-all-start.1 = ((bf16[16,512,128]{2,1,0:T(8,128)(2,1)}), bf16[16,512,128]{2,1,0:T(8,128)(2,1)S(1)}, u32[]{:S(2)}, u32[]{:S(2)}) async-start(bf16[16,512,128]{2,1,0:T(8,128)(2,1)} %owner_gather.2), calls=%async_computation.1 | async-start | bytes 4194304 | tf_op jit(solution)/shard_map/all_to_all | solution.py:836
  134.1 268.1 %reduce-scatter.3.cloned.1.call-start = ((), (), s32[]{:S(2)}) async-start(), calls=%async_computation.8 | async-start | bytes 12582912 | tf_op jit(solution)/shard_map/reduce_scatter | solution.py:873
  175.5 1.3 copy-start.2
  314.5 52.1 %all-to-all-start.4 = ((bf16[16,512,128]{2,1,0:T(8,128)(2,1)}), bf16[16,512,128]{2,1,0:T(8,128)(2,1)S(1)}, u32[]{:S(2)}, u32[]{:S(2)}) async-start(bf16[16,512,128]{2,1,0:T(8,128)(2,1)} %grad_gather.2.refs_0_), calls=%async_computation.5 | async-start | bytes 4194304 | tf_op jit(solution)/shard_map/all_to_all | solution.py:836
  366.6 1.3 copy-start.4
  367.9 52.3 %all-to-all-start.3 = ((bf16[16,512,128]{2,1,0:T(8,128)(2,1)}), bf16[16,512,128]{2,1,0:T(8,128)(2,1)S(1)}, u32[]{:S(2)}, u32[]{:S(2)}) async-start(bf16[16,512,128]{2,1,0:T(8,128)(2,1)} %grad_gather.3.refs_0_), calls=%async_computation.4 | async-start | bytes 4194304 | tf_op jit(solution)/shard_map/all_to_all | solution.py:836
  379.2 139.2 %reduce-scatter.5.cloned.1.call-start = ((), (), s32[]{:S(2)}) async-start(), calls=%async_computation.9 | async-start | bytes 5570560 | tf_op jit(solution)/shard_map/reduce_scatter | solution.py:876
  400.7 25.7 %collective-permute-start.1 = (bf16[4096,128]{1,0:T(8,128)(2,1)}, bf16[4096,128]{1,0:T(8,128)(2,1)S(1)}, u32[]{:S(2)}, u32[]{:S(2)}) collective-permute-start(bf16[4096,128]{1,0:T(8,128)(2,1)} %get-tuple-element.62.refs_0_), channel_id=1, source_target_pairs={{0,16},{16,0},{1,17},{17,1},{2,18},{18,2},{3,19},{19,3},{4,20},{20... | collective-permute-start | bytes 3145736 | tf_op jit(solution)/shard_map/ppermute | solution.py:725
  420.3 6.1 %copy-start = (bf16[16,512,128]{2,1,0:T(8,128)(2,1)}, bf16[16,512,128]{2,1,0:T(8,128)(2,1)S(1)}, u32[]{:S(2)}) copy-start(bf16[16,512,128]{2,1,0:T(8,128)(2,1)S(1)} %all-to-all-done.3.refs_1_.got_ref) | copy-start | bytes 6291460
  426.4 1.0 copy-start.1
  427.3 1.2 copy-start.8
  427.4 55.6 %copy-start.11 = (f32[8,1,512]{2,1,0:T(1,128)S(1)}, f32[8,1,512]{2,1,0:T(1,128)}, u32[]{:S(2)}) copy-start(f32[8,1,512]{2,1,0:T(1,128)} %get-tuple-element.53) | copy-start | bytes 49156
  428.6 24.7 %collective-permute-start.2 = (bf16[4096,128]{1,0:T(8,128)(2,1)S(1)}, bf16[4096,128]{1,0:T(8,128)(2,1)S(1)}, u32[]{:S(2)}, u32[]{:S(2)}) collective-permute-start(bf16[4096,128]{1,0:T(8,128)(2,1)S(1)} %copy-done.8), channel_id=1, source_target_pairs={{0,16},{16,0},{1,17},{17,1},{2,18},{18,2},{3,19},{19,3},{4,20},{20... | collective-permute-start | bytes 3145736 | tf_op jit(solution)/shard_map/ppermute | solution.py:725
  453.3 1.0 copy-start.6
  454.3 24.0 %collective-permute-start.3 = (bf16[4096,128]{1,0:T(8,128)(2,1)}, bf16[4096,128]{1,0:T(8,128)(2,1)S(1)}, u32[]{:S(2)}, u32[]{:S(2)}) collective-permute-start(bf16[4096,128]{1,0:T(8,128)(2,1)} %order.6.refs_2_), channel_id=1, source_target_pairs={{0,16},{16,0},{1,17},{17,1},{2,18},{18,2},{3,19},{19,3},{4,20},{20... | collective-permute-start | bytes 3145736 | tf_op jit(solution)/shard_map/ppermute | solution.py:725
  478.3 1.0 copy-start.5
  479.3 23.2 %collective-permute-start.4 = (bf16[4096,128]{1,0:T(8,128)(2,1)}, bf16[4096,128]{1,0:T(8,128)(2,1)S(1)}, u32[]{:S(2)}, u32[]{:S(2)}) collective-permute-start(bf16[4096,128]{1,0:T(8,128)(2,1)} %order.7.refs_2_), channel_id=1, source_target_pairs={{0,16},{16,0},{1,17},{17,1},{2,18},{18,2},{3,19},{19,3},{4,20},{20... | collective-permute-start | bytes 3145736 | tf_op jit(solution)/shard_map/ppermute | solution.py:725
  502.5 1.0 copy-start.9
  503.5 37.9 %copy-start.14 = (f32[4741]{0:T(1024)S(1)}, f32[4741]{0:T(1024)}, u32[]{:S(2)}) copy-start(f32[4741]{0:T(1024)} %param.38) | copy-start | bytes 56896
  503.5 37.9 %copy-start.15 = (f32[4741]{0:T(1024)S(1)}, f32[4741]{0:T(1024)}, u32[]{:S(2)}) copy-start(f32[4741]{0:T(1024)} %param.39) | copy-start | bytes 56896
  518.4 1.5 collective-permute-start.5
  520.6 3.8 collective-permute-start.6
  524.4 6.6 %collective-permute-start.7 = (f32[40,128]{1,0:T(8,128)S(1)}, f32[40,128]{1,0:T(8,128)S(1)}, u32[]{:S(2)}, u32[]{:S(2)}) collective-permute-start(f32[40,128]{1,0:T(8,128)S(1)} %add.166), channel_id=1, source_target_pairs={{0,4},{1,5},{2,6},{3,7},{4,0},{5,1},{6,2},{7,3},{8,12},{9,13},{10,... | collective-permute-start | bytes 61448 | tf_op jit(solution)/shard_map/ppermute | solution.py:736
  531.0 4.7 collective-permute-start.8
  535.7 3.9 collective-permute-start.9
  538.8 7.3 %collective-permute-start.10 = (bf16[5,64,512]{2,1,0:T(8,128)(2,1)}, bf16[5,64,512]{2,1,0:T(8,128)(2,1)S(1)}, u32[]{:S(2)}, u32[]{:S(2)}) collective-permute-start(bf16[5,64,512]{2,1,0:T(8,128)(2,1)} %order.8.refs_1_.more_ref), channel_id=1, source_target_pairs={{0,16},{16,0},{1,17},{17,1},{2,18},{18,2},{3,19},{19,3},{4,20},{20... | collective-permute-start | bytes 983048 | tf_op jit(solution)/shard_map/ppermute | solution.py:725
  546.1 0.7 copy-start.7
Sparse Core Ops, SparseCore 0:
  11.2 61.0 all-gather.1
  280.7 105.5 reduce-scatter.2
  427.5 80.1 reduce-scatter.4

commit v3 on v2

--- a/solution.py
+++ b/solution.py
@@ -16,7 +16,7 @@
 TOWER = 64
 STEP = 10
 LANES = 128
-UNROLL = 64
+UNROLL = 256
 RMW = 8
 PARTS = 8
 PACKED = 3 * LANES
@@ -69,7 +69,9 @@
     return pl.CostEstimate(flops=0, bytes_accessed=int(micros * 1.0e2), transcendentals=0)
 
 
-def owner_gather_kernel(distinct, table_at, want_ref, table_ref, out_ref, rows_ref):
+def owner_gather_kernel(distinct, table_at, want_ref, table_ref, *refs):
+    out_ref, rows_ref = refs[-2:]
+
     def body(step, carry):
         base = step * UNROLL
         for u in range(UNROLL):
@@ -82,22 +84,23 @@
     out_ref[0] = packed.astype(jnp.bfloat16)
 
 
-def owner_gather(wanted, table, shards, distinct, table_at):
+def owner_gather(wanted, table, after, shards, distinct, table_at):
     rows = table.shape[0]
     return pl.pallas_call(
         functools.partial(owner_gather_kernel, distinct, table_at),
         name="owner_gather",
         grid=(shards,),
         in_specs=[
-            pl.BlockSpec((2 * distinct,), lambda i: (2 * i + table_at,), memory_space=pltpu.SMEM),
+            pl.BlockSpec((2 * distinct,), lambda i: (i,), memory_space=pltpu.SMEM),
             pl.BlockSpec((rows, LANES), lambda i: (0, 0), pipeline_mode=pl.Buffered(1)),
-        ],
+        ]
+        + [ANYWHERE] * len(after),
         out_specs=pl.BlockSpec((1, distinct // 2, LANES), lambda i: (i, 0, 0)),
         out_shape=jax.ShapeDtypeStruct((shards, distinct // 2, LANES), jnp.bfloat16),
         scratch_shapes=[pltpu.VMEM((distinct, LANES), jnp.float32)],
         compiler_params=params(),
         cost_estimate=cost(20),
-    )(wanted, table)
+    )(wanted, table, *after)
 
 
 def pool_kernel(samples, longest, distinct, table_at, *refs):
@@ -147,7 +150,7 @@
         grid=(pairs,),
         in_specs=[
             pl.BlockSpec(
-                (longest * samples,), lambda i: (i + table_at * pairs,), memory_space=pltpu.SMEM
+                (longest * samples,), lambda i: (i,), memory_space=pltpu.SMEM
             ),
             pl.BlockSpec((shards, half, LANES), lambda i: (0, 0, 0), pipeline_mode=pl.Buffered(1)),
         ]
@@ -195,7 +198,7 @@
         name="grad_gather",
         grid=(shards,),
         in_specs=[
-            pl.BlockSpec((2 * distinct,), lambda i: (2 * i + table_at,), memory_space=pltpu.SMEM),
+            pl.BlockSpec((2 * distinct,), lambda i: (i,), memory_space=pltpu.SMEM),
             pl.BlockSpec((count, LANES), lambda i: (0, 0), pipeline_mode=pl.Buffered(1)),
         ]
         + [ANYWHERE] * len(after),
@@ -273,7 +276,7 @@
     shards, half = arrived.shape[:2]
     distinct = 2 * half
     want = lambda j: pl.BlockSpec(
-        (2 * distinct,), lambda i: (2 * (2 * i + j) + table_at,), memory_space=pltpu.SMEM
+        (2 * distinct,), lambda i: (2 * i + j,), memory_space=pltpu.SMEM
     )
     count = rows // 2 // outs
     return pl.pallas_call(
@@ -725,16 +728,14 @@
     return lax.ppermute(value, "rep", [(0, 1), (1, 0)])
 
 
-def sum_everywhere(value):
-    for axis in ("shard", "rep"):
-        size = lax.axis_size(axis)
-        if size & (size - 1):
-            value = lax.psum(value, axis)
-            continue
-        shift = 1
-        while shift < size:
-            value = value + lax.ppermute(value, axis, [(i, i ^ shift) for i in range(size)])
-            shift *= 2
+def sum_over(value, axis, first, last):
+    size = lax.axis_size(axis)
+    if size & (size - 1):
+        return value if first else lax.psum(value, axis)
+    shift = 1 << first
+    while shift < min(size, 1 << last):
+        value = value + lax.ppermute(value, axis, [(i, i ^ shift) for i in range(size)])
+        shift *= 2
     return value
 
 
@@ -803,44 +804,43 @@
         turned = jnp.concatenate([value[part:], value[:part]], axis=0)
         return jnp.where(rep == 0, value, turned)
 
+    def exchange(value):
+        return lax.all_to_all(value, "shard", 0, 0, tiled=True)
+
     ids = jnp.transpose(row_ids, (1, 2, 3, 0))
     row = ids[:, :, 0, :] * ROW_BASE + ids[:, :, 1, :]
-    table_of = lax.broadcasted_iota(int32, row.shape, 0) // pairs
-    key = (row // rows_dev * TABLES + table_of) * rows_dev + row % rows_dev
-    place = lax.broadcasted_iota(int32, row.shape, 1)
-    unused = (place >= jnp.transpose(bag_lengths)[:, None, :]).astype(int32)
-    number = (
-        lax.broadcasted_iota(int32, row.shape, 0) * longest + place
-    ) * samples + lax.broadcasted_iota(int32, row.shape, 2)
-    payload = number + unused * slots
-    key, payload = lax.sort(
-        (key.reshape(slots), payload.reshape(slots)), num_keys=1, is_stable=False
-    )
-    position = jnp.arange(slots, dtype=int32)
-    skipped = payload >= slots
-    number = jnp.where(skipped, payload - slots, payload)
-    wanted = lax.all_to_all(
-        (key % rows_dev).reshape(shards, capacity), "shard", 0, 0, tiled=True
-    ).reshape(slots)
-    bag = number // (longest * samples)
-    grad_place = jnp.where(skipped, pairs * samples, bag % pairs * samples + number % samples)
-    reply_place = jnp.where(
-        skipped,
-        shards * distinct,
-        position // capacity * distinct + position % (2 * distinct) // 2,
-    )
-    span = 2 * shards * distinct
-    places = lax.sort(number * span + reply_place, is_stable=False) % span
-
-    def exchange(value):
-        return lax.all_to_all(value, "shard", 0, 0, tiled=True)
-
-    found = [owner_gather(wanted, tables, shards, distinct, t) for t in both]
-    found[1], places = lax.optimization_barrier((found[1], places))
+    lengths = jnp.transpose(bag_lengths)[:, None, :]
+    number = lax.broadcasted_iota(int32, (pairs, longest, samples), 0) * longest
+    place = lax.broadcasted_iota(int32, (pairs, longest, samples), 1)
+    number = (number + place) * samples + lax.broadcasted_iota(int32, (pairs, longest, samples), 2)
+    table_slots = pairs * longest * samples
+    position = jnp.arange(table_slots, dtype=int32)
+    span = table_slots
+    wanted, grad_place, places = [], [], []
+    for t in both:
+        mine = slice(t * pairs, (t + 1) * pairs)
+        payload = number + jnp.where(place >= lengths[mine], table_slots, 0)
+        key, payload = lax.sort(
+            (row[mine].reshape(table_slots), payload.reshape(table_slots)),
+            num_keys=1,
+            is_stable=False,
+        )
+        wanted.append(exchange((key % rows_dev).reshape(shards, 2 * distinct)).reshape(table_slots))
+        skipped = payload >= table_slots
+        slot = jnp.where(skipped, payload - table_slots, payload)
+        bag = slot // (longest * samples)
+        grad_place.append(
+            jnp.where(skipped, pairs * samples, bag * samples + slot % samples)
+        )
+        reply_place = jnp.where(skipped, shards * distinct, position // 2)
+        places.append(lax.sort(slot * span + reply_place, is_stable=False) % span)
+
+    after = [[], places]
+    found = [owner_gather(wanted[t], tables, after[t], shards, distinct, t) for t in both]
     replies = [exchange(value) for value in found]
     pooled = []
     for t in both:
-        pooled = [pool(places, replies[t], pooled, samples, longest, pairs, t)]
+        pooled = [pool(places[t], replies[t], pooled, samples, longest, pairs, t)]
 
     first_end = EXPERTS * HID
     second_end = first_end + TASKS * TOWER
@@ -891,13 +891,13 @@
     pooled_grad = pooled_grad.reshape(pairs * samples, LANES)
     sent = []
     for t in both:
-        sent.append(grad_gather(grad_place, pooled_grad, sent[:], shards, distinct, t))
+        sent.append(grad_gather(grad_place[t], pooled_grad, sent[:], shards, distinct, t))
     arrived = [exchange(value) for value in sent]
     chunks = (2, 2)
     table_parts = []
     after = [sent[1]]
     for t in both:
-        mine = scatter(wanted, arrived[t], after, rows_dev, t, chunks[t])
+        mine = scatter(wanted[t], arrived[t], after, rows_dev, t, chunks[t])
         if reps == 2:
             table_parts.append([])
             for n, value in enumerate(mine):
@@ -910,6 +910,10 @@
                 [(lax.psum(v.astype(jnp.float32), "rep"), jnp.zeros_like(v)) for v in mine]
             )
 
+    small_grad = order(small_grad, table_parts[1][0][0])
+    small_grad = sum_over(small_grad, "shard", 0, 1)
+    if reps == 2:
+        table_parts[1][0] = (table_parts[1][0][0], order(table_parts[1][0][1], small_grad))
     table_state = []
     tokens = []
     for chunk, second_parts in enumerate(table_parts[1]):
@@ -924,13 +928,15 @@
     if reps == 2:
         kept = order(kept, arrived[1], table_parts[0][0][1])
     summed = owned_sum(kept)
+    shard_bits = 2 if reps == 2 else 1
     expert = (expert_w, expert_m, expert_v)
     gate = [jnp.transpose(value) for value in (gate_w, gate_m, gate_v)]
     tower = (tower_weight_matrix, tower_m, tower_v)
     if reps == 2:
         summed = order(summed, tokens[-1])
-        small_grad = order(small_grad, summed)
         there = swap_rep(summed)
+        small_grad = sum_over(order(small_grad, tokens[-1]), "shard", 1, 2)
+        small_grad = order(small_grad, there)
         here = summed[:part]
         extra = (summed, there)
     else:
@@ -944,7 +950,7 @@
     expert_new, expert_m_new, expert_v_new = expert_new
     gate_new, gate_m_new, gate_v_new = [jnp.transpose(value) for value in gate_new]
     tower_new, tower_m_new, tower_v_new = tower_new
-    small_sum = sum_everywhere(small_grad).reshape(padded)
+    small_sum = sum_over(sum_over(small_grad, "shard", shard_bits, 30), "rep", 0, 30).reshape(padded)
     small_new, small_m_new, small_v_new = adamw(
         small_params, small_sum[:small_size], small_m, small_v, rate_small
     )

time: 571 us -> 552 us (0.967)
  blocking collectives: 21.1 us -> 0 us
  Pallas kernels: 326 us -> 315 us
  starting transfers between devices: 56.8 us -> 67.3 us
  other arithmetic: 45.4 us -> 52.5 us
    all_to_all x1 -> x0, blocking collectives: 21.1 us -> none  [on_device(): lax.all_to_all((key % rows_dev).reshape(shards, capacity), 'shard', 0, 0,...]
    all_to_all x4 -> x6, starting transfers between devices: 39.6 us -> 50.3 us  [exchange(): return lax.all_to_all(value, 'shard', 0, 0, tiled=True)]
    sort x2 -> x4, other arithmetic: 27 us -> 30.2 us  [the longest x2 15.6 us: on_device(): lax.sort((row[mine].reshape(table_slots), payload.reshape(table_slots)),...]
    all_to_all x4 -> x6, waiting for transfers between devices: 23.7 us -> 25.3 us  [exchange(): return lax.all_to_all(value, 'shard', 0, 0, tiled=True)]
  transfers between devices with their start and end apart: 18 -> 20, of which waited for: 13 -> 13; matrix products, arithmetic and copies ran while one was open for 10% -> 11% of each run, Pallas kernels for 44% -> 45%
where the time goes in v3:
time: 552 us; the launch traced here: 544 us
  Pallas kernels  315 us (57%)
  starting transfers between devices  67.3 us (12%)
  waiting for transfers between devices  67.3 us (12%)
  other arithmetic  52.5 us (10%)
  local copies, waits for them, and re-layouts  25.8 us (5%)
  between operations  15.9 us (3%)
    pallas_call x2, Pallas kernels, grad_gather(): pl.pallas_call(functools.partial(grad_gather_kernel, distinct, table_at),...  63.9 us
    pallas_call x2, Pallas kernels, pool(): pl.pallas_call(functools.partial(pool_kernel, samples, longest, distinct,...  62.5 us
    pallas_call x1, Pallas kernels, dense(): pl.pallas_call(functools.partial(dense_kernel, shards, len(weights)), nam...  53.1 us
    all_to_all x6, starting transfers between devices, exchange(): return lax.all_to_all(value, 'shard', 0, 0, tiled=True)  50.3 us
    pallas_call x2, Pallas kernels, scatter(): pl.pallas_call(functools.partial(scatter_kernel, distinct, table_at, outs...  42.9 us
    pallas_call x2, Pallas kernels, owner_gather(): pl.pallas_call(functools.partial(owner_gather_kernel, distinct, table_at)...  38.9 us
    ppermute x6, waiting for transfers between devices, swap_rep(): return lax.ppermute(value, 'rep', [(0, 1), (1, 0)])  33.5 us
    pallas_call x2, Pallas kernels, table_adam(): pl.pallas_call(table_adam_kernel, name='table_adam', grid=(2 * steps,), i...  29.7 us
  transfers between devices with their start and end apart: 20, of which 13 were waited for; matrix products, arithmetic and copies ran while one was open for 11% of the time, Pallas kernels for 45%

profile of v3, /device:TPU:0, one launch (start us, length us, event | category | flops | bytes accessed | tf_op | source)
XLA Modules:
  0.0 544.3 jit_solution(9032982459956726088)
XLA Ops:
  12.0 1.7 slice_add_fusion
  13.8 7.8 %sort.46 = (s32[32768]{0:T(1024)S(1)}, s32[32768]{0:T(1024)S(1)}) sort(s32[32768]{0:T(1024)S(1)} %bitcast.55, s32[32768]{0:T(1024)S(1)} %bitcast.52), dimensions={0}, to_apply=%region_2.3 | sort | flops 491520 | bytes 524288 | tf_op jit(solution)/shard_map/sort | solution.py:823
  22.3 7.9 %all-to-all-start.2 = ((s32[16,1,2048]{2,1,0:T(1,128)}), s32[16,1,2048]{2,1,0:T(1,128)S(1)}, u32[]{:S(2)}, u32[]{:S(2)}) async-start(s32[16,1,2048]{2,1,0:T(1,128)} %bitcast.7), calls=%async_computation.2 | async-start | bytes 262144 | tf_op jit(solution)/shard_map/all_to_all | solution.py:808
  30.2 7.8 %sort.44 = (s32[32768]{0:T(1024)S(1)}, s32[32768]{0:T(1024)S(1)}) sort(s32[32768]{0:T(1024)S(1)} %bitcast.54, s32[32768]{0:T(1024)S(1)} %bitcast.53), dimensions={0}, to_apply=%region_0.1 | sort | flops 491520 | bytes 524288 | tf_op jit(solution)/shard_map/sort | solution.py:823
  38.7 1.5 all-to-all-done.2
  40.2 4.6 all-to-all-start
  44.9 19.4 %owner_gather.3 = bf16[16,512,128]{2,1,0:T(8,128)(2,1)} custom-call(s32[32768]{0:T(1024)} %bitcast.48, f32[16384,128]{1,0:T(8,128)} %refs_4_.3), custom_call_target="tpu_custom_call" | custom-call | bytes 2000 | tf_op jit(solution)/shard_map/owner_gather/pallas_call | solution.py:89
  64.3 6.2 %all-to-all-start.3 = ((bf16[16,512,128]{2,1,0:T(8,128)(2,1)}), bf16[16,512,128]{2,1,0:T(8,128)(2,1)S(1)}, u32[]{:S(2)}, u32[]{:S(2)}) async-start(bf16[16,512,128]{2,1,0:T(8,128)(2,1)} %owner_gather.3), calls=%async_computation.3 | async-start | bytes 4194304 | tf_op jit(solution)/shard_map/all_to_all | solution.py:808
  71.3 7.3 %sort.47 = s32[32768]{0:T(1024)S(1)} sort(s32[32768]{0:T(1024)S(1)} %get-tuple-element.101), dimensions={0}, to_apply=%region_3.4 | sort | flops 491520 | bytes 262144 | tf_op jit(solution)/shard_map/sort | solution.py:836
  79.4 7.3 %sort.45 = s32[32768]{0:T(1024)S(1)} sort(s32[32768]{0:T(1024)S(1)} %get-tuple-element.103), dimensions={0}, to_apply=%region_1.2 | sort | flops 491520 | bytes 262144 | tf_op jit(solution)/shard_map/sort | solution.py:836
  87.4 4.5 slice.119
  91.9 1.5 collective-permute-start
  94.1 19.4 %owner_gather.2 = bf16[16,512,128]{2,1,0:T(8,128)(2,1)} custom-call(s32[32768]{0:T(1024)} %bitcast.45, f32[16384,128]{1,0:T(8,128)} %refs_4_.3, s32[32768]{0:T(1024)} %add_select_fusion.5.refs_0_, s32[32768]{0:T(1024)} %add_select_fusion.8.refs_1_.refs_0_), custom_call_target="tpu_custom_call" | custom-call | bytes 2000 | tf_op jit(solution)/shard_map/owner_gather/pallas_call | solution.py:89
  114.9 9.2 %all-to-all-start.1 = ((bf16[16,512,128]{2,1,0:T(8,128)(2,1)}), bf16[16,512,128]{2,1,0:T(8,128)(2,1)S(1)}, u32[]{:S(2)}, u32[]{:S(2)}) async-start(bf16[16,512,128]{2,1,0:T(8,128)(2,1)} %owner_gather.2), calls=%async_computation.1 | async-start | bytes 4194304 | tf_op jit(solution)/shard_map/all_to_all | solution.py:808
  132.0 31.2 %pool.2.refs_2_ = bf16[8,1024,128]{2,1,0:T(8,128)(2,1)} custom-call(s32[32768]{0:T(1024)} %add_select_fusion.5.refs_0_, bf16[16,512,128]{2,1,0:T(8,128)(2,1)} %copy-done.4), custom_call_target="tpu_custom_call" | custom-call | bytes 3000 | tf_op jit(solution)/shard_map/pool/pallas_call | solution.py:147
  163.3 2.0 all-to-all-done.1.refs_1_
  166.5 31.3 %pool.3.pooled_ref = bf16[8,1024,128]{2,1,0:T(8,128)(2,1)} custom-call(s32[32768]{0:T(1024)} %add_select_fusion.8.refs_1_.refs_0_, bf16[16,512,128]{2,1,0:T(8,128)(2,1)} %copy-done.3, bf16[8,1024,128]{2,1,0:T(8,128)(2,1)} %pool.2.refs_2_), custom_call_target="tpu_custom_call" | custom-call | bytes 3000 | tf_op jit(solution)/shard_map/pool/pallas_call | solution.py:147
  197.8 53.1 %dense.1 = (f32[8,1024,128]{2,1,0:T(8,128)}, bf16[8,1024,512]{2,1,0:T(8,128)(2,1)}, bf16[1024,1024]{1,0:T(8,128)(2,1)}, bf16[1024,128]{1,0:T(8,128)(2,1)}, f32[3...) custom-call(s32[1]{0:T(128)} %bitcast.base_ref, bf16[8,1024,128]{2,1,0:T(8,128)(2,1)} %pool.3.pooled_ref, ...), custom_call_target="tpu_custom_call" | custom-call | bytes 6000 | tf_op jit(solution)/shard_map/dense/pallas_call | solution.py:549
  250.9 17.1 %weight_grads.1 = (bf16[8,1024,512]{2,1,0:T(8,128)(2,1)}, bf16[1,1024,512]{2,1,0:T(8,128)(2,1)}) custom-call(s32[8]{0:T(128)} %and_select_fusion.which_ref, bf16[1024,1024]{1,0:T(8,128)(2,1)} %get-tuple-element.64.x_ref, bf16[8,1024,512]{2,1,0:T(8,128)(2,1)} %get-tuple-element.65.expert_ref, bf16[1024,128]{1,0:T(8,128)(2,1)} %get-tuple-element.66.gate_ref, ...), custom_call_target="tpu_custom_call" | custom-call | bytes 1800 | tf_op jit(solution)/shard_map/weight_grads/pallas_call | solution.py:636
  268.1 31.9 %grad_gather.2.refs_0_ = bf16[16,512,128]{2,1,0:T(8,128)(2,1)} custom-call(s32[32768]{0:T(1024)} %get-tuple-element.100.index_ref, f32[8192,128]{1,0:T(8,128)} %bitcast.43), custom_call_target="tpu_custom_call" | custom-call | bytes 3200 | tf_op jit(solution)/shard_map/grad_gather/pallas_call | solution.py:196
  299.9 11.2 %all-to-all-start.5 = ((bf16[16,512,128]{2,1,0:T(8,128)(2,1)}), bf16[16,512,128]{2,1,0:T(8,128)(2,1)S(1)}, u32[]{:S(2)}, u32[]{:S(2)}) async-start(bf16[16,512,128]{2,1,0:T(8,128)(2,1)} %grad_gather.2.refs_0_), calls=%async_computation.5 | async-start | bytes 4194304 | tf_op jit(solution)/shard_map/all_to_all | solution.py:808
  311.1 32.1 %grad_gather.3.refs_0_ = bf16[16,512,128]{2,1,0:T(8,128)(2,1)} custom-call(s32[32768]{0:T(1024)} %get-tuple-element.102.index_ref, f32[8192,128]{1,0:T(8,128)} %bitcast.44, bf16[16,512,128]{2,1,0:T(8,128)(2,1)} %grad_gather.2.refs_0_), custom_call_target="tpu_custom_call" | custom-call | bytes 3200 | tf_op jit(solution)/shard_map/grad_gather/pallas_call | solution.py:196
  343.2 9.0 %all-to-all-done.5.got_ref = bf16[16,512,128]{2,1,0:T(8,128)(2,1)S(1)} async-done(((bf16[16,512,128]{2,1,0:T(8,128)(2,1)}), bf16[16,512,128]{2,1,0:T(8,128)(2,1)S(1)}, u32[]{:S(2)}, u32[]{:S(2)}) %all-to-all-start.5) | async-done | bytes 2097184 | tf_op jit(solution)/shard_map/all_to_all | solution.py:808
  353.6 11.2 %all-to-all-start.4 = ((bf16[16,512,128]{2,1,0:T(8,128)(2,1)}), bf16[16,512,128]{2,1,0:T(8,128)(2,1)S(1)}, u32[]{:S(2)}, u32[]{:S(2)}) async-start(bf16[16,512,128]{2,1,0:T(8,128)(2,1)} %grad_gather.3.refs_0_), calls=%async_computation.4 | async-start | bytes 4194304 | tf_op jit(solution)/shard_map/all_to_all | solution.py:808
  364.8 21.5 %scatter.2 = (bf16[4096,128]{1,0:T(8,128)(2,1)}, bf16[4096,128]{1,0:T(8,128)(2,1)}) custom-call(s32[32768]{0:T(1024)} %bitcast.49, s32[32768]{0:T(1024)} %bitcast.50, bf16[16,512,128]{2,1,0:T(8,128)(2,1)} %copy-done.5, bf16[16,512,128]{2,1,0:T(8,128)(2,1)} %grad_gather.3.refs_0_), custom_call_target="tpu_custom_call" | custom-call | bytes 2400 | tf_op jit(solution)/shard_map/scatter/pallas_call | solution.py:282
  386.3 1.5 collective-permute-start.1
  387.8 5.3 pad_maximum_fusion.refs_0_
  393.1 12.8 %all-to-all-done.4.got_ref.refs_1_ = bf16[16,512,128]{2,1,0:T(8,128)(2,1)S(1)} async-done(((bf16[16,512,128]{2,1,0:T(8,128)(2,1)}), bf16[16,512,128]{2,1,0:T(8,128)(2,1)S(1)}, u32[]{:S(2)}, u32[]{:S(2)}) %all-to-all-start.4) | async-done | bytes 2097184 | tf_op jit(solution)/shard_map/all_to_all | solution.py:808
  405.9 6.1 %collective-permute-done.1.refs_0_.refs_1_.refs_2_ = bf16[4096,128]{1,0:T(8,128)(2,1)S(1)} collective-permute-done((bf16[4096,128]{1,0:T(8,128)(2,1)}, bf16[4096,128]{1,0:T(8,128)(2,1)S(1)}, u32[]{:S(2)}, u32[]{:S(2)}) %collective-permute-start.1) | collective-permute-done | bytes 1048608 | tf_op jit(solution)/shard_map/ppermute | solution.py:728
  414.2 1.5 collective-permute-start.2
  415.7 21.4 %scatter.3 = (bf16[4096,128]{1,0:T(8,128)(2,1)}, bf16[4096,128]{1,0:T(8,128)(2,1)}) custom-call(s32[32768]{0:T(1024)} %bitcast.46, s32[32768]{0:T(1024)} %bitcast.47, bf16[16,512,128]{2,1,0:T(8,128)(2,1)} %copy-done, bf16[4096,128]{1,0:T(8,128)(2,1)} %copy-done.2), custom_call_target="tpu_custom_call" | custom-call | bytes 2400 | tf_op jit(solution)/shard_map/scatter/pallas_call | solution.py:282
  437.1 1.8 collective-permute-done.2.refs_1_
  439.9 1.5 collective-permute-start.4
  441.4 22.5 %collective-permute-done.4.refs_1_.refs_0_ = bf16[4096,128]{1,0:T(8,128)(2,1)S(1)} collective-permute-done((bf16[4096,128]{1,0:T(8,128)(2,1)}, bf16[4096,128]{1,0:T(8,128)(2,1)S(1)}, u32[]{:S(2)}, u32[]{:S(2)}) %collective-permute-start.4) | collective-permute-done | bytes 1048608 | tf_op jit(solution)/shard_map/ppermute | solution.py:728
  464.9 1.5 collective-permute-start.5
  466.4 1.4 slice_reduce_fusion.2
  470.0 1.4 collective-permute-done.3
  472.7 14.9 %table_adam.2 = (f32[16384,128]{1,0:T(8,128)}, f32[16384,128]{1,0:T(8,128)}, f32[16384,128]{1,0:T(8,128)}, f32[8,128]{1,0:T(8,128)}) custom-call(bf16[4096,128]{1,0:T(8,128)(2,1)} %get-tuple-element.56.refs_0_, bf16[4096,128]{1,0:T(8,128)(2,1)} %copy-done.2, bf16[4096,128]{1,0:T(8,128)(2,1)} %order.8.refs_1_.refs_2_, bf16[4096,128]{1,0:T(8,128)(2,1)} %order.11.refs_3_, ...), custom_call_target="tpu_custom_call" | custom-call | bytes 700 | tf_op jit(solution)/shard_map/table_adam/pallas_call | solution.py:334
  489.1 14.8 %table_adam.3 = (f32[16384,128]{1,0:T(8,128)}, f32[16384,128]{1,0:T(8,128)}, f32[16384,128]{1,0:T(8,128)}, f32[8,128]{1,0:T(8,128)}) custom-call(bf16[4096,128]{1,0:T(8,128)(2,1)} %get-tuple-element.58.refs_0_, bf16[4096,128]{1,0:T(8,128)(2,1)} %copy-done.6, ...), custom_call_target="tpu_custom_call", output_to_operand_aliasing={{0}: (7, {}), {1}: (8, {}), {2}: (9, {})} | custom-call | bytes 700 | tf_op jit(solution)/shard_map/table_adam/pallas_call | solution.py:334
  504.0 1.6 collective-permute-start.7
  506.2 3.3 collective-permute-done.6
  510.9 2.6 collective-permute-done.7.refs_1_.there_ref.other_ref
  514.2 3.2 collective-permute-start.8
  517.5 2.0 collective-permute-done.8
  520.2 3.5 collective-permute-start.9
  523.7 1.8 collective-permute-done.9
  525.9 1.7 slice.121.here_ref
  527.5 7.3 %dense_adam.1 = (f32[8,64,512]{2,1,0:T(8,128)}, f32[8,64,512]{2,1,0:T(8,128)}, f32[8,64,512]{2,1,0:T(8,128)}, f32[40,64]{1,0:T(8,128)}, f32[40,64]{1,0:T(8,128)}...) custom-call(s32[1]{0:T(128)} %bitcast.25.rep_ref, ...), custom_call_target="tpu_custom_call" | custom-call | tf_op jit(solution)/shard_map/dense_adam/pallas_call | solution.py:708
  (116 shorter events, 35.3 us)
Async XLA Ops:
  7.2 80.3 %all-gather.2.cloned.1.call-start = ((), (), s32[]{:S(2)}) async-start(), calls=%async_computation.8 | async-start | bytes 5570560 | tf_op jit(solution)/shard_map/all_gather | solution.py:797
  22.3 17.9 %all-to-all-start.2 = ((s32[16,1,2048]{2,1,0:T(1,128)}), s32[16,1,2048]{2,1,0:T(1,128)S(1)}, u32[]{:S(2)}, u32[]{:S(2)}) async-start(s32[16,1,2048]{2,1,0:T(1,128)} %bitcast.7), calls=%async_computation.2 | async-start | bytes 262144 | tf_op jit(solution)/shard_map/all_to_all | solution.py:808
  40.2 4.6 copy-start.9
  40.2 24.1 %all-to-all-start = ((s32[16,1,2048]{2,1,0:T(1,128)}), s32[16,1,2048]{2,1,0:T(1,128)S(1)}, u32[]{:S(2)}, u32[]{:S(2)}) async-start(s32[16,1,2048]{2,1,0:T(1,128)} %bitcast.4), calls=%async_computation | async-start | bytes 262144 | tf_op jit(solution)/shard_map/all_to_all | solution.py:808
  64.3 27.6 %copy-start.8 = (s32[16,1,2048]{2,1,0:T(1,128)}, s32[16,1,2048]{2,1,0:T(1,128)S(1)}, u32[]{:S(2)}) copy-start(s32[16,1,2048]{2,1,0:T(1,128)S(1)} %all-to-all-done) | copy-start | bytes 393220
  64.3 49.3 %all-to-all-start.3 = ((bf16[16,512,128]{2,1,0:T(8,128)(2,1)}), bf16[16,512,128]{2,1,0:T(8,128)(2,1)S(1)}, u32[]{:S(2)}, u32[]{:S(2)}) async-start(bf16[16,512,128]{2,1,0:T(8,128)(2,1)} %owner_gather.3), calls=%async_computation.3 | async-start | bytes 4194304 | tf_op jit(solution)/shard_map/all_to_all | solution.py:808
  91.9 105.9 %collective-permute-start = (bf16[4,1024,512]{2,1,0:T(8,128)(2,1)}, bf16[4,1024,512]{2,1,0:T(8,128)(2,1)}, u32[]{:S(2)}, u32[]{:S(2)}) collective-permute-start(bf16[4,1024,512]{2,1,0:T(8,128)(2,1)} %slice.119), channel_id=1, source_target_pairs={{0,16},{16,0},{1,17},{17,1},{2,18},{18,2},{3,19},{19,3},{4,20},{20... | collective-permute-start | bytes 12582920 | tf_op jit(solution)/shard_map/ppermute | solution.py:728
  94.1 30.1 %copy-start.18 = (s32[32]{0:T(128)S(1)}, s32[32]{0:T(128)}, u32[]{:S(2)}) copy-start(s32[32]{0:T(128)} %param.22) | copy-start | bytes 388
  94.1 31.3 %copy-start.12 = (f32[4741]{0:T(1024)S(1)}, f32[4741]{0:T(1024)}, u32[]{:S(2)}) copy-start(f32[4741]{0:T(1024)} %param.37) | copy-start | bytes 56896
  94.1 33.2 %copy-start.14 = (s32[1024,5]{0,1:T(8,128)S(1)}, s32[1024,5]{0,1:T(8,128)}, u32[]{:S(2)}) copy-start(s32[1024,5]{0,1:T(8,128)} %param.23) | copy-start | bytes 61444
  94.1 33.2 %copy-start.15 = (s32[1024,5]{0,1:T(8,128)S(1)}, s32[1024,5]{0,1:T(8,128)}, u32[]{:S(2)}) copy-start(s32[1024,5]{0,1:T(8,128)} %param.24) | copy-start | bytes 61444
  113.6 17.8 %slice-start = ((f32[4741]{0:T(1024)}), f32[4096]{0:T(1024)S(1)}, s32[]{:S(2)}) async-start(f32[4741]{0:T(1024)} %param.37), calls=%async_computation.11 | async-start | bytes 32768 | tf_op jit(solution)/shard_map/slice | solution.py:858
  113.6 1.3 copy-start.4
  114.9 50.3 %all-to-all-start.1 = ((bf16[16,512,128]{2,1,0:T(8,128)(2,1)}), bf16[16,512,128]{2,1,0:T(8,128)(2,1)S(1)}, u32[]{:S(2)}, u32[]{:S(2)}) async-start(bf16[16,512,128]{2,1,0:T(8,128)(2,1)} %owner_gather.2), calls=%async_computation.1 | async-start | bytes 4194304 | tf_op jit(solution)/shard_map/all_to_all | solution.py:808
  124.1 263.7 %reduce-scatter.3.cloned.1.call-start = ((), (), s32[]{:S(2)}) async-start(), calls=%async_computation.9 | async-start | bytes 12582912 | tf_op jit(solution)/shard_map/reduce_scatter | solution.py:873
  165.2 1.3 copy-start.3
  299.9 52.3 %all-to-all-start.5 = ((bf16[16,512,128]{2,1,0:T(8,128)(2,1)}), bf16[16,512,128]{2,1,0:T(8,128)(2,1)S(1)}, u32[]{:S(2)}, u32[]{:S(2)}) async-start(bf16[16,512,128]{2,1,0:T(8,128)(2,1)} %grad_gather.2.refs_0_), calls=%async_computation.5 | async-start | bytes 4194304 | tf_op jit(solution)/shard_map/all_to_all | solution.py:808
  352.2 1.3 copy-start.5
  353.6 52.3 %all-to-all-start.4 = ((bf16[16,512,128]{2,1,0:T(8,128)(2,1)}), bf16[16,512,128]{2,1,0:T(8,128)(2,1)S(1)}, u32[]{:S(2)}, u32[]{:S(2)}) async-start(bf16[16,512,128]{2,1,0:T(8,128)(2,1)} %grad_gather.3.refs_0_), calls=%async_computation.4 | async-start | bytes 4194304 | tf_op jit(solution)/shard_map/all_to_all | solution.py:808
  364.8 139.2 %reduce-scatter.5.cloned.1.call-start = ((), (), s32[]{:S(2)}) async-start(), calls=%async_computation.10 | async-start | bytes 5570560 | tf_op jit(solution)/shard_map/reduce_scatter | solution.py:876
  386.3 25.7 %collective-permute-start.1 = (bf16[4096,128]{1,0:T(8,128)(2,1)}, bf16[4096,128]{1,0:T(8,128)(2,1)S(1)}, u32[]{:S(2)}, u32[]{:S(2)}) collective-permute-start(bf16[4096,128]{1,0:T(8,128)(2,1)} %get-tuple-element.56.refs_0_), channel_id=1, source_target_pairs={{0,16},{16,0},{1,17},{17,1},{2,18},{18,2},{3,19},{19,3},{4,20},{20... | collective-permute-start | bytes 3145736 | tf_op jit(solution)/shard_map/ppermute | solution.py:728
  405.9 6.1 %copy-start = (bf16[16,512,128]{2,1,0:T(8,128)(2,1)}, bf16[16,512,128]{2,1,0:T(8,128)(2,1)S(1)}, u32[]{:S(2)}) copy-start(bf16[16,512,128]{2,1,0:T(8,128)(2,1)S(1)} %all-to-all-done.4.got_ref.refs_1_) | copy-start | bytes 6291460
  412.0 1.0 copy-start.2
  413.0 1.2 copy-start.10
  413.0 55.6 %copy-start.13 = (f32[8,1,512]{2,1,0:T(1,128)S(1)}, f32[8,1,512]{2,1,0:T(1,128)}, u32[]{:S(2)}) copy-start(f32[8,1,512]{2,1,0:T(1,128)} %get-tuple-element.53) | copy-start | bytes 49156
  414.2 24.7 %collective-permute-start.2 = (bf16[4096,128]{1,0:T(8,128)(2,1)S(1)}, bf16[4096,128]{1,0:T(8,128)(2,1)S(1)}, u32[]{:S(2)}, u32[]{:S(2)}) collective-permute-start(bf16[4096,128]{1,0:T(8,128)(2,1)S(1)} %copy-done.10), channel_id=1, source_target_pairs={{0,16},{16,0},{1,17},{17,1},{2,18},{18,2},{3,19},{19,3},{4,20},{20... | collective-permute-start | bytes 3145736 | tf_op jit(solution)/shard_map/ppermute | solution.py:728
  438.9 1.0 copy-start.6
  439.9 24.0 %collective-permute-start.4 = (bf16[4096,128]{1,0:T(8,128)(2,1)}, bf16[4096,128]{1,0:T(8,128)(2,1)S(1)}, u32[]{:S(2)}, u32[]{:S(2)}) collective-permute-start(bf16[4096,128]{1,0:T(8,128)(2,1)} %order.8.refs_1_.refs_2_), channel_id=1, source_target_pairs={{0,16},{16,0},{1,17},{17,1},{2,18},{18,2},{3,19},{19,3},{4,20},{20... | collective-permute-start | bytes 3145736 | tf_op jit(solution)/shard_map/ppermute | solution.py:728
  463.9 1.0 copy-start.1
  464.9 23.2 %collective-permute-start.5 = (bf16[4096,128]{1,0:T(8,128)(2,1)}, bf16[4096,128]{1,0:T(8,128)(2,1)S(1)}, u32[]{:S(2)}, u32[]{:S(2)}) collective-permute-start(bf16[4096,128]{1,0:T(8,128)(2,1)} %order.10.refs_2_), channel_id=1, source_target_pairs={{0,16},{16,0},{1,17},{17,1},{2,18},{18,2},{3,19},{19,3},{4,20},{20... | collective-permute-start | bytes 3145736 | tf_op jit(solution)/shard_map/ppermute | solution.py:728
  470.0 1.4 collective-permute-start.3
  488.1 1.0 copy-start.11
  503.9 32.8 %copy-start.16 = (f32[4741]{0:T(1024)S(1)}, f32[4741]{0:T(1024)}, u32[]{:S(2)}) copy-start(f32[4741]{0:T(1024)} %param.38) | copy-start | bytes 56896
  503.9 32.8 %copy-start.17 = (f32[4741]{0:T(1024)S(1)}, f32[4741]{0:T(1024)}, u32[]{:S(2)}) copy-start(f32[4741]{0:T(1024)} %param.39) | copy-start | bytes 56896
  504.0 9.5 %collective-permute-start.7 = (bf16[5,64,512]{2,1,0:T(8,128)(2,1)}, bf16[5,64,512]{2,1,0:T(8,128)(2,1)S(1)}, u32[]{:S(2)}, u32[]{:S(2)}) collective-permute-start(bf16[5,64,512]{2,1,0:T(8,128)(2,1)} %order.14.more_ref), channel_id=1, source_target_pairs={{0,16},{16,0},{1,17},{17,1},{2,18},{18,2},{3,19},{19,3},{4,20},{20... | collective-permute-start | bytes 983048 | tf_op jit(solution)/shard_map/ppermute | solution.py:728
  505.5 4.0 collective-permute-start.6
  513.5 0.7 copy-start.7
  514.2 5.2 collective-permute-start.8
  520.2 5.3 collective-permute-start.9
  525.4 9.4 %collective-permute-start.10 = (f32[40,128]{1,0:T(8,128)S(1)}, f32[40,128]{1,0:T(8,128)S(1)}, u32[]{:S(2)}, u32[]{:S(2)}) collective-permute-start(f32[40,128]{1,0:T(8,128)S(1)} %add.167), channel_id=1, source_target_pairs={{0,16},{16,0},{1,17},{17,1},{2,18},{18,2},{3,19},{19,3},{4,20},{20... | collective-permute-start | bytes 61448 | tf_op jit(solution)/shard_map/ppermute | solution.py:737
Sparse Core Ops, SparseCore 0:
  11.2 62.7 all-gather.1
  268.2 105.7 reduce-scatter.2
  413.1 80.0 reduce-scatter.4

commit v4 on v3

--- a/solution.py
+++ b/solution.py
@@ -21,7 +21,6 @@
 PARTS = 8
 PACKED = 3 * LANES
 ANYWHERE = pl.BlockSpec(memory_space=pl.ANY)
-VMEM_BYTES = 60 << 20
 
 beta_first = 0.9
 beta_second = 0.999
@@ -49,8 +48,8 @@
     return lax.broadcasted_iota(jnp.int32, (rows, LANES), 1) < WIDTH
 
 
-def params(**kw):
-    return pltpu.CompilerParams(vmem_limit_bytes=VMEM_BYTES, **kw)
+def params(mebibytes=60):
+    return pltpu.CompilerParams(vmem_limit_bytes=mebibytes << 20)
 
 
 def pack(first, second, table):
@@ -150,9 +149,9 @@
         grid=(pairs,),
         in_specs=[
             pl.BlockSpec(
-                (longest * samples,), lambda i: (i,), memory_space=pltpu.SMEM
+                (longest * samples,), lambda i: (i + table_at * pairs,), memory_space=pltpu.SMEM
             ),
-            pl.BlockSpec((shards, half, LANES), lambda i: (0, 0, 0), pipeline_mode=pl.Buffered(1)),
+            pl.BlockSpec(memory_space=pltpu.VMEM),
         ]
         + [block] * len(before),
         out_specs=block,
@@ -161,7 +160,7 @@
             pltpu.VMEM((shards * distinct + 8, LANES), jnp.float32),
             pltpu.VMEM((samples, LANES), jnp.float32),
         ],
-        compiler_params=params(),
+        compiler_params=params(20),
         cost_estimate=cost(30),
     )(places, replies, *before)
 
@@ -296,7 +295,7 @@
             pltpu.VMEM((rows, LANES), jnp.float32),
             pltpu.VMEM((2, distinct, LANES), jnp.float32),
         ],
-        compiler_params=params(),
+        compiler_params=params(36),
         cost_estimate=cost(24),
     )(wanted, wanted, arrived, *after)
 
@@ -468,7 +467,7 @@
         pre = dot(x_ref[...], weight(e)) + bias_ref[e]
         sigma = jax.nn.sigmoid(pre)
         out = pre * sigma
-        slope_ref[e] = sigma + out * (1.0 - sigma)
+        slope_ref[e] = (sigma + out * (1.0 - sigma)).astype(bf16)
         out_low = out.astype(bf16)
         out_ref[e] = out_low
         product = dot(out_low, tower_ref[...])
@@ -540,7 +539,7 @@
     pairs, samples = pooled.shape[:2]
     inner = weights[0].shape[1]
     slabs = [weights[0].shape[0], EXPERTS + 1 - weights[0].shape[0]][: len(weights)]
-    block = 256
+    block = 512
     whole = lambda *shape: pl.BlockSpec(
         shape, lambda i: (0,) * len(shape), pipeline_mode=pl.Buffered(1)
     )
@@ -584,7 +583,7 @@
         ],
         scratch_shapes=[
             pltpu.VMEM((EXPERTS, block, HID), bf16),
-            pltpu.VMEM((EXPERTS, block, HID), f32),
+            pltpu.VMEM((EXPERTS, block, HID), bf16),
             pltpu.VMEM((EXPERTS, block, PACKED), f32),
             pltpu.VMEM((EXPERTS, block, PACKED), f32),
             pltpu.VMEM((block, PACKED), f32),
@@ -816,7 +815,7 @@
     table_slots = pairs * longest * samples
     position = jnp.arange(table_slots, dtype=int32)
     span = table_slots
-    wanted, grad_place, places = [], [], []
+    wanted, grad_place, inverse = [], [], []
     for t in both:
         mine = slice(t * pairs, (t + 1) * pairs)
         payload = number + jnp.where(place >= lengths[mine], table_slots, 0)
@@ -833,14 +832,15 @@
             jnp.where(skipped, pairs * samples, bag * samples + slot % samples)
         )
         reply_place = jnp.where(skipped, shards * distinct, position // 2)
-        places.append(lax.sort(slot * span + reply_place, is_stable=False) % span)
-
-    after = [[], places]
+        inverse.append((slot + t * table_slots) * span + reply_place)
+    places = lax.sort(jnp.concatenate(inverse), is_stable=False) % span
+
+    after = [[], [places]]
     found = [owner_gather(wanted[t], tables, after[t], shards, distinct, t) for t in both]
     replies = [exchange(value) for value in found]
     pooled = []
     for t in both:
-        pooled = [pool(places[t], replies[t], pooled, samples, longest, pairs, t)]
+        pooled = [pool(places, replies[t], pooled, samples, longest, pairs, t)]
 
     first_end = EXPERTS * HID
     second_end = first_end + TASKS * TOWER
@@ -928,14 +928,14 @@
     if reps == 2:
         kept = order(kept, arrived[1], table_parts[0][0][1])
     summed = owned_sum(kept)
-    shard_bits = 2 if reps == 2 else 1
+    shard_bits = 3 if reps == 2 else 1
     expert = (expert_w, expert_m, expert_v)
     gate = [jnp.transpose(value) for value in (gate_w, gate_m, gate_v)]
     tower = (tower_weight_matrix, tower_m, tower_v)
     if reps == 2:
         summed = order(summed, tokens[-1])
         there = swap_rep(summed)
-        small_grad = sum_over(order(small_grad, tokens[-1]), "shard", 1, 2)
+        small_grad = sum_over(order(small_grad, tokens[-1]), "shard", 1, 3)
         small_grad = order(small_grad, there)
         here = summed[:part]
         extra = (summed, there)

time: 552 us -> 548 us (level)
  local copies, waits for them, and re-layouts: 25.8 us -> 34.6 us
  Pallas kernels: 315 us -> 308 us
  other arithmetic: 52.5 us -> 46.1 us
    unnamed x41 -> x63, local copies, waits for them, and re-layouts: 10.7 us -> 19.5 us
    sort x2 -> x1, other arithmetic: 14.6 us -> 8.79 us  [on_device(): places = lax.sort(jnp.concatenate(inverse), is_stable=False) % span]
  transfers between devices with their start and end apart: 20 -> 20, of which waited for: 13 -> 13; matrix products, arithmetic and copies ran while one was open for 11% -> 10% of each run, Pallas kernels for 45% -> 44%
where the time goes in v4:
time: 548 us; the launch traced here: 540 us
  Pallas kernels  308 us (56%)
  waiting for transfers between devices  70.3 us (13%)
  starting transfers between devices  65 us (12%)
  other arithmetic  46.1 us (8%)
  local copies, waits for them, and re-layouts  34.6 us (6%)
  between operations  15.9 us (3%)
    pallas_call x2, Pallas kernels, grad_gather(): pl.pallas_call(functools.partial(grad_gather_kernel, distinct, table_at),...  64 us
    pallas_call x2, Pallas kernels, pool(): pl.pallas_call(functools.partial(pool_kernel, samples, longest, distinct,...  59 us
    all_to_all x6, starting transfers between devices, exchange(): return lax.all_to_all(value, 'shard', 0, 0, tiled=True)  52.3 us
    pallas_call x1, Pallas kernels, dense(): pl.pallas_call(functools.partial(dense_kernel, shards, len(weights)), nam...  51.1 us
    pallas_call x2, Pallas kernels, scatter(): pl.pallas_call(functools.partial(scatter_kernel, distinct, table_at, outs...  40.9 us
    pallas_call x2, Pallas kernels, owner_gather(): pl.pallas_call(functools.partial(owner_gather_kernel, distinct, table_at)...  38.9 us
    ppermute x6, waiting for transfers between devices, swap_rep(): return lax.ppermute(value, 'rep', [(0, 1), (1, 0)])  34.7 us
    pallas_call x2, Pallas kernels, table_adam(): pl.pallas_call(table_adam_kernel, name='table_adam', grid=(2 * steps,), i...  29.7 us
  transfers between devices with their start and end apart: 20, of which 13 were waited for; matrix products, arithmetic and copies ran while one was open for 10% of the time, Pallas kernels for 44%

profile of v4, /device:TPU:0, one launch (start us, length us, event | category | flops | bytes accessed | tf_op | source)
XLA Modules:
  0.0 539.7 jit_solution(15424617894137270110)
XLA Ops:
  12.0 1.7 slice_add_fusion
  13.8 7.8 %sort.37 = (s32[32768]{0:T(1024)S(1)}, s32[32768]{0:T(1024)S(1)}) sort(s32[32768]{0:T(1024)S(1)} %bitcast.55, s32[32768]{0:T(1024)S(1)} %bitcast.52), dimensions={0}, to_apply=%region_0.1 | sort | flops 491520 | bytes 524288 | tf_op jit(solution)/shard_map/sort | solution.py:822
  22.3 7.6 %all-to-all-start.2 = ((s32[16,1,2048]{2,1,0:T(1,128)}), s32[16,1,2048]{2,1,0:T(1,128)S(1)}, u32[]{:S(2)}, u32[]{:S(2)}) async-start(s32[16,1,2048]{2,1,0:T(1,128)} %bitcast.7), calls=%async_computation.2 | async-start | bytes 262144 | tf_op jit(solution)/shard_map/all_to_all | solution.py:807
  30.0 7.8 %sort.38 = (s32[32768]{0:T(1024)S(1)}, s32[32768]{0:T(1024)S(1)}) sort(s32[32768]{0:T(1024)S(1)} %bitcast.54, s32[32768]{0:T(1024)S(1)} %bitcast.53), dimensions={0}, to_apply=%region_1.2 | sort | flops 491520 | bytes 524288 | tf_op jit(solution)/shard_map/sort | solution.py:822
  38.5 1.5 all-to-all-done.2
  40.0 4.6 all-to-all-start
  44.6 19.4 %owner_gather.3 = bf16[16,512,128]{2,1,0:T(8,128)(2,1)} custom-call(s32[32768]{0:T(1024)} %bitcast.46, f32[16384,128]{1,0:T(8,128)} %refs_4_.3), custom_call_target="tpu_custom_call" | custom-call | bytes 2000 | tf_op jit(solution)/shard_map/owner_gather/pallas_call | solution.py:88
  64.1 6.5 %all-to-all-start.3 = ((bf16[16,512,128]{2,1,0:T(8,128)(2,1)}), bf16[16,512,128]{2,1,0:T(8,128)(2,1)S(1)}, u32[]{:S(2)}, u32[]{:S(2)}) async-start(bf16[16,512,128]{2,1,0:T(8,128)(2,1)} %owner_gather.3), calls=%async_computation.3 | async-start | bytes 4194304 | tf_op jit(solution)/shard_map/all_to_all | solution.py:807
  72.2 8.8 %sort.39 = s32[65536]{0:T(1024)S(1)} sort(s32[65536]{0:T(1024)S(1)} %pad_add_fusion), dimensions={0}, to_apply=%region_2.3 | sort | flops 1048576 | bytes 524288 | tf_op jit(solution)/shard_map/sort | solution.py:836
  81.0 4.5 slice.119
  85.5 1.5 collective-permute-start
  87.8 19.4 %owner_gather.2 = bf16[16,512,128]{2,1,0:T(8,128)(2,1)} custom-call(s32[32768]{0:T(1024)} %bitcast.43, f32[16384,128]{1,0:T(8,128)} %refs_4_.3, s32[65536]{0:T(1024)} %add_select_fusion.refs_0_), custom_call_target="tpu_custom_call" | custom-call | bytes 2000 | tf_op jit(solution)/shard_map/owner_gather/pallas_call | solution.py:88
  107.2 4.4 all-to-all-done.3.refs_1_
  111.6 1.3 copy-done.8
  112.9 11.2 %all-to-all-start.1 = ((bf16[16,512,128]{2,1,0:T(8,128)(2,1)}), bf16[16,512,128]{2,1,0:T(8,128)(2,1)S(1)}, u32[]{:S(2)}, u32[]{:S(2)}) async-start(bf16[16,512,128]{2,1,0:T(8,128)(2,1)} %owner_gather.2), calls=%async_computation.1 | async-start | bytes 4194304 | tf_op jit(solution)/shard_map/all_to_all | solution.py:807
  132.1 1.6 copy-done.9
  133.7 29.4 %pool.2.refs_2_ = bf16[8,1024,128]{2,1,0:T(8,128)(2,1)S(1)} custom-call(s32[65536]{0:T(1024)S(1)} %copy-done.13, bf16[16,512,128]{2,1,0:T(8,128)(2,1)S(1)} %copy-done.9), custom_call_target="tpu_custom_call" | custom-call | bytes 3000 | tf_op jit(solution)/shard_map/pool/pallas_call | solution.py:146
  165.3 1.6 copy-done.7
  166.9 29.6 %pool.3.pooled_ref = bf16[8,1024,128]{2,1,0:T(8,128)(2,1)S(1)} custom-call(s32[65536]{0:T(1024)S(1)} %copy-done.13, bf16[16,512,128]{2,1,0:T(8,128)(2,1)S(1)} %all-to-all-done.1.refs_1_, bf16[8,1024,128]{2,1,0:T(8,128)(2,1)S(1)} %copy-done.7), custom_call_target="tpu_custom_call" | custom-call | bytes 3000 | tf_op jit(solution)/shard_map/pool/pallas_call | solution.py:146
  197.8 51.1 %dense.1 = (f32[8,1024,128]{2,1,0:T(8,128)}, bf16[8,1024,512]{2,1,0:T(8,128)(2,1)}, bf16[1024,1024]{1,0:T(8,128)(2,1)}, bf16[1024,128]{1,0:T(8,128)(2,1)}, f32[3...) custom-call(s32[1]{0:T(128)} %bitcast.base_ref, bf16[8,1024,128]{2,1,0:T(8,128)(2,1)} %copy-done.10, ...), custom_call_target="tpu_custom_call" | custom-call | bytes 6000 | tf_op jit(solution)/shard_map/dense/pallas_call | solution.py:548
  248.9 16.9 %weight_grads.1 = (bf16[8,1024,512]{2,1,0:T(8,128)(2,1)}, bf16[1,1024,512]{2,1,0:T(8,128)(2,1)}) custom-call(s32[8]{0:T(128)} %and_select_fusion.which_ref, bf16[1024,1024]{1,0:T(8,128)(2,1)} %get-tuple-element.64.x_ref, bf16[8,1024,512]{2,1,0:T(8,128)(2,1)} %get-tuple-element.65.expert_ref, bf16[1024,128]{1,0:T(8,128)(2,1)} %get-tuple-element.66.gate_ref, ...), custom_call_target="tpu_custom_call" | custom-call | bytes 1800 | tf_op jit(solution)/shard_map/weight_grads/pallas_call | solution.py:635
  265.8 31.9 %grad_gather.2.refs_0_ = bf16[16,512,128]{2,1,0:T(8,128)(2,1)} custom-call(s32[32768]{0:T(1024)} %get-tuple-element.100.index_ref, f32[8192,128]{1,0:T(8,128)} %bitcast.49), custom_call_target="tpu_custom_call" | custom-call | bytes 3200 | tf_op jit(solution)/shard_map/grad_gather/pallas_call | solution.py:195
  297.7 11.2 %all-to-all-start.5 = ((bf16[16,512,128]{2,1,0:T(8,128)(2,1)}), bf16[16,512,128]{2,1,0:T(8,128)(2,1)S(1)}, u32[]{:S(2)}, u32[]{:S(2)}) async-start(bf16[16,512,128]{2,1,0:T(8,128)(2,1)} %grad_gather.2.refs_0_), calls=%async_computation.5 | async-start | bytes 4194304 | tf_op jit(solution)/shard_map/all_to_all | solution.py:807
  308.9 32.1 %grad_gather.3.refs_0_ = bf16[16,512,128]{2,1,0:T(8,128)(2,1)} custom-call(s32[32768]{0:T(1024)} %get-tuple-element.102.index_ref, f32[8192,128]{1,0:T(8,128)} %bitcast.50, bf16[16,512,128]{2,1,0:T(8,128)(2,1)} %grad_gather.2.refs_0_), custom_call_target="tpu_custom_call" | custom-call | bytes 3200 | tf_op jit(solution)/shard_map/grad_gather/pallas_call | solution.py:195
  341.0 9.0 %all-to-all-done.5.got_ref = bf16[16,512,128]{2,1,0:T(8,128)(2,1)S(1)} async-done(((bf16[16,512,128]{2,1,0:T(8,128)(2,1)}), bf16[16,512,128]{2,1,0:T(8,128)(2,1)S(1)}, u32[]{:S(2)}, u32[]{:S(2)}) %all-to-all-start.5) | async-done | bytes 2097184 | tf_op jit(solution)/shard_map/all_to_all | solution.py:807
  351.3 11.2 %all-to-all-start.4 = ((bf16[16,512,128]{2,1,0:T(8,128)(2,1)}), bf16[16,512,128]{2,1,0:T(8,128)(2,1)S(1)}, u32[]{:S(2)}, u32[]{:S(2)}) async-start(bf16[16,512,128]{2,1,0:T(8,128)(2,1)} %grad_gather.3.refs_0_), calls=%async_computation.4 | async-start | bytes 4194304 | tf_op jit(solution)/shard_map/all_to_all | solution.py:807
  362.6 1.6 copy-done.2
  364.2 1.6 copy-done.12
  365.8 20.9 %scatter.2 = (bf16[4096,128]{1,0:T(8,128)(2,1)}, bf16[4096,128]{1,0:T(8,128)(2,1)S(1)}) custom-call(s32[32768]{0:T(1024)S(1)} %bitcast.47, s32[32768]{0:T(1024)S(1)} %bitcast.48, bf16[16,512,128]{2,1,0:T(8,128)(2,1)S(1)} %copy-done.12, bf16[16,512,128]{2,1,0:T(8,128)(2,1)S(1)} %copy-done.2), custom_call_target="tpu_custom_call" | custom-call | bytes 2400 | tf_op jit(solution)/shard_map/scatter/pallas_call | solution.py:281
  387.8 1.6 collective-permute-start.1
  389.3 5.3 pad_maximum_fusion.refs_0_
  394.6 9.0 %all-to-all-done.4.got_ref.refs_1_ = bf16[16,512,128]{2,1,0:T(8,128)(2,1)S(1)} async-done(((bf16[16,512,128]{2,1,0:T(8,128)(2,1)}), bf16[16,512,128]{2,1,0:T(8,128)(2,1)S(1)}, u32[]{:S(2)}, u32[]{:S(2)}) %all-to-all-start.4) | async-done | bytes 2097184 | tf_op jit(solution)/shard_map/all_to_all | solution.py:807
  403.7 9.8 %collective-permute-done.1.refs_0_.refs_1_.refs_2_ = bf16[4096,128]{1,0:T(8,128)(2,1)S(1)} collective-permute-done((bf16[4096,128]{1,0:T(8,128)(2,1)}, bf16[4096,128]{1,0:T(8,128)(2,1)S(1)}, u32[]{:S(2)}, u32[]{:S(2)}) %collective-permute-start.1) | collective-permute-done | bytes 1048608 | tf_op jit(solution)/shard_map/ppermute | solution.py:727
  414.5 1.5 collective-permute-start.2
  416.3 20.0 %scatter.3 = (bf16[4096,128]{1,0:T(8,128)(2,1)S(1)}, bf16[4096,128]{1,0:T(8,128)(2,1)S(1)}) custom-call(s32[32768]{0:T(1024)S(1)} %bitcast.44, s32[32768]{0:T(1024)S(1)} %bitcast.45, bf16[16,512,128]{2,1,0:T(8,128)(2,1)S(1)} %copy-done.1, bf16[4096,128]{1,0:T(8,128)(2,1)S(1)} %copy-done.5), custom_call_target="tpu_custom_call" | custom-call | bytes 2400 | tf_op jit(solution)/shard_map/scatter/pallas_call | solution.py:281
  439.6 1.3 collective-permute-start.4
  441.0 22.7 %collective-permute-done.4.refs_1_.refs_0_ = bf16[4096,128]{1,0:T(8,128)(2,1)S(1)} collective-permute-done((bf16[4096,128]{1,0:T(8,128)(2,1)}, bf16[4096,128]{1,0:T(8,128)(2,1)S(1)}, u32[]{:S(2)}, u32[]{:S(2)}) %collective-permute-start.4) | collective-permute-done | bytes 1048608 | tf_op jit(solution)/shard_map/ppermute | solution.py:727
  465.9 1.4 slice_reduce_fusion.2
  469.4 1.4 collective-permute-done.3
  470.8 1.3 add.164.refs_1_.refs_0_
  472.2 14.9 %table_adam.2 = (f32[16384,128]{1,0:T(8,128)}, f32[16384,128]{1,0:T(8,128)}, f32[16384,128]{1,0:T(8,128)}, f32[8,128]{1,0:T(8,128)}) custom-call(bf16[4096,128]{1,0:T(8,128)(2,1)} %get-tuple-element.56.refs_0_, bf16[4096,128]{1,0:T(8,128)(2,1)} %copy-done.4, bf16[4096,128]{1,0:T(8,128)(2,1)} %order.8.refs_1_.refs_2_, bf16[4096,128]{1,0:T(8,128)(2,1)} %order.11.refs_3_, ...), custom_call_target="tpu_custom_call" | custom-call | bytes 700 | tf_op jit(solution)/shard_map/table_adam/pallas_call | solution.py:333
  488.9 14.8 %table_adam.3 = (f32[16384,128]{1,0:T(8,128)}, f32[16384,128]{1,0:T(8,128)}, f32[16384,128]{1,0:T(8,128)}, f32[8,128]{1,0:T(8,128)}) custom-call(bf16[4096,128]{1,0:T(8,128)(2,1)} %copy-done.19, bf16[4096,128]{1,0:T(8,128)(2,1)} %collective-permute-done.2.refs_1_, ...), custom_call_target="tpu_custom_call", output_to_operand_aliasing={{0}: (7, {}), {1}: (8, {}), {2}: (9, {})} | custom-call | bytes 700 | tf_op jit(solution)/shard_map/table_adam/pallas_call | solution.py:333
  505.7 3.2 collective-permute-done.6
  510.4 3.0 collective-permute-done.7
  514.7 1.7 collective-permute-start.9
  516.4 3.2 collective-permute-done.9
  521.3 1.7 slice.121.here_ref
  523.0 7.3 %dense_adam.1 = (f32[8,64,512]{2,1,0:T(8,128)}, f32[8,64,512]{2,1,0:T(8,128)}, f32[8,64,512]{2,1,0:T(8,128)}, f32[40,64]{1,0:T(8,128)}, f32[40,64]{1,0:T(8,128)}...) custom-call(s32[1]{0:T(128)} %bitcast.25.rep_ref, ...), custom_call_target="tpu_custom_call" | custom-call | tf_op jit(solution)/shard_map/dense_adam/pallas_call | solution.py:707
  (137 shorter events, 40.8 us)
Async XLA Ops:
  7.2 73.8 %all-gather.2.cloned.1.call-start = ((), (), s32[]{:S(2)}) async-start(), calls=%async_computation.8 | async-start | bytes 5570560 | tf_op jit(solution)/shard_map/all_gather | solution.py:796
  22.3 17.7 %all-to-all-start.2 = ((s32[16,1,2048]{2,1,0:T(1,128)}), s32[16,1,2048]{2,1,0:T(1,128)S(1)}, u32[]{:S(2)}, u32[]{:S(2)}) async-start(s32[16,1,2048]{2,1,0:T(1,128)} %bitcast.7), calls=%async_computation.2 | async-start | bytes 262144 | tf_op jit(solution)/shard_map/all_to_all | solution.py:807
  40.0 4.6 copy-start.17
  40.0 24.0 %all-to-all-start = ((s32[16,1,2048]{2,1,0:T(1,128)}), s32[16,1,2048]{2,1,0:T(1,128)S(1)}, u32[]{:S(2)}, u32[]{:S(2)}) async-start(s32[16,1,2048]{2,1,0:T(1,128)} %bitcast.5), calls=%async_computation | async-start | bytes 262144 | tf_op jit(solution)/shard_map/all_to_all | solution.py:807
  64.1 21.4 %copy-start.15 = (s32[16,1,2048]{2,1,0:T(1,128)}, s32[16,1,2048]{2,1,0:T(1,128)S(1)}, u32[]{:S(2)}) copy-start(s32[16,1,2048]{2,1,0:T(1,128)S(1)} %all-to-all-done) | copy-start | bytes 393220
  64.1 47.6 %all-to-all-start.3 = ((bf16[16,512,128]{2,1,0:T(8,128)(2,1)}), bf16[16,512,128]{2,1,0:T(8,128)(2,1)S(1)}, u32[]{:S(2)}, u32[]{:S(2)}) async-start(bf16[16,512,128]{2,1,0:T(8,128)(2,1)} %owner_gather.3), calls=%async_computation.3 | async-start | bytes 4194304 | tf_op jit(solution)/shard_map/all_to_all | solution.py:807
  85.5 112.3 %collective-permute-start = (bf16[4,1024,512]{2,1,0:T(8,128)(2,1)}, bf16[4,1024,512]{2,1,0:T(8,128)(2,1)}, u32[]{:S(2)}, u32[]{:S(2)}) collective-permute-start(bf16[4,1024,512]{2,1,0:T(8,128)(2,1)} %slice.119), channel_id=1, source_target_pairs={{0,16},{16,0},{1,17},{17,1},{2,18},{18,2},{3,19},{19,3},{4,20},{20... | collective-permute-start | bytes 12582920 | tf_op jit(solution)/shard_map/ppermute | solution.py:727
  87.8 36.5 %copy-start.29 = (s32[32]{0:T(128)S(1)}, s32[32]{0:T(128)}, u32[]{:S(2)}) copy-start(s32[32]{0:T(128)} %param.22) | copy-start | bytes 388
  87.8 37.7 %copy-start.23 = (f32[4741]{0:T(1024)S(1)}, f32[4741]{0:T(1024)}, u32[]{:S(2)}) copy-start(f32[4741]{0:T(1024)} %param.37) | copy-start | bytes 56896
  87.8 39.6 %copy-start.25 = (s32[1024,5]{0,1:T(8,128)S(1)}, s32[1024,5]{0,1:T(8,128)}, u32[]{:S(2)}) copy-start(s32[1024,5]{0,1:T(8,128)} %param.23) | copy-start | bytes 61444
  87.8 39.6 %copy-start.26 = (s32[1024,5]{0,1:T(8,128)S(1)}, s32[1024,5]{0,1:T(8,128)}, u32[]{:S(2)}) copy-start(s32[1024,5]{0,1:T(8,128)} %param.24) | copy-start | bytes 61444
  107.2 24.2 %slice-start = ((f32[4741]{0:T(1024)}), f32[4096]{0:T(1024)S(1)}, s32[]{:S(2)}) async-start(f32[4741]{0:T(1024)} %param.37), calls=%async_computation.11 | async-start | bytes 32768 | tf_op jit(solution)/shard_map/slice | solution.py:858
  107.2 24.8 %copy-start.13 = (s32[65536]{0:T(1024)S(1)}, s32[65536]{0:T(1024)}, u32[]{:S(2)}) copy-start(s32[65536]{0:T(1024)} %add_select_fusion.refs_0_) | copy-start | bytes 786436
  111.6 1.3 copy-start.8
  112.9 52.3 %all-to-all-start.1 = ((bf16[16,512,128]{2,1,0:T(8,128)(2,1)}), bf16[16,512,128]{2,1,0:T(8,128)(2,1)S(1)}, u32[]{:S(2)}, u32[]{:S(2)}) async-start(bf16[16,512,128]{2,1,0:T(8,128)(2,1)} %owner_gather.2), calls=%async_computation.1 | async-start | bytes 4194304 | tf_op jit(solution)/shard_map/all_to_all | solution.py:807
  124.2 265.2 %reduce-scatter.3.cloned.1.call-start = ((), (), s32[]{:S(2)}) async-start(), calls=%async_computation.9 | async-start | bytes 12582912 | tf_op jit(solution)/shard_map/reduce_scatter | solution.py:873
  132.1 1.6 copy-start.9
  163.1 1.3 copy-start.6
  165.3 1.6 copy-start.7
  196.4 1.3 copy-start.10
  297.7 52.3 %all-to-all-start.5 = ((bf16[16,512,128]{2,1,0:T(8,128)(2,1)}), bf16[16,512,128]{2,1,0:T(8,128)(2,1)S(1)}, u32[]{:S(2)}, u32[]{:S(2)}) async-start(bf16[16,512,128]{2,1,0:T(8,128)(2,1)} %grad_gather.2.refs_0_), calls=%async_computation.5 | async-start | bytes 4194304 | tf_op jit(solution)/shard_map/all_to_all | solution.py:807
  308.9 53.7 %copy-start.18 = (s32[16,1,2048]{2,1,0:T(1,128)S(1)}, s32[16,1,2048]{2,1,0:T(1,128)}, u32[]{:S(2)}) copy-start(s32[16,1,2048]{2,1,0:T(1,128)} %copy-done.17) | copy-start | bytes 393220
  350.0 1.3 copy-start.11
  351.3 52.3 %all-to-all-start.4 = ((bf16[16,512,128]{2,1,0:T(8,128)(2,1)}), bf16[16,512,128]{2,1,0:T(8,128)(2,1)S(1)}, u32[]{:S(2)}, u32[]{:S(2)}) async-start(bf16[16,512,128]{2,1,0:T(8,128)(2,1)} %grad_gather.3.refs_0_), calls=%async_computation.4 | async-start | bytes 4194304 | tf_op jit(solution)/shard_map/all_to_all | solution.py:807
  362.6 141.2 %reduce-scatter.5.cloned.1.call-start = ((), (), s32[]{:S(2)}) async-start(), calls=%async_computation.10 | async-start | bytes 5570560 | tf_op jit(solution)/shard_map/reduce_scatter | solution.py:876
  362.6 1.6 copy-start.2
  364.2 1.6 copy-start.12
  386.7 1.0 copy-start.19
  387.8 25.7 %collective-permute-start.1 = (bf16[4096,128]{1,0:T(8,128)(2,1)}, bf16[4096,128]{1,0:T(8,128)(2,1)S(1)}, u32[]{:S(2)}, u32[]{:S(2)}) collective-permute-start(bf16[4096,128]{1,0:T(8,128)(2,1)} %get-tuple-element.56.refs_0_), channel_id=1, source_target_pairs={{0,16},{16,0},{1,17},{17,1},{2,18},{18,2},{3,19},{19,3},{4,20},{20... | collective-permute-start | bytes 3145736 | tf_op jit(solution)/shard_map/ppermute | solution.py:727
  403.7 9.8 %copy-start = (bf16[16,512,128]{2,1,0:T(8,128)(2,1)}, bf16[16,512,128]{2,1,0:T(8,128)(2,1)S(1)}, u32[]{:S(2)}) copy-start(bf16[16,512,128]{2,1,0:T(8,128)(2,1)S(1)} %all-to-all-done.4.got_ref.refs_1_) | copy-start | bytes 6291460
  414.5 1.6 copy-start.1
  414.5 1.9 copy-start.5
  414.5 1.9 copy-start.16
  414.5 53.5 %copy-start.24 = (f32[8,1,512]{2,1,0:T(1,128)S(1)}, f32[8,1,512]{2,1,0:T(1,128)}, u32[]{:S(2)}) copy-start(f32[8,1,512]{2,1,0:T(1,128)} %get-tuple-element.53) | copy-start | bytes 49156
  414.5 25.1 %collective-permute-start.2 = (bf16[4096,128]{1,0:T(8,128)(2,1)}, bf16[4096,128]{1,0:T(8,128)(2,1)}, u32[]{:S(2)}, u32[]{:S(2)}) collective-permute-start(bf16[4096,128]{1,0:T(8,128)(2,1)} %copy-done.19), channel_id=1, source_target_pairs={{0,16},{16,0},{1,17},{17,1},{2,18},{18,2},{3,19},{19,3},{4,20},{20... | collective-permute-start | bytes 3145736 | tf_op jit(solution)/shard_map/ppermute | solution.py:727
  436.3 1.0 copy-start.3
  437.3 1.0 copy-start.14
  439.6 24.0 %collective-permute-start.4 = (bf16[4096,128]{1,0:T(8,128)(2,1)}, bf16[4096,128]{1,0:T(8,128)(2,1)S(1)}, u32[]{:S(2)}, u32[]{:S(2)}) collective-permute-start(bf16[4096,128]{1,0:T(8,128)(2,1)} %order.8.refs_1_.refs_2_), channel_id=1, source_target_pairs={{0,16},{16,0},{1,17},{17,1},{2,18},{18,2},{3,19},{19,3},{4,20},{20... | collective-permute-start | bytes 3145736 | tf_op jit(solution)/shard_map/ppermute | solution.py:727
  463.7 1.0 copy-start.20
  464.7 23.2 %collective-permute-start.5 = (bf16[4096,128]{1,0:T(8,128)(2,1)}, bf16[4096,128]{1,0:T(8,128)(2,1)S(1)}, u32[]{:S(2)}, u32[]{:S(2)}) collective-permute-start(bf16[4096,128]{1,0:T(8,128)(2,1)} %order.10.refs_2_), channel_id=1, source_target_pairs={{0,16},{16,0},{1,17},{17,1},{2,18},{18,2},{3,19},{19,3},{4,20},{20... | collective-permute-start | bytes 3145736 | tf_op jit(solution)/shard_map/ppermute | solution.py:727
  469.4 1.4 collective-permute-start.3
  503.7 28.4 %copy-start.27 = (f32[4741]{0:T(1024)S(1)}, f32[4741]{0:T(1024)}, u32[]{:S(2)}) copy-start(f32[4741]{0:T(1024)} %param.38) | copy-start | bytes 56896
  503.7 28.4 %copy-start.28 = (f32[4741]{0:T(1024)S(1)}, f32[4741]{0:T(1024)}, u32[]{:S(2)}) copy-start(f32[4741]{0:T(1024)} %param.39) | copy-start | bytes 56896
  503.8 10.3 %collective-permute-start.8 = (bf16[5,64,512]{2,1,0:T(8,128)(2,1)}, bf16[5,64,512]{2,1,0:T(8,128)(2,1)S(1)}, u32[]{:S(2)}, u32[]{:S(2)}) collective-permute-start(bf16[5,64,512]{2,1,0:T(8,128)(2,1)} %order.14.more_ref), channel_id=1, source_target_pairs={{0,16},{16,0},{1,17},{17,1},{2,18},{18,2},{3,19},{19,3},{4,20},{20... | collective-permute-start | bytes 983048 | tf_op jit(solution)/shard_map/ppermute | solution.py:727
  504.9 4.0 collective-permute-start.6
  509.6 3.8 collective-permute-start.7
  514.7 4.9 collective-permute-start.9
  520.4 9.9 %collective-permute-start.10 = (f32[40,128]{1,0:T(8,128)S(1)}, f32[40,128]{1,0:T(8,128)S(1)}, u32[]{:S(2)}, u32[]{:S(2)}) collective-permute-start(f32[40,128]{1,0:T(8,128)S(1)} %add.168), channel_id=1, source_target_pairs={{0,16},{16,0},{1,17},{17,1},{2,18},{18,2},{3,19},{19,3},{4,20},{20... | collective-permute-start | bytes 61448 | tf_op jit(solution)/shard_map/ppermute | solution.py:736
  (3 other events, 2.7 us)
Sparse Core Ops, SparseCore 0:
  11.2 62.5 all-gather.1
  266.0 105.7 reduce-scatter.2
  414.6 79.3 reduce-scatter.4
